TPU v7x, 32 devices: a whole 2x2x4 slice. The times are simulated.
32 devices in a mesh: groups: 2 (over y), ctx: 8 (over z, x), chan: 2 (over core).
Axes of the slice: x: 2, y: 2, z: 4, core: 2. Of those that a mesh axis runs over, the one named last changes fastest.
Arguments:
- first_gate: bfloat16 [128, 8192], P('chan', ('groups', 'ctx')), parts along dimension 1, may hold values from -6 to 6
- second_gate: bfloat16 [128, 8192], P('chan', ('groups', 'ctx')), parts along dimension 1, may hold values from -6 to 6
- values: bfloat16 [128, 8192], P('chan', ('groups', 'ctx')), parts along dimension 1, may hold values from -6 to 6
- filters: float32 [128, 8192], P('chan', ('groups', 'ctx')), parts along dimension 1, may hold values from -0.09375 to 0.09375
- skip_gain: float32 [128], P('chan'), may hold values from -4 to 4
- grad_output: bfloat16 [128, 8192], P('chan', ('groups', 'ctx')), parts along dimension 1, may hold values from -6 to 6
Outputs:
- output: float32 [128, 8192], P('chan', ('groups', 'ctx')), parts along dimension 1
- grad_first: float32 [128, 8192], P('chan', ('groups', 'ctx')), parts along dimension 1
- grad_second: float32 [128, 8192], P('chan', ('groups', 'ctx')), parts along dimension 1
- grad_values: float32 [128, 8192], P('chan', ('groups', 'ctx')), parts along dimension 1
- grad_filters: float32 [128, 8192], P('chan', ('groups', 'ctx')), parts along dimension 1
- grad_skip: float32 [256], P(('groups', 'chan')), parts along dimension 0
There are 2 independent parts, one for each index of `groups`. A program takes and returns all parts, laid end to end along the dimension named above; an argument that names none is the same for every part. Nothing has to cross between parts.
All inputs are finite; a program needn't handle non-finite values.
Results may differ from a plain program's by a relative error of at most 0.0003.
Values sent between devices are 32-bit elements; how exact they have to be, the bound alone decides.
No kernel may reach another device: no remote copies, remote signals or barrier semaphores. Data moves between devices by JAX's collectives and lax.ppermute only.
A program may use at most 64 MiB of HBM per device.

v0:
```python
import math

import jax
import jax.numpy as jnp
import numpy as np
from jax import lax
from jax.experimental import pallas as pl
from jax.experimental.pallas import tpu as pltpu
from jax.sharding import PartitionSpec as P

HIGHEST = lax.Precision.HIGHEST
LANES = 128
ROWS = 8
VMEM = pl.BlockSpec(memory_space=pltpu.VMEM)
PARAMS = pltpu.CompilerParams(vmem_limit_bytes=48 * 1024 * 1024)


def halves(table):
    high = table.astype(np.float32).astype(jnp.bfloat16)
    low = (table - high.astype(np.float64)).astype(np.float32).astype(jnp.bfloat16)
    return high, low


def make_tables(length):
    groups = length // LANES
    period = 2 * length
    turns = 2 * groups
    k1 = np.arange(groups + 1)
    inner = np.arange(1, groups)
    a = np.arange(groups)
    eye = np.eye(ROWS)
    angle = 2.0 * np.pi / turns
    outer = np.concatenate([np.cos(angle * (k1[:, None] * a % turns)), np.sin(angle * (inner[:, None] * a % turns))])
    weight = np.where((k1 == 0) | (k1 == groups), 1.0, 2.0) / period
    back = np.concatenate(
        [weight[:, None] * np.cos(angle * (k1[:, None] * a % turns)), -2.0 / period * np.sin(angle * (inner[:, None] * a % turns))]
    )
    b = np.arange(LANES)
    wave = 2.0 * np.pi / LANES * (b[:, None] * b % LANES)
    cosine, sine = np.cos(wave), np.sin(wave)
    lane_fwd = np.block([[cosine, -sine], [sine, cosine]])
    lane_back = np.block([[cosine, sine], [-sine, cosine]])
    twist = 2.0 * np.pi / period * (k1[:, None] * b % period)
    twist = np.repeat(twist, ROWS, axis=0)
    return (
        *halves(np.kron(outer, eye)),
        *halves(np.kron(back.T, eye)),
        *halves(lane_fwd),
        *halves(lane_back),
        np.cos(twist).astype(np.float32),
        np.sin(twist).astype(np.float32),
    )


def split(data):
    high = data.astype(jnp.bfloat16)
    return high, (data - high.astype(jnp.float32)).astype(jnp.bfloat16)


def dot(left, right):
    return jnp.dot(left, right, preferred_element_type=jnp.float32)


def table_left(high, low, data):
    data_high, data_low = split(data)
    return dot(high, data_high) + (dot(high, data_low) + dot(low, data_high))


def table_right(data, high, low):
    data_high, data_low = split(data)
    return dot(data_high, high) + (dot(data_low, high) + dot(data_high, low))


def gate_kernel(first_ref, second_ref, values_ref, filters_ref, grad_ref, out_ref):
    mixed = first_ref[...].astype(jnp.float32) * values_ref[...].astype(jnp.float32)
    carried = grad_ref[...].astype(jnp.float32) * second_ref[...].astype(jnp.float32)
    shards = out_ref.shape[0]
    tiles = filters_ref.shape[1] // LANES
    for s, signal in enumerate((mixed, filters_ref[...], carried)):
        for j in range(tiles):
            tile = signal[:, j * LANES : (j + 1) * LANES].reshape(shards, ROWS, LANES)
            row = (s * tiles + j) * ROWS
            out_ref[:, row : row + ROWS, :] = tile


def spectral_kernel(in_ref, oh, ol, bh, bl, fh, fl, ih, il, cos_ref, sin_ref, out_ref):
    shards = in_ref.shape[0]
    span = in_ref.shape[1] // 3
    rows = shards * span
    spec_rows = rows + ROWS
    signals = [in_ref[:, s * span : (s + 1) * span, :].reshape(rows, LANES) for s in range(3)]
    total = jnp.sum((signals[0] * signals[2]).reshape(rows // ROWS, ROWS, LANES), axis=0)
    total = jnp.broadcast_to(jnp.sum(total, axis=1, keepdims=True), (ROWS, LANES))
    out_ref[:, 3 * span :, :] = jnp.broadcast_to(total[None], (shards, ROWS, LANES))
    columns = table_left(oh[...], ol[...], jnp.concatenate(signals, axis=1))
    cosine, sine = cos_ref[...], sin_ref[...]
    edge = jnp.zeros((ROWS, LANES), jnp.float32)
    spectra = []
    for s in range(3):
        lanes = slice(s * LANES, (s + 1) * LANES)
        real = columns[:spec_rows, lanes]
        imag = jnp.concatenate([edge, columns[spec_rows:, lanes], edge], axis=0)
        turned = jnp.concatenate([real * cosine - imag * sine, -(real * sine + imag * cosine)], axis=1)
        spectra.append(table_right(turned, fh[...], fl[...]))
    (mr, mi), (fr, fi), (cr, ci) = [(x[:, :LANES], x[:, LANES:]) for x in spectra]
    products = (
        (fr * mr - fi * mi, fr * mi + fi * mr),
        (fr * cr + fi * ci, fr * ci - fi * cr),
        (mr * cr + mi * ci, mr * ci - mi * cr),
    )
    reverted = []
    for real, imag in products:
        waves = table_right(jnp.concatenate([real, imag], axis=1), ih[...], il[...])
        real, imag = waves[:, :LANES], waves[:, LANES:]
        turned_imag = real * sine + imag * cosine
        reverted.append(jnp.concatenate([real * cosine - imag * sine, turned_imag[ROWS:-ROWS]], axis=0))
    result = table_left(bh[...], bl[...], jnp.concatenate(reverted, axis=1))
    for s in range(3):
        out_ref[:, s * span : (s + 1) * span, :] = result[:, s * LANES : (s + 1) * LANES].reshape(shards, span, LANES)


def output_kernel(in_ref, first_ref, second_ref, values_ref, grad_ref, gain_ref, out_ref, gfirst_ref, gsecond_ref, gvalues_ref, gfilters_ref, gskip_ref):
    channels, blocks = first_ref.shape
    tiles = blocks // LANES
    first = first_ref[...].astype(jnp.float32)
    second = second_ref[...].astype(jnp.float32)
    values = values_ref[...].astype(jnp.float32)
    grad = grad_ref[...].astype(jnp.float32)
    diagonal = lax.broadcasted_iota(jnp.int32, (channels, channels), 0) == lax.broadcasted_iota(jnp.int32, (channels, channels), 1)
    gain = jnp.sum(jnp.where(diagonal, gain_ref[...], 0.0), axis=1, keepdims=True)
    result = []
    for s in range(3):
        parts = [in_ref[:, (s * tiles + j) * ROWS : (s * tiles + j + 1) * ROWS, :].reshape(channels, LANES) for j in range(tiles)]
        result.append(jnp.concatenate(parts, axis=1))
    before = result[0] + gain * (first * values)
    out_ref[...] = second * before
    gsecond_ref[...] = grad * before
    back = result[1] + gain * (grad * second)
    gfirst_ref[...] = back * values
    gvalues_ref[...] = back * first
    gfilters_ref[...] = result[2]
    total = in_ref[:, 3 * tiles * ROWS :, :].reshape(channels, LANES)[:, :channels]
    gskip_ref[...] = jnp.sum(jnp.where(diagonal, total, 0.0), axis=0, keepdims=True)


def by_channels(first_gate, second_gate, values, filters, skip_gain, grad_output):
    channels, blocks = filters.shape
    shards = lax.axis_size("ctx")
    tiles = blocks // LANES
    length = blocks * shards
    full = jax.ShapeDtypeStruct((channels, blocks), jnp.float32)
    slabs = pl.pallas_call(
        gate_kernel,
        out_shape=jax.ShapeDtypeStruct((shards, 3 * tiles * ROWS, LANES), jnp.float32),
        in_specs=[VMEM] * 5,
        out_specs=VMEM,
        compiler_params=PARAMS,
    )(first_gate, second_gate, values, filters, grad_output)
    slabs = lax.all_to_all(slabs, "ctx", split_axis=0, concat_axis=0, tiled=True)
    tables = make_tables(length)
    slabs = pl.pallas_call(
        spectral_kernel,
        out_shape=jax.ShapeDtypeStruct((shards, (3 * tiles + 1) * ROWS, LANES), jnp.float32),
        in_specs=[VMEM] * (1 + len(tables)),
        out_specs=VMEM,
        compiler_params=PARAMS,
    )(slabs, *tables)
    slabs = lax.all_to_all(slabs, "ctx", split_axis=0, concat_axis=0, tiled=True)
    *wide, grad_skip = pl.pallas_call(
        output_kernel,
        out_shape=(full,) * 5 + (jax.ShapeDtypeStruct((1, channels), jnp.float32),),
        in_specs=[VMEM] * 6,
        out_specs=(VMEM,) * 6,
        compiler_params=PARAMS,
    )(slabs, first_gate, second_gate, values, grad_output, skip_gain.reshape(1, channels))
    return (*wide, grad_skip.reshape(channels))


def turn_table(first_index, second_index, period):
    product = first_index[:, None] * second_index[None, :] % period
    angles = 2.0 * math.pi / period * product.astype(jnp.float32)
    return (jnp.cos(angles), jnp.sin(angles))


def right_dot(data, table):
    return jnp.dot(data, table, precision=HIGHEST)


def by_columns(first_gate, second_gate, values, filters, skip_gain, grad_output):
    channels, length = filters.shape
    shards = lax.axis_size("ctx")
    blocks = length // shards
    position = lax.axis_index("ctx")
    period = 2 * shards * length
    first = first_gate.astype(jnp.float32)
    second = second_gate.astype(jnp.float32)
    values_wide = values.astype(jnp.float32)
    mixed = first * values_wide
    carried = grad_output.astype(jnp.float32) * second
    signal = jnp.stack([mixed, filters, carried]).reshape(3, channels, blocks, shards)
    spread = lax.all_to_all(signal, "ctx", split_axis=3, concat_axis=3, tiled=True)
    shard_index = jnp.arange(shards, dtype=jnp.int32)
    cosine, sines = turn_table(shard_index, shard_index, 2 * shards)
    parity = (1 - 2 * (shard_index % 2)).astype(jnp.float32)
    fwd_real = jnp.stack([cosine, parity[:, None] * cosine], axis=1)
    fwd_imag = jnp.stack([-sines, -parity[:, None] * sines], axis=1)
    real_part = jnp.einsum("scbm,mjk->scjbk", spread, fwd_real, precision=HIGHEST)
    imag_part = jnp.einsum("scbm,mjk->scjbk", spread, fwd_imag, precision=HIGHEST)
    sectioned = jnp.stack([real_part, imag_part])
    moved = lax.all_to_all(sectioned, "ctx", split_axis=5, concat_axis=5, tiled=True).reshape(
        2, 3, channels, 2, length
    )
    col_real = moved[0]
    col_imag = moved[1]
    col_index = jnp.stack([position, position + shards])
    line_index = jnp.arange(length, dtype=jnp.int32)
    twist_cos, twist_sin = turn_table(col_index, line_index, period)
    turned_real = col_real * twist_cos + col_imag * twist_sin
    turned_imag = col_imag * twist_cos - col_real * twist_sin
    wave_cos, wave_sin = turn_table(line_index, line_index, length)
    spec_real = right_dot(turned_real, wave_cos) + right_dot(turned_imag, wave_sin)
    spec_imag = right_dot(turned_imag, wave_cos) - right_dot(turned_real, wave_sin)
    mixed_real, filter_real, carry_real = (spec_real[0], spec_real[1], spec_real[2])
    mixed_imag, filter_imag, carry_imag = (spec_imag[0], spec_imag[1], spec_imag[2])
    prod_real = jnp.stack(
        [
            filter_real * mixed_real - filter_imag * mixed_imag,
            filter_real * carry_real + filter_imag * carry_imag,
            mixed_real * carry_real + mixed_imag * carry_imag,
        ]
    )
    prod_imag = jnp.stack(
        [
            filter_real * mixed_imag + filter_imag * mixed_real,
            filter_real * carry_imag - filter_imag * carry_real,
            mixed_real * carry_imag - mixed_imag * carry_real,
        ]
    )
    back_real = right_dot(prod_real, wave_cos) - right_dot(prod_imag, wave_sin)
    back_imag = right_dot(prod_real, wave_sin) + right_dot(prod_imag, wave_cos)
    reverted_real = back_real * twist_cos - back_imag * twist_sin
    reverted_imag = back_real * twist_sin + back_imag * twist_cos
    packed = jnp.stack([reverted_real, reverted_imag])
    returned = lax.all_to_all(
        packed.reshape(2, 3, channels, 2, blocks, shards),
        "ctx",
        split_axis=5,
        concat_axis=5,
        tiled=True,
    )
    inv_real = jnp.stack([cosine, cosine * parity[None, :]])
    inv_imag = jnp.stack([-sines, -sines * parity[None, :]])
    timed = jnp.einsum("scjbk,jkm->scbm", returned[0], inv_real, precision=HIGHEST)
    timed = timed + jnp.einsum("scjbk,jkm->scbm", returned[1], inv_imag, precision=HIGHEST)
    timed = timed * (1.0 / period)
    result = lax.all_to_all(timed, "ctx", split_axis=3, concat_axis=3, tiled=True).reshape(
        3, channels, length
    )
    gain = skip_gain[:, None]
    before = result[0] + gain * mixed
    output = second * before
    grad_second = grad_output.astype(jnp.float32) * before
    back_mixed = result[1] + gain * carried
    grad_first = back_mixed * values_wide
    grad_values = back_mixed * first
    grad_filters = result[2]
    grad_skip = lax.psum(jnp.sum(carried * mixed, axis=1), "ctx")
    return (output, grad_first, grad_second, grad_values, grad_filters, grad_skip)


def per_device(first_gate, second_gate, values, filters, skip_gain, grad_output):
    channels, blocks = filters.shape
    shards = lax.axis_size("ctx")
    fits = channels == ROWS * shards and blocks % LANES == 0 and channels <= LANES
    plan = by_channels if fits else by_columns
    return plan(first_gate, second_gate, values, filters, skip_gain, grad_output)


def solution(mesh):
    placed = (
        P("chan", ("groups", "ctx")),
        P("chan", ("groups", "ctx")),
        P("chan", ("groups", "ctx")),
        P("chan", ("groups", "ctx")),
        P("chan"),
        P("chan", ("groups", "ctx")),
    )
    return jax.shard_map(
        per_device,
        mesh=mesh,
        in_specs=placed,
        out_specs=(
            P("chan", ("groups", "ctx")),
            P("chan", ("groups", "ctx")),
            P("chan", ("groups", "ctx")),
            P("chan", ("groups", "ctx")),
            P("chan", ("groups", "ctx")),
            P(("groups", "chan")),
        ),
        check_vma=False,
    )
```

profile of v0, /device:TPU:0, one launch (start us, length us, event | category | flops | bytes accessed | tf_op | source)
XLA Modules:
  0.0 46.4 jit_solution(12471832380976492700)
XLA Ops:
  0.6 0.0 copy-start
  0.6 0.8 %copy-done = bf16[64,512]{1,0:T(8,128)(2,1)S(1)} copy-done((bf16[64,512]{1,0:T(8,128)(2,1)S(1)}, bf16[64,512]{1,0:T(8,128)(2,1)}, u32[]{:S(2)}) %copy-start) | copy-done | bytes 65560
  1.5 0.8 %copy-done.2 = bf16[64,512]{1,0:T(8,128)(2,1)S(1)} copy-done((bf16[64,512]{1,0:T(8,128)(2,1)S(1)}, bf16[64,512]{1,0:T(8,128)(2,1)}, u32[]{:S(2)}) %copy-start.2) | copy-done | bytes 65560
  2.3 0.8 %copy-done.4 = bf16[64,512]{1,0:T(8,128)(2,1)S(1)} copy-done((bf16[64,512]{1,0:T(8,128)(2,1)S(1)}, bf16[64,512]{1,0:T(8,128)(2,1)}, u32[]{:S(2)}) %copy-start.4) | copy-done | bytes 65560
  3.2 0.8 %copy-done.6 = bf16[64,512]{1,0:T(8,128)(2,1)S(1)} copy-done((bf16[64,512]{1,0:T(8,128)(2,1)S(1)}, bf16[64,512]{1,0:T(8,128)(2,1)}, u32[]{:S(2)}) %copy-start.6) | copy-done | bytes 65560
  4.0 0.9 %copy-done.14 = f32[64,512]{1,0:T(8,128)S(1)} copy-done((f32[64,512]{1,0:T(8,128)S(1)}, f32[64,512]{1,0:T(8,128)}, u32[]{:S(2)}) %copy-start.14) | copy-done | bytes 131096
  5.0 0.0 copy-start.8
  5.0 0.0 copy-start.9
  5.0 0.0 copy-start.10
  5.0 19.3 %all_to_all.10.in_ref = f32[8,96,128]{2,1,0:T(8,128)S(1)} all-to-all(f32[8,96,128]{2,1,0:T(8,128)S(1)} %shard_map.199), channel_id=1, replica_groups=mesh['groups'=2,'ctx'=8,'chan'=2] {'ctx'}, dimensions={0} | all-to-all | bytes 786432 | tf_op jit(solution)/shard_map/all_to_all | solution.py:159
  24.3 0.0 copy-done.12
  24.3 0.0 copy-start.16
  24.3 0.9 %copy-done.16 = bf16[256,256]{1,0:T(8,128)(2,1)S(1)} copy-done((bf16[256,256]{1,0:T(8,128)(2,1)S(1)}, bf16[256,256]{1,0:T(8,128)(2,1)}, u32[]{:S(2)}) %copy-start.16) | copy-done | bytes 131096
  25.2 0.9 %copy-done.17 = bf16[256,256]{1,0:T(8,128)(2,1)S(1)} copy-done((bf16[256,256]{1,0:T(8,128)(2,1)S(1)}, bf16[256,256]{1,0:T(8,128)(2,1)}, u32[]{:S(2)}) %copy-start.17) | copy-done | bytes 131096
  26.1 0.9 %copy-done.18 = bf16[256,256]{1,0:T(8,128)(2,1)S(1)} copy-done((bf16[256,256]{1,0:T(8,128)(2,1)S(1)}, bf16[256,256]{1,0:T(8,128)(2,1)}, u32[]{:S(2)}) %copy-start.18) | copy-done | bytes 131096
  27.0 2.0 %shard_map.200 = f32[8,104,128]{2,1,0:T(8,128)S(1)} custom-call(f32[8,96,128]{2,1,0:T(8,128)S(1)} %all_to_all.10.in_ref, bf16[512,256]{1,0:T(8,128)(2,1)S(1)} %copy-done.11, bf16[512,256]{1,0:T(8,128)(2,1)S(1)} %copy-done.10, bf16[256,512]{1,0:T(8,128)(2,1)S(1)} %copy-done.9, bf16[256,512]{1,0:T(8,128)(2,1)S(1)} %copy-done.8, ...), custom_call_target="tpu_custom_call" | custom-call | tf_op jit(solution)/shard_map/pallas_call | solution.py:161
  29.1 0.0 copy-start.1
  29.1 0.0 copy-start.3
  29.1 0.0 copy-start.5
  29.1 0.0 copy-start.7
  29.1 15.6 %all_to_all.11.in_ref = f32[8,104,128]{2,1,0:T(8,128)S(1)} all-to-all(f32[8,104,128]{2,1,0:T(8,128)S(1)} %shard_map.200), channel_id=1, replica_groups=mesh['groups'=2,'ctx'=8,'chan'=2] {'ctx'}, dimensions={0} | all-to-all | bytes 851968 | tf_op jit(solution)/shard_map/all_to_all | solution.py:168
  44.8 0.0 copy-done.7
  44.8 0.6 %copy-done.19 = f32[64]{0:T(128)S(1)} copy-done((f32[64]{0:T(128)S(1)}, f32[64]{0:T(128)}, u32[]{:S(2)}) %copy-start.19) | copy-done | bytes 280
  45.4 1.0 %shard_map.201 = (f32[64,512]{1,0:T(8,128)}, f32[64,512]{1,0:T(8,128)}, f32[64,512]{1,0:T(8,128)}, f32[64,512]{1,0:T(8,128)}, f32[64,512]{1,0:T(8,128)}, /*index=5*/f32[1,64]{1,0:T(1,128)}) custom-call(f32[8,104,128]{2,1,0:T(8,128)S(1)} %all_to_all.11.in_ref, bf16[64,512]{1,0:T(8,128)(2,1)S(1)} %copy-done.1, bf16[64,512]{1,0:T(8,128)(2,1)S(1)} %copy-done.3, ...), custom_call_target="tpu_custom_call" | custom-call | tf_op jit(solution)/shard_map/pallas_call | solution.py:169
  (21 shorter events, 0.1 us)
Async XLA Ops:
  0.6 0.8 %copy-start = (bf16[64,512]{1,0:T(8,128)(2,1)S(1)}, bf16[64,512]{1,0:T(8,128)(2,1)}, u32[]{:S(2)}) copy-start(bf16[64,512]{1,0:T(8,128)(2,1)} %first_ref.3) | copy-start | bytes 196612
  1.5 0.8 %copy-start.2 = (bf16[64,512]{1,0:T(8,128)(2,1)S(1)}, bf16[64,512]{1,0:T(8,128)(2,1)}, u32[]{:S(2)}) copy-start(bf16[64,512]{1,0:T(8,128)(2,1)} %second_ref.3) | copy-start | bytes 196612
  2.3 0.8 %copy-start.4 = (bf16[64,512]{1,0:T(8,128)(2,1)S(1)}, bf16[64,512]{1,0:T(8,128)(2,1)}, u32[]{:S(2)}) copy-start(bf16[64,512]{1,0:T(8,128)(2,1)} %values_ref.3) | copy-start | bytes 196612
  3.2 0.8 %copy-start.6 = (bf16[64,512]{1,0:T(8,128)(2,1)S(1)}, bf16[64,512]{1,0:T(8,128)(2,1)}, u32[]{:S(2)}) copy-start(bf16[64,512]{1,0:T(8,128)(2,1)} %grad_ref.3) | copy-start | bytes 196612
  4.0 0.9 %copy-start.14 = (f32[64,512]{1,0:T(8,128)S(1)}, f32[64,512]{1,0:T(8,128)}, u32[]{:S(2)}) copy-start(f32[64,512]{1,0:T(8,128)} %filters_ref.1) | copy-start | bytes 393220
  4.9 19.4 %copy-start.11 = (bf16[512,256]{1,0:T(8,128)(2,1)S(1)}, bf16[512,256]{1,0:T(8,128)(2,1)}, u32[]{:S(2)}) copy-start(bf16[512,256]{1,0:T(8,128)(2,1)} %constant.20.clone.oh) | copy-start | bytes 786436
  4.9 19.4 %copy-start.12 = (f32[264,128]{1,0:T(8,128)S(1)}, f32[264,128]{1,0:T(8,128)}, u32[]{:S(2)}) copy-start(f32[264,128]{1,0:T(8,128)} %constant.29.clone.sin_ref) | copy-start | bytes 405508
  4.9 19.4 %copy-start.13 = (f32[264,128]{1,0:T(8,128)S(1)}, f32[264,128]{1,0:T(8,128)}, u32[]{:S(2)}) copy-start(f32[264,128]{1,0:T(8,128)} %constant.28.clone.cos_ref) | copy-start | bytes 405508
  4.9 19.4 %copy-start.15 = (bf16[256,256]{1,0:T(8,128)(2,1)S(1)}, bf16[256,256]{1,0:T(8,128)(2,1)}, u32[]{:S(2)}) copy-start(bf16[256,256]{1,0:T(8,128)(2,1)} %constant.27.clone.il) | copy-start | bytes 393220
  5.0 19.3 %copy-start.8 = (bf16[256,512]{1,0:T(8,128)(2,1)S(1)}, bf16[256,512]{1,0:T(8,128)(2,1)}, u32[]{:S(2)}) copy-start(bf16[256,512]{1,0:T(8,128)(2,1)} %constant.23.clone.bl) | copy-start | bytes 786436
  5.0 19.3 %copy-start.9 = (bf16[256,512]{1,0:T(8,128)(2,1)S(1)}, bf16[256,512]{1,0:T(8,128)(2,1)}, u32[]{:S(2)}) copy-start(bf16[256,512]{1,0:T(8,128)(2,1)} %constant.22.clone.bh) | copy-start | bytes 786436
  5.0 19.3 %copy-start.10 = (bf16[512,256]{1,0:T(8,128)(2,1)S(1)}, bf16[512,256]{1,0:T(8,128)(2,1)}, u32[]{:S(2)}) copy-start(bf16[512,256]{1,0:T(8,128)(2,1)} %constant.21.clone.ol) | copy-start | bytes 786436
  24.3 0.9 %copy-start.16 = (bf16[256,256]{1,0:T(8,128)(2,1)S(1)}, bf16[256,256]{1,0:T(8,128)(2,1)}, u32[]{:S(2)}) copy-start(bf16[256,256]{1,0:T(8,128)(2,1)} %constant.26.clone.ih) | copy-start | bytes 393220
  25.2 0.9 %copy-start.17 = (bf16[256,256]{1,0:T(8,128)(2,1)S(1)}, bf16[256,256]{1,0:T(8,128)(2,1)}, u32[]{:S(2)}) copy-start(bf16[256,256]{1,0:T(8,128)(2,1)} %constant.25.clone.fl) | copy-start | bytes 393220
  26.1 0.9 %copy-start.18 = (bf16[256,256]{1,0:T(8,128)(2,1)S(1)}, bf16[256,256]{1,0:T(8,128)(2,1)}, u32[]{:S(2)}) copy-start(bf16[256,256]{1,0:T(8,128)(2,1)} %constant.24.clone.fh) | copy-start | bytes 393220
  29.1 15.7 %copy-start.1 = (bf16[64,512]{1,0:T(8,128)(2,1)S(1)}, bf16[64,512]{1,0:T(8,128)(2,1)}, u32[]{:S(2)}) copy-start(bf16[64,512]{1,0:T(8,128)(2,1)} %first_ref.3) | copy-start | bytes 196612
  29.1 15.7 %copy-start.3 = (bf16[64,512]{1,0:T(8,128)(2,1)S(1)}, bf16[64,512]{1,0:T(8,128)(2,1)}, u32[]{:S(2)}) copy-start(bf16[64,512]{1,0:T(8,128)(2,1)} %second_ref.3) | copy-start | bytes 196612
  29.1 15.7 %copy-start.5 = (bf16[64,512]{1,0:T(8,128)(2,1)S(1)}, bf16[64,512]{1,0:T(8,128)(2,1)}, u32[]{:S(2)}) copy-start(bf16[64,512]{1,0:T(8,128)(2,1)} %values_ref.3) | copy-start | bytes 196612
  29.1 15.7 %copy-start.7 = (bf16[64,512]{1,0:T(8,128)(2,1)S(1)}, bf16[64,512]{1,0:T(8,128)(2,1)}, u32[]{:S(2)}) copy-start(bf16[64,512]{1,0:T(8,128)(2,1)} %grad_ref.3) | copy-start | bytes 196612
  44.7 0.7 %copy-start.19 = (f32[64]{0:T(128)S(1)}, f32[64]{0:T(128)}, u32[]{:S(2)}) copy-start(f32[64]{0:T(128)} %param.20) | copy-start | bytes 772
where the time goes:
time: 46.9 us; the launch traced here: 46.4 us
  blocking collectives  34.9 us (74%)
  local copies, waits for them, and re-layouts  7.66 us (16%)
  Pallas kernels  3.01 us (6%)
  between operations  0.78 us (2%)
    all_to_all x2, blocking collectives, by_channels(): lax.all_to_all(slabs, 'ctx', split_axis=0, concat_axis=0, tiled=True)  34.9 us
    unnamed x40, local copies, waits for them, and re-layouts  7.66 us
    pallas_call x1, Pallas kernels, by_channels(): pl.pallas_call(spectral_kernel, out_shape=jax.ShapeDtypeStruct((shards, (...  2.02 us
    pallas_call x1, Pallas kernels, by_channels(): pl.pallas_call(output_kernel, out_shape=(full,) * 5 + (jax.ShapeDtypeStru...  0.96 us

commit v1 on v0

--- a/solution.py
+++ b/solution.py
@@ -15,41 +15,36 @@
 PARAMS = pltpu.CompilerParams(vmem_limit_bytes=48 * 1024 * 1024)
 
 
-def halves(table):
-    high = table.astype(np.float32).astype(jnp.bfloat16)
-    low = (table - high.astype(np.float64)).astype(np.float32).astype(jnp.bfloat16)
-    return high, low
-
-
 def make_tables(length):
     groups = length // LANES
     period = 2 * length
     turns = 2 * groups
     k1 = np.arange(groups + 1)
-    inner = np.arange(1, groups)
+    inner = k1[1:-1]
     a = np.arange(groups)
-    eye = np.eye(ROWS)
-    angle = 2.0 * np.pi / turns
-    outer = np.concatenate([np.cos(angle * (k1[:, None] * a % turns)), np.sin(angle * (inner[:, None] * a % turns))])
+    b = np.arange(LANES)
+    cosine = np.cos(2.0 * np.pi / turns * (k1[:, None] * a % turns))
+    sine = np.sin(2.0 * np.pi / turns * (inner[:, None] * a % turns))
     weight = np.where((k1 == 0) | (k1 == groups), 1.0, 2.0) / period
-    back = np.concatenate(
-        [weight[:, None] * np.cos(angle * (k1[:, None] * a % turns)), -2.0 / period * np.sin(angle * (inner[:, None] * a % turns))]
-    )
-    b = np.arange(LANES)
+    outer = np.concatenate([cosine, sine])
+    back = np.concatenate([weight[:, None] * cosine, -2.0 / period * sine]).T
     wave = 2.0 * np.pi / LANES * (b[:, None] * b % LANES)
-    cosine, sine = np.cos(wave), np.sin(wave)
-    lane_fwd = np.block([[cosine, -sine], [sine, cosine]])
-    lane_back = np.block([[cosine, sine], [-sine, cosine]])
     twist = 2.0 * np.pi / period * (k1[:, None] * b % period)
-    twist = np.repeat(twist, ROWS, axis=0)
-    return (
-        *halves(np.kron(outer, eye)),
-        *halves(np.kron(back.T, eye)),
-        *halves(lane_fwd),
-        *halves(lane_back),
-        np.cos(twist).astype(np.float32),
-        np.sin(twist).astype(np.float32),
-    )
+    parts = [np.repeat(outer, ROWS, axis=1), np.repeat(back, ROWS, axis=1)]
+    parts = [np.concatenate(np.split(part, part.shape[1] // LANES, axis=1)) for part in parts]
+    parts += [np.cos(wave), np.sin(wave), np.cos(twist), np.sin(twist)]
+    parts.append(np.zeros((-2 * (groups + 1) % ROWS, LANES)))
+    return np.concatenate(parts).astype(np.float32)
+
+
+def spread_rows(table, masked):
+    rows, columns = table.shape
+    wide = jnp.broadcast_to(table[:, None, :], (rows, ROWS, columns))
+    if masked:
+        shape = (ROWS, columns)
+        own = lax.broadcasted_iota(jnp.int32, shape, 0) == lax.broadcasted_iota(jnp.int32, shape, 1) % ROWS
+        wide = jnp.where(own[None], wide, 0.0)
+    return wide.reshape(rows * ROWS, columns)
 
 
 def split(data):
@@ -61,39 +56,48 @@
     return jnp.dot(left, right, preferred_element_type=jnp.float32)
 
 
-def table_left(high, low, data):
-    data_high, data_low = split(data)
-    return dot(high, data_high) + (dot(high, data_low) + dot(low, data_high))
-
-
-def table_right(data, high, low):
-    data_high, data_low = split(data)
-    return dot(data_high, high) + (dot(data_low, high) + dot(data_high, low))
-
-
-def gate_kernel(first_ref, second_ref, values_ref, filters_ref, grad_ref, out_ref):
-    mixed = first_ref[...].astype(jnp.float32) * values_ref[...].astype(jnp.float32)
-    carried = grad_ref[...].astype(jnp.float32) * second_ref[...].astype(jnp.float32)
-    shards = out_ref.shape[0]
-    tiles = filters_ref.shape[1] // LANES
-    for s, signal in enumerate((mixed, filters_ref[...], carried)):
-        for j in range(tiles):
-            tile = signal[:, j * LANES : (j + 1) * LANES].reshape(shards, ROWS, LANES)
-            row = (s * tiles + j) * ROWS
-            out_ref[:, row : row + ROWS, :] = tile
-
-
-def spectral_kernel(in_ref, oh, ol, bh, bl, fh, fl, ih, il, cos_ref, sin_ref, out_ref):
+def long_dot(left, right):
+    return dot(left[0], right[0]) + (dot(left[0], right[1]) + dot(left[1], right[0]))
+
+
+def read_tables(table_ref, groups):
+    tiles = groups * ROWS // LANES
+    row = 0
+
+    def take(rows, pieces=1):
+        nonlocal row
+        parts = [table_ref[row + i * rows : row + (i + 1) * rows, :] for i in range(pieces)]
+        row += rows * pieces
+        return jnp.concatenate(parts, axis=1)
+
+    outer = split(spread_rows(take(2 * groups, tiles), True))
+    back = split(spread_rows(take(groups, 2 * tiles), True))
+    cosine, sine = split(take(LANES)), split(take(LANES))
+    forward, inverse = [], []
+    for c, s in zip(cosine, sine):
+        forward.append(jnp.concatenate([jnp.concatenate([c, -s], axis=1), jnp.concatenate([s, c], axis=1)], axis=0))
+        inverse.append(jnp.concatenate([jnp.concatenate([c, s], axis=1), jnp.concatenate([-s, c], axis=1)], axis=0))
+    twist = (spread_rows(take(groups + 1), False), spread_rows(take(groups + 1), False))
+    return outer, back, forward, inverse, twist
+
+
+def spectral_kernel(in_ref, table_ref, out_ref):
     shards = in_ref.shape[0]
-    span = in_ref.shape[1] // 3
+    tiles = in_ref.shape[3] // LANES
+    span = tiles * ROWS
     rows = shards * span
     spec_rows = rows + ROWS
-    signals = [in_ref[:, s * span : (s + 1) * span, :].reshape(rows, LANES) for s in range(3)]
+    outer, back, forward, inverse, (cosine, sine) = read_tables(table_ref, rows // ROWS)
+
+    def take(s):
+        parts = [in_ref[:, s, :, j * LANES : (j + 1) * LANES] for j in range(tiles)]
+        return jnp.stack(parts, axis=1).reshape(rows, LANES)
+
+    signals = [take(s) for s in range(3)]
     total = jnp.sum((signals[0] * signals[2]).reshape(rows // ROWS, ROWS, LANES), axis=0)
     total = jnp.broadcast_to(jnp.sum(total, axis=1, keepdims=True), (ROWS, LANES))
     out_ref[:, 3 * span :, :] = jnp.broadcast_to(total[None], (shards, ROWS, LANES))
-    columns = table_left(oh[...], ol[...], jnp.concatenate(signals, axis=1))
-    cosine, sine = cos_ref[...], sin_ref[...]
+    columns = long_dot(outer, split(jnp.concatenate(signals, axis=1)))
     edge = jnp.zeros((ROWS, LANES), jnp.float32)
     spectra = []
     for s in range(3):
@@ -101,7 +105,7 @@
         real = columns[:spec_rows, lanes]
         imag = jnp.concatenate([edge, columns[spec_rows:, lanes], edge], axis=0)
         turned = jnp.concatenate([real * cosine - imag * sine, -(real * sine + imag * cosine)], axis=1)
-        spectra.append(table_right(turned, fh[...], fl[...]))
+        spectra.append(long_dot(split(turned), forward))
     (mr, mi), (fr, fi), (cr, ci) = [(x[:, :LANES], x[:, LANES:]) for x in spectra]
     products = (
         (fr * mr - fi * mi, fr * mi + fi * mr),
@@ -110,35 +114,31 @@
     )
     reverted = []
     for real, imag in products:
-        waves = table_right(jnp.concatenate([real, imag], axis=1), ih[...], il[...])
+        waves = long_dot(split(jnp.concatenate([real, imag], axis=1)), inverse)
         real, imag = waves[:, :LANES], waves[:, LANES:]
         turned_imag = real * sine + imag * cosine
         reverted.append(jnp.concatenate([real * cosine - imag * sine, turned_imag[ROWS:-ROWS]], axis=0))
-    result = table_left(bh[...], bl[...], jnp.concatenate(reverted, axis=1))
+    result = long_dot(back, split(jnp.concatenate(reverted, axis=1)))
     for s in range(3):
         out_ref[:, s * span : (s + 1) * span, :] = result[:, s * LANES : (s + 1) * LANES].reshape(shards, span, LANES)
 
 
-def output_kernel(in_ref, first_ref, second_ref, values_ref, grad_ref, gain_ref, out_ref, gfirst_ref, gsecond_ref, gvalues_ref, gfilters_ref, gskip_ref):
-    channels, blocks = first_ref.shape
+def output_kernel(in_ref, first_ref, second_ref, values_ref, grad_ref, out_ref, gfirst_ref, gsecond_ref, gvalues_ref, gfilters_ref, gskip_ref):
+    channels, blocks = out_ref.shape
     tiles = blocks // LANES
-    first = first_ref[...].astype(jnp.float32)
-    second = second_ref[...].astype(jnp.float32)
-    values = values_ref[...].astype(jnp.float32)
-    grad = grad_ref[...].astype(jnp.float32)
+
+    def take(s):
+        parts = [in_ref[:, (s * tiles + j) * ROWS : (s * tiles + j + 1) * ROWS, :].reshape(channels, LANES) for j in range(tiles)]
+        return jnp.concatenate(parts, axis=1)
+
+    before = take(0)
+    out_ref[...] = second_ref[...].astype(jnp.float32) * before
+    gsecond_ref[...] = grad_ref[...].astype(jnp.float32) * before
+    back = take(1)
+    gfirst_ref[...] = back * values_ref[...].astype(jnp.float32)
+    gvalues_ref[...] = back * first_ref[...].astype(jnp.float32)
+    gfilters_ref[...] = take(2)
     diagonal = lax.broadcasted_iota(jnp.int32, (channels, channels), 0) == lax.broadcasted_iota(jnp.int32, (channels, channels), 1)
-    gain = jnp.sum(jnp.where(diagonal, gain_ref[...], 0.0), axis=1, keepdims=True)
-    result = []
-    for s in range(3):
-        parts = [in_ref[:, (s * tiles + j) * ROWS : (s * tiles + j + 1) * ROWS, :].reshape(channels, LANES) for j in range(tiles)]
-        result.append(jnp.concatenate(parts, axis=1))
-    before = result[0] + gain * (first * values)
-    out_ref[...] = second * before
-    gsecond_ref[...] = grad * before
-    back = result[1] + gain * (grad * second)
-    gfirst_ref[...] = back * values
-    gvalues_ref[...] = back * first
-    gfilters_ref[...] = result[2]
     total = in_ref[:, 3 * tiles * ROWS :, :].reshape(channels, LANES)[:, :channels]
     gskip_ref[...] = jnp.sum(jnp.where(diagonal, total, 0.0), axis=0, keepdims=True)
 
@@ -149,30 +149,27 @@
     tiles = blocks // LANES
     length = blocks * shards
     full = jax.ShapeDtypeStruct((channels, blocks), jnp.float32)
-    slabs = pl.pallas_call(
-        gate_kernel,
-        out_shape=jax.ShapeDtypeStruct((shards, 3 * tiles * ROWS, LANES), jnp.float32),
-        in_specs=[VMEM] * 5,
-        out_specs=VMEM,
-        compiler_params=PARAMS,
-    )(first_gate, second_gate, values, filters, grad_output)
+    mixed = first_gate.astype(jnp.float32) * values.astype(jnp.float32)
+    carried = grad_output.astype(jnp.float32) * second_gate.astype(jnp.float32)
+    first_tap = (lax.broadcasted_iota(jnp.int32, filters.shape, 1) == 0) & (lax.axis_index("ctx") == 0)
+    filters = filters + jnp.where(first_tap, skip_gain[:, None], 0.0)
+    slabs = jnp.stack([x.reshape(shards, ROWS, blocks) for x in (mixed, filters, carried)], axis=1)
     slabs = lax.all_to_all(slabs, "ctx", split_axis=0, concat_axis=0, tiled=True)
-    tables = make_tables(length)
     slabs = pl.pallas_call(
         spectral_kernel,
         out_shape=jax.ShapeDtypeStruct((shards, (3 * tiles + 1) * ROWS, LANES), jnp.float32),
-        in_specs=[VMEM] * (1 + len(tables)),
+        in_specs=[VMEM] * 2,
         out_specs=VMEM,
         compiler_params=PARAMS,
-    )(slabs, *tables)
+    )(slabs, make_tables(length))
     slabs = lax.all_to_all(slabs, "ctx", split_axis=0, concat_axis=0, tiled=True)
     *wide, grad_skip = pl.pallas_call(
         output_kernel,
         out_shape=(full,) * 5 + (jax.ShapeDtypeStruct((1, channels), jnp.float32),),
-        in_specs=[VMEM] * 6,
+        in_specs=[VMEM] * 5,
         out_specs=(VMEM,) * 6,
         compiler_params=PARAMS,
-    )(slabs, first_gate, second_gate, values, grad_output, skip_gain.reshape(1, channels))
+    )(slabs, first_gate, second_gate, values, grad_output)
     return (*wide, grad_skip.reshape(channels))
 
 

time: 46.9 us -> 40 us (0.85)
  local copies, waits for them, and re-layouts: 7.66 us -> 0.08 us
  other arithmetic: 0 us -> 1.05 us
    unnamed x40 -> x14, local copies, waits for them, and re-layouts: 7.66 us -> 0.08 us
    another operation x0 -> x3, other arithmetic: none -> 1.04 us  [by_channels(): jnp.stack([x.reshape(shards, ROWS, blocks) for x in (mixed, filters, carr...]
where the time goes in v1:
time: 40 us; the launch traced here: 39.7 us
  blocking collectives  34.9 us (87%)
  Pallas kernels  2.93 us (7%)
  other arithmetic  1.05 us (3%)
  between operations  0.75 us (2%)
    all_to_all x2, blocking collectives, by_channels(): lax.all_to_all(slabs, 'ctx', split_axis=0, concat_axis=0, tiled=True)  34.9 us
    pallas_call x1, Pallas kernels, by_channels(): pl.pallas_call(spectral_kernel, out_shape=jax.ShapeDtypeStruct((shards, (...  2.06 us
    another operation x3, other arithmetic, by_channels(): jnp.stack([x.reshape(shards, ROWS, blocks) for x in (mixed, filters, carr...  1.04 us
    pallas_call x1, Pallas kernels, by_channels(): pl.pallas_call(output_kernel, out_shape=(full,) * 5 + (jax.ShapeDtypeStru...  0.87 us

profile of v1, /device:TPU:0, one launch (start us, length us, event | category | flops | bytes accessed | tf_op | source)
XLA Modules:
  0.0 39.7 jit_solution(3212465209341275521)
XLA Ops:
  0.6 0.0 copy-start.6
  0.7 0.0 copy-start.3
  0.7 0.0 copy-start.4
  0.7 0.0 copy-start.5
  0.7 0.9 %multiply_bitcast_fusion.1 = f32[8,1,8,512]{3,2,1,0:T(8,128)S(1)} fusion(bf16[64,512]{1,0:T(8,128)(2,1)} %values_ref.1, bf16[64,512]{1,0:T(8,128)(2,1)} %first_ref.1), kind=kLoop, calls=%fused_computation.3 | loop fusion | flops 98304 | bytes 262144 | tf_op jit(solution)/shard_map/stack;reshape | solution.py:156
  1.6 0.0 copy-done.6
  1.6 0.0 copy-done.3
  1.7 0.0 copy-done.4
  1.7 0.0 copy-done.5
  1.7 0.1 multiply_bitcast_fusion
  1.8 0.0 copy-start
  1.8 19.3 %all_to_all.10.in_ref = f32[8,3,8,512]{3,2,1,0:T(8,128)S(1)} all-to-all(f32[8,3,8,512]{3,2,1,0:T(8,128)S(1)} %pad_maximum_fusion), channel_id=1, replica_groups=mesh['groups'=2,'ctx'=8,'chan'=2] {'ctx'}, dimensions={0} | all-to-all | bytes 786432 | tf_op jit(solution)/shard_map/all_to_all | solution.py:157
  21.1 0.0 copy-done
  21.1 2.1 %shard_map.118 = f32[8,104,128]{2,1,0:T(8,128)S(1)} custom-call(f32[8,3,8,512]{3,2,1,0:T(8,128)S(1)} %all_to_all.10.in_ref, f32[584,128]{1,0:T(8,128)S(1)} %copy-done), custom_call_target="tpu_custom_call" | custom-call | tf_op jit(solution)/shard_map/pallas_call | solution.py:158
  23.2 0.0 copy-start.1
  23.2 0.0 copy-start.2
  23.2 15.6 %all_to_all.11.in_ref = f32[8,104,128]{2,1,0:T(8,128)S(1)} all-to-all(f32[8,104,128]{2,1,0:T(8,128)S(1)} %shard_map.118), channel_id=1, replica_groups=mesh['groups'=2,'ctx'=8,'chan'=2] {'ctx'}, dimensions={0} | all-to-all | bytes 851968 | tf_op jit(solution)/shard_map/all_to_all | solution.py:165
  38.8 0.0 copy-done.1
  38.9 0.0 copy-done.2
  38.9 0.9 %shard_map.119 = (f32[64,512]{1,0:T(8,128)}, f32[64,512]{1,0:T(8,128)}, f32[64,512]{1,0:T(8,128)}, f32[64,512]{1,0:T(8,128)}, f32[64,512]{1,0:T(8,128)}, /*index=5*/f32[1,64]{1,0:T(1,128)}) custom-call(f32[8,104,128]{2,1,0:T(8,128)S(1)} %all_to_all.11.in_ref, bf16[64,512]{1,0:T(8,128)(2,1)S(1)} %copy-done.2, bf16[64,512]{1,0:T(8,128)(2,1)S(1)} %copy-done.3, ...), custom_call_target="tpu_custom_call" | custom-call | tf_op jit(solution)/shard_map/pallas_call | solution.py:166
  (2 shorter events, 0.0 us)
Async XLA Ops:
  0.6 1.0 %copy-start.6 = (f32[64]{0:T(128)S(1)}, f32[64]{0:T(128)}, u32[]{:S(2)}) copy-start(f32[64]{0:T(128)} %param.11) | copy-start | bytes 772
  0.7 1.0 %copy-start.3 = (bf16[64,512]{1,0:T(8,128)(2,1)S(1)}, bf16[64,512]{1,0:T(8,128)(2,1)}, u32[]{:S(2)}) copy-start(bf16[64,512]{1,0:T(8,128)(2,1)} %second_ref.1) | copy-start | bytes 196612
  0.7 1.0 %copy-start.4 = (bf16[64,512]{1,0:T(8,128)(2,1)S(1)}, bf16[64,512]{1,0:T(8,128)(2,1)}, u32[]{:S(2)}) copy-start(bf16[64,512]{1,0:T(8,128)(2,1)} %grad_ref.1) | copy-start | bytes 196612
  0.7 1.0 %copy-start.5 = (f32[64,512]{1,0:T(8,128)S(1)}, f32[64,512]{1,0:T(8,128)}, u32[]{:S(2)}) copy-start(f32[64,512]{1,0:T(8,128)} %param.10) | copy-start | bytes 393220
  1.8 19.3 %copy-start = (f32[584,128]{1,0:T(8,128)S(1)}, f32[584,128]{1,0:T(8,128)}, u32[]{:S(2)}) copy-start(f32[584,128]{1,0:T(8,128)} %constant.13.clone.table_ref) | copy-start | bytes 897028
  23.2 15.7 %copy-start.1 = (bf16[64,512]{1,0:T(8,128)(2,1)S(1)}, bf16[64,512]{1,0:T(8,128)(2,1)}, u32[]{:S(2)}) copy-start(bf16[64,512]{1,0:T(8,128)(2,1)} %values_ref.1) | copy-start | bytes 196612
  23.2 15.7 %copy-start.2 = (bf16[64,512]{1,0:T(8,128)(2,1)S(1)}, bf16[64,512]{1,0:T(8,128)(2,1)}, u32[]{:S(2)}) copy-start(bf16[64,512]{1,0:T(8,128)(2,1)} %first_ref.1) | copy-start | bytes 196612

commit v2 on v1

--- a/solution.py
+++ b/solution.py
@@ -12,6 +12,7 @@
 LANES = 128
 ROWS = 8
 VMEM = pl.BlockSpec(memory_space=pltpu.VMEM)
+HBM = pl.BlockSpec(memory_space=pltpu.HBM)
 PARAMS = pltpu.CompilerParams(vmem_limit_bytes=48 * 1024 * 1024)
 
 
@@ -60,34 +61,87 @@
     return dot(left[0], right[0]) + (dot(left[0], right[1]) + dot(left[1], right[0]))
 
 
-def read_tables(table_ref, groups):
-    tiles = groups * ROWS // LANES
+def table_kernel(in_ref, outer_ref, back_ref, forward_ref, inverse_ref, twist_ref):
+    groups = outer_ref.shape[2] // ROWS
+    tiles = outer_ref.shape[2] // LANES
     row = 0
 
     def take(rows, pieces=1):
         nonlocal row
-        parts = [table_ref[row + i * rows : row + (i + 1) * rows, :] for i in range(pieces)]
+        parts = [in_ref[row + i * rows : row + (i + 1) * rows, :] for i in range(pieces)]
         row += rows * pieces
         return jnp.concatenate(parts, axis=1)
 
-    outer = split(spread_rows(take(2 * groups, tiles), True))
-    back = split(spread_rows(take(groups, 2 * tiles), True))
+    outer_ref[0], outer_ref[1] = split(spread_rows(take(2 * groups, tiles), True))
+    back_ref[0], back_ref[1] = split(spread_rows(take(groups, 2 * tiles), True))
     cosine, sine = split(take(LANES)), split(take(LANES))
-    forward, inverse = [], []
-    for c, s in zip(cosine, sine):
-        forward.append(jnp.concatenate([jnp.concatenate([c, -s], axis=1), jnp.concatenate([s, c], axis=1)], axis=0))
-        inverse.append(jnp.concatenate([jnp.concatenate([c, s], axis=1), jnp.concatenate([-s, c], axis=1)], axis=0))
-    twist = (spread_rows(take(groups + 1), False), spread_rows(take(groups + 1), False))
-    return outer, back, forward, inverse, twist
-
-
-def spectral_kernel(in_ref, table_ref, out_ref):
-    shards = in_ref.shape[0]
+    for i, (c, s) in enumerate(zip(cosine, sine)):
+        forward_ref[i] = jnp.concatenate([jnp.concatenate([c, -s], axis=1), jnp.concatenate([s, c], axis=1)], axis=0)
+        inverse_ref[i] = jnp.concatenate([jnp.concatenate([c, s], axis=1), jnp.concatenate([-s, c], axis=1)], axis=0)
+    twist_ref[0] = spread_rows(take(groups + 1), False)
+    twist_ref[1] = spread_rows(take(groups + 1), False)
+
+
+def partners(shards):
+    far = shards // 2
+    return [*range(shards - 1, far - 1, -1), *range(far - 1, -1, -1)] if shards != 8 else [7, 5, 6, 4, 3, 2, 1, 0]
+
+
+def swap(slabs):
+    shards = len(slabs)
+    moved = []
+    for turn, slab in zip(partners(shards), slabs):
+        pairs = [(i, i ^ turn) for i in range(shards)]
+        moved.append(lax.ppermute(slab, "ctx", pairs) if turn else slab)
+    return moved
+
+
+def gate_kernel(first_hbm, values_hbm, grad_hbm, second_hbm, filters_hbm, gain_hbm, *refs):
+    *out_refs, kept_ref, all_ref, filters_ref, gain_ref, sems = refs
+    gates = [kept_ref.at[i] for i in range(4)]
+    sources = (first_hbm, values_hbm, filters_hbm, gain_hbm, grad_hbm, second_hbm)
+    places = (*gates[:2], filters_ref, gain_ref, *gates[2:])
+    copies = [pltpu.make_async_copy(source, place, sems.at[i]) for i, (source, place) in enumerate(zip(sources, places))]
+    for copy in copies:
+        copy.start()
+    shards = len(out_refs)
+    channels, blocks = filters_ref.shape
+    me = lax.axis_index("ctx")
+
+    def place(s, signal):
+        for j in range(blocks // LANES):
+            tile = signal[:, j * LANES : (j + 1) * LANES].reshape(shards, ROWS, LANES)
+            all_ref[:, s, :, j * LANES : (j + 1) * LANES] = tile
+
+    copies[0].wait()
+    copies[1].wait()
+    place(0, kept_ref[0].astype(jnp.float32) * kept_ref[1].astype(jnp.float32))
+    copies[2].wait()
+    copies[3].wait()
+    shape = (channels, channels)
+    diagonal = lax.broadcasted_iota(jnp.int32, shape, 0) == lax.broadcasted_iota(jnp.int32, shape, 1)
+    gain = jnp.sum(jnp.where(diagonal, gain_ref[...], 0.0), axis=1, keepdims=True)
+    position = me * blocks + lax.broadcasted_iota(jnp.int32, (channels, blocks), 1)
+    place(1, filters_ref[...] + jnp.where(position == 0, gain, 0.0))
+    copies[4].wait()
+    copies[5].wait()
+    place(2, kept_ref[2].astype(jnp.float32) * kept_ref[3].astype(jnp.float32))
+    for turn, out_ref in zip(partners(shards), out_refs):
+        out_ref[...] = all_ref[me ^ turn]
+
+
+def spectral_kernel(outer_ref, back_ref, forward_ref, inverse_ref, twist_ref, *refs):
+    *refs, all_ref, in_ref = refs
+    shards = len(refs) // 2
+    in_refs, out_refs = refs[:shards], refs[shards:]
+    me = lax.axis_index("ctx")
+    for turn, ref in zip(partners(shards), in_refs):
+        in_ref[me ^ turn] = ref[...]
     tiles = in_ref.shape[3] // LANES
     span = tiles * ROWS
     rows = shards * span
     spec_rows = rows + ROWS
-    outer, back, forward, inverse, (cosine, sine) = read_tables(table_ref, rows // ROWS)
+    cosine, sine = twist_ref[0], twist_ref[1]
 
     def take(s):
         parts = [in_ref[:, s, :, j * LANES : (j + 1) * LANES] for j in range(tiles)]
@@ -96,8 +150,8 @@
     signals = [take(s) for s in range(3)]
     total = jnp.sum((signals[0] * signals[2]).reshape(rows // ROWS, ROWS, LANES), axis=0)
     total = jnp.broadcast_to(jnp.sum(total, axis=1, keepdims=True), (ROWS, LANES))
-    out_ref[:, 3 * span :, :] = jnp.broadcast_to(total[None], (shards, ROWS, LANES))
-    columns = long_dot(outer, split(jnp.concatenate(signals, axis=1)))
+    all_ref[:, 3 * span :, :] = jnp.broadcast_to(total[None], (shards, ROWS, LANES))
+    columns = long_dot(outer_ref, split(jnp.concatenate(signals, axis=1)))
     edge = jnp.zeros((ROWS, LANES), jnp.float32)
     spectra = []
     for s in range(3):
@@ -105,7 +159,7 @@
         real = columns[:spec_rows, lanes]
         imag = jnp.concatenate([edge, columns[spec_rows:, lanes], edge], axis=0)
         turned = jnp.concatenate([real * cosine - imag * sine, -(real * sine + imag * cosine)], axis=1)
-        spectra.append(long_dot(split(turned), forward))
+        spectra.append(long_dot(split(turned), forward_ref))
     (mr, mi), (fr, fi), (cr, ci) = [(x[:, :LANES], x[:, LANES:]) for x in spectra]
     products = (
         (fr * mr - fi * mi, fr * mi + fi * mr),
@@ -114,33 +168,50 @@
     )
     reverted = []
     for real, imag in products:
-        waves = long_dot(split(jnp.concatenate([real, imag], axis=1)), inverse)
+        waves = long_dot(split(jnp.concatenate([real, imag], axis=1)), inverse_ref)
         real, imag = waves[:, :LANES], waves[:, LANES:]
         turned_imag = real * sine + imag * cosine
         reverted.append(jnp.concatenate([real * cosine - imag * sine, turned_imag[ROWS:-ROWS]], axis=0))
-    result = long_dot(back, split(jnp.concatenate(reverted, axis=1)))
+    result = long_dot(back_ref, split(jnp.concatenate(reverted, axis=1)))
     for s in range(3):
-        out_ref[:, s * span : (s + 1) * span, :] = result[:, s * LANES : (s + 1) * LANES].reshape(shards, span, LANES)
-
-
-def output_kernel(in_ref, first_ref, second_ref, values_ref, grad_ref, out_ref, gfirst_ref, gsecond_ref, gvalues_ref, gfilters_ref, gskip_ref):
-    channels, blocks = out_ref.shape
+        all_ref[:, s * span : (s + 1) * span, :] = result[:, s * LANES : (s + 1) * LANES].reshape(shards, span, LANES)
+    for turn, out_ref in zip(partners(shards), out_refs):
+        out_ref[...] = all_ref[me ^ turn]
+
+
+def output_kernel(kept_ref, *refs):
+    _, channels, blocks = kept_ref.shape
     tiles = blocks // LANES
-
-    def take(s):
-        parts = [in_ref[:, (s * tiles + j) * ROWS : (s * tiles + j + 1) * ROWS, :].reshape(channels, LANES) for j in range(tiles)]
-        return jnp.concatenate(parts, axis=1)
-
-    before = take(0)
-    out_ref[...] = second_ref[...].astype(jnp.float32) * before
-    gsecond_ref[...] = grad_ref[...].astype(jnp.float32) * before
-    back = take(1)
-    gfirst_ref[...] = back * values_ref[...].astype(jnp.float32)
-    gvalues_ref[...] = back * first_ref[...].astype(jnp.float32)
-    gfilters_ref[...] = take(2)
-    diagonal = lax.broadcasted_iota(jnp.int32, (channels, channels), 0) == lax.broadcasted_iota(jnp.int32, (channels, channels), 1)
-    total = in_ref[:, 3 * tiles * ROWS :, :].reshape(channels, LANES)[:, :channels]
-    gskip_ref[...] = jnp.sum(jnp.where(diagonal, total, 0.0), axis=0, keepdims=True)
+    shards = channels // ROWS
+    in_refs, (out_ref, gfirst_ref, gsecond_ref, gvalues_ref, gfilters_ref, gskip_ref, result_ref, total_ref) = refs[:shards], refs[shards:]
+    me = lax.axis_index("ctx")
+    for turn, in_ref in zip(partners(shards), in_refs):
+        own = pl.ds(pl.multiple_of((me ^ turn) * ROWS, ROWS), ROWS)
+        for s, dst_ref in enumerate((result_ref.at[0], result_ref.at[1], gfilters_ref)):
+            for j in range(tiles):
+                dst_ref[own, j * LANES : (j + 1) * LANES] = in_ref[(s * tiles + j) * ROWS : (s * tiles + j + 1) * ROWS, :]
+        total_ref[own, :] = in_ref[3 * tiles * ROWS :, :]
+    first, values, grad, second = [kept_ref[i].astype(jnp.float32) for i in range(4)]
+    before = result_ref[0]
+    out_ref[...] = second * before
+    gsecond_ref[...] = grad * before
+    back = result_ref[1]
+    gfirst_ref[...] = back * values
+    gvalues_ref[...] = back * first
+    shape = (channels, channels)
+    diagonal = lax.broadcasted_iota(jnp.int32, shape, 0) == lax.broadcasted_iota(jnp.int32, shape, 1)
+    gskip_ref[...] = jnp.sum(jnp.where(diagonal, total_ref[:, :channels], 0.0), axis=0, keepdims=True)
+
+
+def call(kernel, out_shape, args, scratch_shapes=()):
+    return pl.pallas_call(
+        kernel,
+        out_shape=out_shape,
+        in_specs=[VMEM] * len(args),
+        out_specs=[VMEM] * len(out_shape),
+        scratch_shapes=scratch_shapes,
+        compiler_params=PARAMS,
+    )(*args)
 
 
 def by_channels(first_gate, second_gate, values, filters, skip_gain, grad_output):
@@ -148,29 +219,47 @@
     shards = lax.axis_size("ctx")
     tiles = blocks // LANES
     length = blocks * shards
-    full = jax.ShapeDtypeStruct((channels, blocks), jnp.float32)
-    mixed = first_gate.astype(jnp.float32) * values.astype(jnp.float32)
-    carried = grad_output.astype(jnp.float32) * second_gate.astype(jnp.float32)
-    first_tap = (lax.broadcasted_iota(jnp.int32, filters.shape, 1) == 0) & (lax.axis_index("ctx") == 0)
-    filters = filters + jnp.where(first_tap, skip_gain[:, None], 0.0)
-    slabs = jnp.stack([x.reshape(shards, ROWS, blocks) for x in (mixed, filters, carried)], axis=1)
-    slabs = lax.all_to_all(slabs, "ctx", split_axis=0, concat_axis=0, tiled=True)
-    slabs = pl.pallas_call(
+    rows = length // LANES * ROWS
+    wide, half = jnp.float32, jnp.bfloat16
+    sources = (first_gate, values, grad_output, second_gate, filters, skip_gain.reshape(1, channels))
+    *slabs, kept = pl.pallas_call(
+        gate_kernel,
+        out_shape=[pltpu.VMEM((3, ROWS, blocks), wide)] * shards + [pltpu.VMEM((4, channels, blocks), half)],
+        in_specs=[HBM] * len(sources),
+        out_specs=[VMEM] * (shards + 1),
+        scratch_shapes=[
+            pltpu.VMEM((shards, 3, ROWS, blocks), wide),
+            pltpu.VMEM((channels, blocks), wide),
+            pltpu.VMEM((1, channels), wide),
+            pltpu.SemaphoreType.DMA((len(sources),)),
+        ],
+        compiler_params=PARAMS,
+    )(*[pltpu.with_memory_space_constraint(source, pltpu.HBM) for source in sources])
+    tables = call(
+        table_kernel,
+        [
+            pltpu.VMEM((2, 2 * rows, rows), half),
+            pltpu.VMEM((2, rows, 2 * rows), half),
+            pltpu.VMEM((2, 2 * LANES, 2 * LANES), half),
+            pltpu.VMEM((2, 2 * LANES, 2 * LANES), half),
+            pltpu.VMEM((2, rows + ROWS, LANES), wide),
+        ],
+        [jnp.asarray(make_tables(length))],
+    )
+    slab = ((3 * tiles + 1) * ROWS, LANES)
+    slabs = call(
         spectral_kernel,
-        out_shape=jax.ShapeDtypeStruct((shards, (3 * tiles + 1) * ROWS, LANES), jnp.float32),
-        in_specs=[VMEM] * 2,
-        out_specs=VMEM,
-        compiler_params=PARAMS,
-    )(slabs, make_tables(length))
-    slabs = lax.all_to_all(slabs, "ctx", split_axis=0, concat_axis=0, tiled=True)
-    *wide, grad_skip = pl.pallas_call(
+        [pltpu.VMEM(slab, wide)] * shards,
+        (*tables, *swap(slabs)),
+        [pltpu.VMEM((shards, *slab), wide), pltpu.VMEM((shards, 3, ROWS, blocks), wide)],
+    )
+    *full, grad_skip = call(
         output_kernel,
-        out_shape=(full,) * 5 + (jax.ShapeDtypeStruct((1, channels), jnp.float32),),
-        in_specs=[VMEM] * 5,
-        out_specs=(VMEM,) * 6,
-        compiler_params=PARAMS,
-    )(slabs, first_gate, second_gate, values, grad_output)
-    return (*wide, grad_skip.reshape(channels))
+        [jax.ShapeDtypeStruct((channels, blocks), wide)] * 5 + [jax.ShapeDtypeStruct((1, channels), wide)],
+        (kept, *swap(slabs)),
+        [pltpu.VMEM((2, channels, blocks), wide), pltpu.VMEM((channels, LANES), wide)],
+    )
+    return (*full, grad_skip.reshape(channels))
 
 
 def turn_table(first_index, second_index, period):

time: 40 us -> 36.9 us (0.922)
  blocking collectives: 34.9 us -> 0 us
  starting transfers between devices: 0 us -> 22.3 us
  waiting for transfers between devices: 0 us -> 9.32 us
  Pallas kernels: 2.93 us -> 4.51 us
  other arithmetic: 1.05 us -> 0 us
    all_to_all x2 -> x0, blocking collectives: 34.9 us -> none  [by_channels(): lax.all_to_all(slabs, 'ctx', split_axis=0, concat_axis=0, tiled=True)]
    ppermute x0 -> x14, starting transfers between devices: none -> 22.3 us  [swap(): moved.append(lax.ppermute(slab, 'ctx', pairs) if turn else slab)]
    ppermute x0 -> x14, waiting for transfers between devices: none -> 9.32 us  [swap(): moved.append(lax.ppermute(slab, 'ctx', pairs) if turn else slab)]
    pallas_call x2 -> x4, Pallas kernels: 2.93 us -> 4.51 us  [the longest x3 3.3 us: call(): pl.pallas_call(kernel, out_shape=out_shape, in_specs=[VMEM] * len(args),...]
    another operation x3 -> x0, other arithmetic: 1.04 us -> none  [by_channels(): jnp.stack([x.reshape(shards, ROWS, blocks) for x in (mixed, filters, carr...]
  transfers between devices with their start and end apart: 0 -> 14, of which waited for: 0 -> 9; matrix products, arithmetic and copies ran while one was open for 0% -> 0% of each run, Pallas kernels for 0% -> 1%
where the time goes in v2:
time: 36.9 us; the launch traced here: 36.8 us
  starting transfers between devices  22.3 us (60%)
  waiting for transfers between devices  9.32 us (25%)
  Pallas kernels  4.51 us (12%)
  between operations  0.68 us (2%)
    ppermute x14, starting transfers between devices, swap(): moved.append(lax.ppermute(slab, 'ctx', pairs) if turn else slab)  22.3 us
    ppermute x14, waiting for transfers between devices, swap(): moved.append(lax.ppermute(slab, 'ctx', pairs) if turn else slab)  9.32 us
    pallas_call x3, Pallas kernels, call(): pl.pallas_call(kernel, out_shape=out_shape, in_specs=[VMEM] * len(args),...  3.3 us
    pallas_call x1, Pallas kernels, by_channels(): pl.pallas_call(gate_kernel, out_shape=[pltpu.VMEM((3, ROWS, blocks), wide...  1.21 us
  transfers between devices with their start and end apart: 14, of which 9 were waited for; matrix products, arithmetic and copies ran while one was open for 0% of the time, Pallas kernels for 1%

profile of v2, /device:TPU:0, one launch (start us, length us, event | category | flops | bytes accessed | tf_op | source)
XLA Modules:
  0.0 36.8 jit_solution(14262149320098953182)
XLA Ops:
  0.6 1.2 %shard_map.118 = (f32[3,8,512]{2,1,0:T(8,128)S(1)}, f32[3,8,512]{2,1,0:T(8,128)S(1)}, f32[3,8,512]{2,1,0:T(8,128)S(1)}, f32[3,8,512]{2,1,0:T(8,128)S(1)}, f32[3,...) custom-call(bf16[64,512]{1,0:T(8,128)(2,1)} %first_hbm.1, ...), custom_call_target="tpu_custom_call" | custom-call | tf_op jit(solution)/shard_map/pallas_call | solution.py:225
  1.9 6.0 %collective-permute-start = (f32[3,8,512]{2,1,0:T(8,128)S(1)}, f32[3,8,512]{2,1,0:T(8,128)S(1)}, u32[]{:S(2)}, u32[]{:S(2)}) collective-permute-start(f32[3,8,512]{2,1,0:T(8,128)S(1)} %get-tuple-element.40), channel_id=1, source_target_pairs={{0,14},{2,12},{4,10},{6,8},{8,6},{10,4},{12,2},{14,0},{1,15},{3,13... | collective-permute-start | bytes 147464 | tf_op jit(solution)/shard_map/ppermute | solution.py:95
  7.9 1.9 %collective-permute-start.2 = (f32[3,8,512]{2,1,0:T(8,128)S(1)}, f32[3,8,512]{2,1,0:T(8,128)S(1)}, u32[]{:S(2)}, u32[]{:S(2)}) collective-permute-start(f32[3,8,512]{2,1,0:T(8,128)S(1)} %get-tuple-element.42), channel_id=1, source_target_pairs={{0,12},{2,14},{4,8},{6,10},{8,4},{10,6},{12,0},{14,2},{1,13},{3,15... | collective-permute-start | bytes 147464 | tf_op jit(solution)/shard_map/ppermute | solution.py:95
  9.8 1.0 %collective-permute-start.3 = (f32[3,8,512]{2,1,0:T(8,128)S(1)}, f32[3,8,512]{2,1,0:T(8,128)S(1)}, u32[]{:S(2)}, u32[]{:S(2)}) collective-permute-start(f32[3,8,512]{2,1,0:T(8,128)S(1)} %get-tuple-element.43), channel_id=1, source_target_pairs={{0,8},{2,10},{4,12},{6,14},{8,0},{10,2},{12,4},{14,6},{1,9},{3,11}... | collective-permute-start | bytes 147464 | tf_op jit(solution)/shard_map/ppermute | solution.py:95
  10.8 1.8 %collective-permute-start.4 = (f32[3,8,512]{2,1,0:T(8,128)S(1)}, f32[3,8,512]{2,1,0:T(8,128)S(1)}, u32[]{:S(2)}, u32[]{:S(2)}) collective-permute-start(f32[3,8,512]{2,1,0:T(8,128)S(1)} %get-tuple-element.44), channel_id=1, source_target_pairs={{0,6},{2,4},{4,2},{6,0},{8,14},{10,12},{12,10},{14,8},{1,7},{3,5},... | collective-permute-start | bytes 147464 | tf_op jit(solution)/shard_map/ppermute | solution.py:95
  12.6 1.1 %collective-permute-start.5 = (f32[3,8,512]{2,1,0:T(8,128)S(1)}, f32[3,8,512]{2,1,0:T(8,128)S(1)}, u32[]{:S(2)}, u32[]{:S(2)}) collective-permute-start(f32[3,8,512]{2,1,0:T(8,128)S(1)} %get-tuple-element.45), channel_id=1, source_target_pairs={{0,4},{2,6},{4,0},{6,2},{8,12},{10,14},{12,8},{14,10},{1,5},{3,7},... | collective-permute-start | bytes 147464 | tf_op jit(solution)/shard_map/ppermute | solution.py:95
  13.8 1.7 %collective-permute-done.1.refs_1_ = f32[3,8,512]{2,1,0:T(8,128)S(1)} collective-permute-done((f32[3,8,512]{2,1,0:T(8,128)S(1)}, f32[3,8,512]{2,1,0:T(8,128)S(1)}, u32[]{:S(2)}, u32[]{:S(2)}) %collective-permute-start.1) | collective-permute-done | bytes 49184 | tf_op jit(solution)/shard_map/ppermute | solution.py:95
  15.4 0.7 %collective-permute-start.6 = (f32[3,8,512]{2,1,0:T(8,128)S(1)}, f32[3,8,512]{2,1,0:T(8,128)S(1)}, u32[]{:S(2)}, u32[]{:S(2)}) collective-permute-start(f32[3,8,512]{2,1,0:T(8,128)S(1)} %get-tuple-element.46), channel_id=1, source_target_pairs={{0,2},{2,0},{4,6},{6,4},{8,10},{10,8},{12,14},{14,12},{1,3},{3,1},... | collective-permute-start | bytes 147464 | tf_op jit(solution)/shard_map/ppermute | solution.py:95
  16.1 0.3 shard_map.119
  16.4 0.4 collective-permute-done.3.refs_3_
  16.8 0.5 %collective-permute-done.5.refs_5_ = f32[3,8,512]{2,1,0:T(8,128)S(1)} collective-permute-done((f32[3,8,512]{2,1,0:T(8,128)S(1)}, f32[3,8,512]{2,1,0:T(8,128)S(1)}, u32[]{:S(2)}, u32[]{:S(2)}) %collective-permute-start.5) | collective-permute-done | bytes 49184 | tf_op jit(solution)/shard_map/ppermute | solution.py:95
  17.2 2.3 %collective-permute-done.6.refs_6_ = f32[3,8,512]{2,1,0:T(8,128)S(1)} collective-permute-done((f32[3,8,512]{2,1,0:T(8,128)S(1)}, f32[3,8,512]{2,1,0:T(8,128)S(1)}, u32[]{:S(2)}, u32[]{:S(2)}) %collective-permute-start.6) | collective-permute-done | bytes 49184 | tf_op jit(solution)/shard_map/ppermute | solution.py:95
  19.5 2.1 %shard_map.120 = (f32[104,128]{1,0:T(8,128)S(1)}, f32[104,128]{1,0:T(8,128)S(1)}, f32[104,128]{1,0:T(8,128)S(1)}, f32[104,128]{1,0:T(8,128)S(1)}, f32[104,128]{1...) custom-call(bf16[2,512,256]{2,1,0:T(8,128)(2,1)S(1)} %get-tuple-element.35.outer_ref, ...), custom_call_target="tpu_custom_call" | custom-call | tf_op jit(solution)/shard_map/pallas_call | solution.py:207
  21.6 3.2 %collective-permute-start.7 = (f32[104,128]{1,0:T(8,128)S(1)}, f32[104,128]{1,0:T(8,128)S(1)}, u32[]{:S(2)}, u32[]{:S(2)}) collective-permute-start(f32[104,128]{1,0:T(8,128)S(1)} %get-tuple-element.48), channel_id=1, source_target_pairs={{0,14},{2,12},{4,10},{6,8},{8,6},{10,4},{12,2},{14,0},{1,15},{3,13... | collective-permute-start | bytes 159752 | tf_op jit(solution)/shard_map/ppermute | solution.py:95
  24.8 0.9 %collective-permute-start.9 = (f32[104,128]{1,0:T(8,128)S(1)}, f32[104,128]{1,0:T(8,128)S(1)}, u32[]{:S(2)}, u32[]{:S(2)}) collective-permute-start(f32[104,128]{1,0:T(8,128)S(1)} %get-tuple-element.50), channel_id=1, source_target_pairs={{0,12},{2,14},{4,8},{6,10},{8,4},{10,6},{12,0},{14,2},{1,13},{3,15... | collective-permute-start | bytes 159752 | tf_op jit(solution)/shard_map/ppermute | solution.py:95
  25.8 2.7 %collective-permute-start.10 = (f32[104,128]{1,0:T(8,128)S(1)}, f32[104,128]{1,0:T(8,128)S(1)}, u32[]{:S(2)}, u32[]{:S(2)}) collective-permute-start(f32[104,128]{1,0:T(8,128)S(1)} %get-tuple-element.51), channel_id=1, source_target_pairs={{0,8},{2,10},{4,12},{6,14},{8,0},{10,2},{12,4},{14,6},{1,9},{3,11}... | collective-permute-start | bytes 159752 | tf_op jit(solution)/shard_map/ppermute | solution.py:95
  28.5 0.8 %collective-permute-start.11 = (f32[104,128]{1,0:T(8,128)S(1)}, f32[104,128]{1,0:T(8,128)S(1)}, u32[]{:S(2)}, u32[]{:S(2)}) collective-permute-start(f32[104,128]{1,0:T(8,128)S(1)} %get-tuple-element.52), channel_id=1, source_target_pairs={{0,6},{2,4},{4,2},{6,0},{8,14},{10,12},{12,10},{14,8},{1,7},{3,5},... | collective-permute-start | bytes 159752 | tf_op jit(solution)/shard_map/ppermute | solution.py:95
  29.2 1.5 %collective-permute-start.12 = (f32[104,128]{1,0:T(8,128)S(1)}, f32[104,128]{1,0:T(8,128)S(1)}, u32[]{:S(2)}, u32[]{:S(2)}) collective-permute-start(f32[104,128]{1,0:T(8,128)S(1)} %get-tuple-element.53), channel_id=1, source_target_pairs={{0,4},{2,6},{4,0},{6,2},{8,12},{10,14},{12,8},{14,10},{1,5},{3,7},... | collective-permute-start | bytes 159752 | tf_op jit(solution)/shard_map/ppermute | solution.py:95
  30.7 1.1 %collective-permute-done.8.refs_1_ = f32[104,128]{1,0:T(8,128)S(1)} collective-permute-done((f32[104,128]{1,0:T(8,128)S(1)}, f32[104,128]{1,0:T(8,128)S(1)}, u32[]{:S(2)}, u32[]{:S(2)}) %collective-permute-start.8) | collective-permute-done | bytes 53280 | tf_op jit(solution)/shard_map/ppermute | solution.py:95
  31.8 0.6 %collective-permute-start.13 = (f32[104,128]{1,0:T(8,128)S(1)}, f32[104,128]{1,0:T(8,128)S(1)}, u32[]{:S(2)}, u32[]{:S(2)}) collective-permute-start(f32[104,128]{1,0:T(8,128)S(1)} %get-tuple-element.54), channel_id=1, source_target_pairs={{0,2},{2,0},{4,6},{6,4},{8,10},{10,8},{12,14},{14,12},{1,3},{3,1},... | collective-permute-start | bytes 159752 | tf_op jit(solution)/shard_map/ppermute | solution.py:95
  32.4 1.0 %collective-permute-done.10.refs_3_ = f32[104,128]{1,0:T(8,128)S(1)} collective-permute-done((f32[104,128]{1,0:T(8,128)S(1)}, f32[104,128]{1,0:T(8,128)S(1)}, u32[]{:S(2)}, u32[]{:S(2)}) %collective-permute-start.10) | collective-permute-done | bytes 53280 | tf_op jit(solution)/shard_map/ppermute | solution.py:95
  33.5 0.6 %collective-permute-done.12.refs_5_ = f32[104,128]{1,0:T(8,128)S(1)} collective-permute-done((f32[104,128]{1,0:T(8,128)S(1)}, f32[104,128]{1,0:T(8,128)S(1)}, u32[]{:S(2)}, u32[]{:S(2)}) %collective-permute-start.12) | collective-permute-done | bytes 53280 | tf_op jit(solution)/shard_map/ppermute | solution.py:95
  34.1 1.8 %collective-permute-done.13.refs_6_ = f32[104,128]{1,0:T(8,128)S(1)} collective-permute-done((f32[104,128]{1,0:T(8,128)S(1)}, f32[104,128]{1,0:T(8,128)S(1)}, u32[]{:S(2)}, u32[]{:S(2)}) %collective-permute-start.13) | collective-permute-done | bytes 53280 | tf_op jit(solution)/shard_map/ppermute | solution.py:95
  35.9 0.9 %shard_map.121 = (f32[64,512]{1,0:T(8,128)}, f32[64,512]{1,0:T(8,128)}, f32[64,512]{1,0:T(8,128)}, f32[64,512]{1,0:T(8,128)}, f32[64,512]{1,0:T(8,128)}, /*index=5*/f32[1,64]{1,0:T(1,128)}) custom-call(bf16[4,64,512]{2,1,0:T(8,128)(2,1)S(1)} %get-tuple-element.34.kept_ref, f32[104,128]{1,0:T(8,128)S(1)} %collective-permute-done.7.refs_0_, ...), custom_call_target="tpu_custom_call" | custom-call | tf_op jit(solution)/shard_map/pallas_call | solution.py:207
  (10 shorter events, 0.1 us)
Async XLA Ops:
  0.6 15.5 %copy-start = (f32[584,128]{1,0:T(8,128)S(1)}, f32[584,128]{1,0:T(8,128)}, u32[]{:S(2)}) copy-start(f32[584,128]{1,0:T(8,128)} %constant.2.clone.in_ref) | copy-start | bytes 897028
  1.9 10.8 %collective-permute-start = (f32[3,8,512]{2,1,0:T(8,128)S(1)}, f32[3,8,512]{2,1,0:T(8,128)S(1)}, u32[]{:S(2)}, u32[]{:S(2)}) collective-permute-start(f32[3,8,512]{2,1,0:T(8,128)S(1)} %get-tuple-element.40), channel_id=1, source_target_pairs={{0,14},{2,12},{4,10},{6,8},{8,6},{10,4},{12,2},{14,0},{1,15},{3,13... | collective-permute-start | bytes 147464 | tf_op jit(solution)/shard_map/ppermute | solution.py:95
  7.9 7.5 %collective-permute-start.1 = (f32[3,8,512]{2,1,0:T(8,128)S(1)}, f32[3,8,512]{2,1,0:T(8,128)S(1)}, u32[]{:S(2)}, u32[]{:S(2)}) collective-permute-start(f32[3,8,512]{2,1,0:T(8,128)S(1)} %get-tuple-element.41), channel_id=1, source_target_pairs={{0,10},{2,8},{4,14},{6,12},{8,2},{10,0},{12,6},{14,4},{1,11},{3,9}... | collective-permute-start | bytes 147464 | tf_op jit(solution)/shard_map/ppermute | solution.py:95
  7.9 8.5 %collective-permute-start.2 = (f32[3,8,512]{2,1,0:T(8,128)S(1)}, f32[3,8,512]{2,1,0:T(8,128)S(1)}, u32[]{:S(2)}, u32[]{:S(2)}) collective-permute-start(f32[3,8,512]{2,1,0:T(8,128)S(1)} %get-tuple-element.42), channel_id=1, source_target_pairs={{0,12},{2,14},{4,8},{6,10},{8,4},{10,6},{12,0},{14,2},{1,13},{3,15... | collective-permute-start | bytes 147464 | tf_op jit(solution)/shard_map/ppermute | solution.py:95
  9.8 7.0 %collective-permute-start.3 = (f32[3,8,512]{2,1,0:T(8,128)S(1)}, f32[3,8,512]{2,1,0:T(8,128)S(1)}, u32[]{:S(2)}, u32[]{:S(2)}) collective-permute-start(f32[3,8,512]{2,1,0:T(8,128)S(1)} %get-tuple-element.43), channel_id=1, source_target_pairs={{0,8},{2,10},{4,12},{6,14},{8,0},{10,2},{12,4},{14,6},{1,9},{3,11}... | collective-permute-start | bytes 147464 | tf_op jit(solution)/shard_map/ppermute | solution.py:95
  10.8 6.0 %collective-permute-start.4 = (f32[3,8,512]{2,1,0:T(8,128)S(1)}, f32[3,8,512]{2,1,0:T(8,128)S(1)}, u32[]{:S(2)}, u32[]{:S(2)}) collective-permute-start(f32[3,8,512]{2,1,0:T(8,128)S(1)} %get-tuple-element.44), channel_id=1, source_target_pairs={{0,6},{2,4},{4,2},{6,0},{8,14},{10,12},{12,10},{14,8},{1,7},{3,5},... | collective-permute-start | bytes 147464 | tf_op jit(solution)/shard_map/ppermute | solution.py:95
  12.6 4.6 %collective-permute-start.5 = (f32[3,8,512]{2,1,0:T(8,128)S(1)}, f32[3,8,512]{2,1,0:T(8,128)S(1)}, u32[]{:S(2)}, u32[]{:S(2)}) collective-permute-start(f32[3,8,512]{2,1,0:T(8,128)S(1)} %get-tuple-element.45), channel_id=1, source_target_pairs={{0,4},{2,6},{4,0},{6,2},{8,12},{10,14},{12,8},{14,10},{1,5},{3,7},... | collective-permute-start | bytes 147464 | tf_op jit(solution)/shard_map/ppermute | solution.py:95
  15.4 4.1 %collective-permute-start.6 = (f32[3,8,512]{2,1,0:T(8,128)S(1)}, f32[3,8,512]{2,1,0:T(8,128)S(1)}, u32[]{:S(2)}, u32[]{:S(2)}) collective-permute-start(f32[3,8,512]{2,1,0:T(8,128)S(1)} %get-tuple-element.46), channel_id=1, source_target_pairs={{0,2},{2,0},{4,6},{6,4},{8,10},{10,8},{12,14},{14,12},{1,3},{3,1},... | collective-permute-start | bytes 147464 | tf_op jit(solution)/shard_map/ppermute | solution.py:95
  21.6 7.6 %collective-permute-start.7 = (f32[104,128]{1,0:T(8,128)S(1)}, f32[104,128]{1,0:T(8,128)S(1)}, u32[]{:S(2)}, u32[]{:S(2)}) collective-permute-start(f32[104,128]{1,0:T(8,128)S(1)} %get-tuple-element.48), channel_id=1, source_target_pairs={{0,14},{2,12},{4,10},{6,8},{8,6},{10,4},{12,2},{14,0},{1,15},{3,13... | collective-permute-start | bytes 159752 | tf_op jit(solution)/shard_map/ppermute | solution.py:95
  24.8 6.9 %collective-permute-start.8 = (f32[104,128]{1,0:T(8,128)S(1)}, f32[104,128]{1,0:T(8,128)S(1)}, u32[]{:S(2)}, u32[]{:S(2)}) collective-permute-start(f32[104,128]{1,0:T(8,128)S(1)} %get-tuple-element.49), channel_id=1, source_target_pairs={{0,10},{2,8},{4,14},{6,12},{8,2},{10,0},{12,6},{14,4},{1,11},{3,9}... | collective-permute-start | bytes 159752 | tf_op jit(solution)/shard_map/ppermute | solution.py:95
  24.8 7.5 %collective-permute-start.9 = (f32[104,128]{1,0:T(8,128)S(1)}, f32[104,128]{1,0:T(8,128)S(1)}, u32[]{:S(2)}, u32[]{:S(2)}) collective-permute-start(f32[104,128]{1,0:T(8,128)S(1)} %get-tuple-element.50), channel_id=1, source_target_pairs={{0,12},{2,14},{4,8},{6,10},{8,4},{10,6},{12,0},{14,2},{1,13},{3,15... | collective-permute-start | bytes 159752 | tf_op jit(solution)/shard_map/ppermute | solution.py:95
  25.8 7.6 %collective-permute-start.10 = (f32[104,128]{1,0:T(8,128)S(1)}, f32[104,128]{1,0:T(8,128)S(1)}, u32[]{:S(2)}, u32[]{:S(2)}) collective-permute-start(f32[104,128]{1,0:T(8,128)S(1)} %get-tuple-element.51), channel_id=1, source_target_pairs={{0,8},{2,10},{4,12},{6,14},{8,0},{10,2},{12,4},{14,6},{1,9},{3,11}... | collective-permute-start | bytes 159752 | tf_op jit(solution)/shard_map/ppermute | solution.py:95
  28.5 5.0 %collective-permute-start.11 = (f32[104,128]{1,0:T(8,128)S(1)}, f32[104,128]{1,0:T(8,128)S(1)}, u32[]{:S(2)}, u32[]{:S(2)}) collective-permute-start(f32[104,128]{1,0:T(8,128)S(1)} %get-tuple-element.52), channel_id=1, source_target_pairs={{0,6},{2,4},{4,2},{6,0},{8,14},{10,12},{12,10},{14,8},{1,7},{3,5},... | collective-permute-start | bytes 159752 | tf_op jit(solution)/shard_map/ppermute | solution.py:95
  29.2 4.9 %collective-permute-start.12 = (f32[104,128]{1,0:T(8,128)S(1)}, f32[104,128]{1,0:T(8,128)S(1)}, u32[]{:S(2)}, u32[]{:S(2)}) collective-permute-start(f32[104,128]{1,0:T(8,128)S(1)} %get-tuple-element.53), channel_id=1, source_target_pairs={{0,4},{2,6},{4,0},{6,2},{8,12},{10,14},{12,8},{14,10},{1,5},{3,7},... | collective-permute-start | bytes 159752 | tf_op jit(solution)/shard_map/ppermute | solution.py:95
  31.8 4.1 %collective-permute-start.13 = (f32[104,128]{1,0:T(8,128)S(1)}, f32[104,128]{1,0:T(8,128)S(1)}, u32[]{:S(2)}, u32[]{:S(2)}) collective-permute-start(f32[104,128]{1,0:T(8,128)S(1)} %get-tuple-element.54), channel_id=1, source_target_pairs={{0,2},{2,0},{4,6},{6,4},{8,10},{10,8},{12,14},{14,12},{1,3},{3,1},... | collective-permute-start | bytes 159752 | tf_op jit(solution)/shard_map/ppermute | solution.py:95

commit v3 on v2

--- a/solution.py
+++ b/solution.py
@@ -9,6 +9,8 @@
 from jax.sharding import PartitionSpec as P
 
 HIGHEST = lax.Precision.HIGHEST
+OUTWARD = (4, 7, 3, 5, 6, 2, 1, 0)
+HOMEWARD = (7, 3, 6, 5, 4, 2, 1, 0)
 LANES = 128
 ROWS = 8
 VMEM = pl.BlockSpec(memory_space=pltpu.VMEM)
@@ -82,16 +84,14 @@
     twist_ref[1] = spread_rows(take(groups + 1), False)
 
 
-def partners(shards):
-    far = shards // 2
-    return [*range(shards - 1, far - 1, -1), *range(far - 1, -1, -1)] if shards != 8 else [7, 5, 6, 4, 3, 2, 1, 0]
-
-
-def swap(slabs):
-    shards = len(slabs)
+def turns(shards, order):
+    return order if len(order) == shards else tuple(range(shards - 1, -1, -1))
+
+
+def swap(slabs, order):
     moved = []
-    for turn, slab in zip(partners(shards), slabs):
-        pairs = [(i, i ^ turn) for i in range(shards)]
+    for turn, slab in zip(order, slabs):
+        pairs = [(i, i ^ turn) for i in range(len(slabs))]
         moved.append(lax.ppermute(slab, "ctx", pairs) if turn else slab)
     return moved
 
@@ -126,7 +126,7 @@
     copies[4].wait()
     copies[5].wait()
     place(2, kept_ref[2].astype(jnp.float32) * kept_ref[3].astype(jnp.float32))
-    for turn, out_ref in zip(partners(shards), out_refs):
+    for turn, out_ref in zip(turns(shards, OUTWARD), out_refs):
         out_ref[...] = all_ref[me ^ turn]
 
 
@@ -135,7 +135,7 @@
     shards = len(refs) // 2
     in_refs, out_refs = refs[:shards], refs[shards:]
     me = lax.axis_index("ctx")
-    for turn, ref in zip(partners(shards), in_refs):
+    for turn, ref in zip(turns(shards, OUTWARD), in_refs):
         in_ref[me ^ turn] = ref[...]
     tiles = in_ref.shape[3] // LANES
     span = tiles * ROWS
@@ -175,7 +175,7 @@
     result = long_dot(back_ref, split(jnp.concatenate(reverted, axis=1)))
     for s in range(3):
         all_ref[:, s * span : (s + 1) * span, :] = result[:, s * LANES : (s + 1) * LANES].reshape(shards, span, LANES)
-    for turn, out_ref in zip(partners(shards), out_refs):
+    for turn, out_ref in zip(turns(shards, HOMEWARD), out_refs):
         out_ref[...] = all_ref[me ^ turn]
 
 
@@ -185,7 +185,7 @@
     shards = channels // ROWS
     in_refs, (out_ref, gfirst_ref, gsecond_ref, gvalues_ref, gfilters_ref, gskip_ref, result_ref, total_ref) = refs[:shards], refs[shards:]
     me = lax.axis_index("ctx")
-    for turn, in_ref in zip(partners(shards), in_refs):
+    for turn, in_ref in zip(turns(shards, HOMEWARD), in_refs):
         own = pl.ds(pl.multiple_of((me ^ turn) * ROWS, ROWS), ROWS)
         for s, dst_ref in enumerate((result_ref.at[0], result_ref.at[1], gfilters_ref)):
             for j in range(tiles):
@@ -250,13 +250,13 @@
     slabs = call(
         spectral_kernel,
         [pltpu.VMEM(slab, wide)] * shards,
-        (*tables, *swap(slabs)),
+        (*tables, *swap(slabs, turns(shards, OUTWARD))),
         [pltpu.VMEM((shards, *slab), wide), pltpu.VMEM((shards, 3, ROWS, blocks), wide)],
     )
     *full, grad_skip = call(
         output_kernel,
         [jax.ShapeDtypeStruct((channels, blocks), wide)] * 5 + [jax.ShapeDtypeStruct((1, channels), wide)],
-        (kept, *swap(slabs)),
+        (kept, *swap(slabs, turns(shards, HOMEWARD))),
         [pltpu.VMEM((2, channels, blocks), wide), pltpu.VMEM((channels, LANES), wide)],
     )
     return (*full, grad_skip.reshape(channels))
@@ -357,7 +357,7 @@
 def per_device(first_gate, second_gate, values, filters, skip_gain, grad_output):
     channels, blocks = filters.shape
     shards = lax.axis_size("ctx")
-    fits = channels == ROWS * shards and blocks % LANES == 0 and channels <= LANES
+    fits = channels == ROWS * shards and shards & (shards - 1) == 0 and blocks % LANES == 0 and channels <= LANES
     plan = by_channels if fits else by_columns
     return plan(first_gate, second_gate, values, filters, skip_gain, grad_output)
 

time: 36.9 us -> 34.3 us (0.930)
  waiting for transfers between devices: 9.32 us -> 6.12 us
  starting transfers between devices: 22.3 us -> 22.8 us
    ppermute x14, waiting for transfers between devices: 9.32 us -> 6.12 us  [swap(): moved.append(lax.ppermute(slab, 'ctx', pairs) if turn else slab)]
    ppermute x14, starting transfers between devices: 22.3 us -> 22.8 us  [swap(): moved.append(lax.ppermute(slab, 'ctx', pairs) if turn else slab)]
  transfers between devices with their start and end apart: 14 -> 14, of which waited for: 9 -> 6; matrix products, arithmetic and copies ran while one was open for 0% -> 0% of each run, Pallas kernels for 1% -> 1%
where the time goes in v3:
time: 34.3 us; the launch traced here: 34.1 us
  starting transfers between devices  22.8 us (66%)
  waiting for transfers between devices  6.12 us (18%)
  Pallas kernels  4.5 us (13%)
  between operations  0.68 us (2%)
    ppermute x14, starting transfers between devices, swap(): moved.append(lax.ppermute(slab, 'ctx', pairs) if turn else slab)  22.8 us
    ppermute x14, waiting for transfers between devices, swap(): moved.append(lax.ppermute(slab, 'ctx', pairs) if turn else slab)  6.12 us
    pallas_call x3, Pallas kernels, call(): pl.pallas_call(kernel, out_shape=out_shape, in_specs=[VMEM] * len(args),...  3.3 us
    pallas_call x1, Pallas kernels, by_channels(): pl.pallas_call(gate_kernel, out_shape=[pltpu.VMEM((3, ROWS, blocks), wide...  1.2 us
  transfers between devices with their start and end apart: 14, of which 6 were waited for; matrix products, arithmetic and copies ran while one was open for 0% of the time, Pallas kernels for 1%

profile of v3, /device:TPU:0, one launch (start us, length us, event | category | flops | bytes accessed | tf_op | source)
XLA Modules:
  0.0 34.1 jit_solution(10264639820287538468)
XLA Ops:
  0.6 0.0 copy-start
  0.6 1.2 %shard_map.118 = (f32[3,8,512]{2,1,0:T(8,128)S(1)}, f32[3,8,512]{2,1,0:T(8,128)S(1)}, f32[3,8,512]{2,1,0:T(8,128)S(1)}, f32[3,8,512]{2,1,0:T(8,128)S(1)}, f32[3,...) custom-call(bf16[64,512]{1,0:T(8,128)(2,1)} %first_hbm.1, ...), custom_call_target="tpu_custom_call" | custom-call | tf_op jit(solution)/shard_map/pallas_call | solution.py:225
  1.9 4.1 %collective-permute-start = (f32[3,8,512]{2,1,0:T(8,128)S(1)}, f32[3,8,512]{2,1,0:T(8,128)S(1)}, u32[]{:S(2)}, u32[]{:S(2)}) collective-permute-start(f32[3,8,512]{2,1,0:T(8,128)S(1)} %get-tuple-element.40), channel_id=1, source_target_pairs={{0,8},{2,10},{4,12},{6,14},{8,0},{10,2},{12,4},{14,6},{1,9},{3,11}... | collective-permute-start | bytes 147464 | tf_op jit(solution)/shard_map/ppermute | solution.py:95
  6.0 2.3 %collective-permute-start.1 = (f32[3,8,512]{2,1,0:T(8,128)S(1)}, f32[3,8,512]{2,1,0:T(8,128)S(1)}, u32[]{:S(2)}, u32[]{:S(2)}) collective-permute-start(f32[3,8,512]{2,1,0:T(8,128)S(1)} %get-tuple-element.41), channel_id=1, source_target_pairs={{0,14},{2,12},{4,10},{6,8},{8,6},{10,4},{12,2},{14,0},{1,15},{3,13... | collective-permute-start | bytes 147464 | tf_op jit(solution)/shard_map/ppermute | solution.py:95
  8.2 0.2 collective-permute-start.2
  8.5 3.7 %collective-permute-start.3 = (f32[3,8,512]{2,1,0:T(8,128)S(1)}, f32[3,8,512]{2,1,0:T(8,128)S(1)}, u32[]{:S(2)}, u32[]{:S(2)}) collective-permute-start(f32[3,8,512]{2,1,0:T(8,128)S(1)} %get-tuple-element.43), channel_id=1, source_target_pairs={{0,10},{2,8},{4,14},{6,12},{8,2},{10,0},{12,6},{14,4},{1,11},{3,9}... | collective-permute-start | bytes 147464 | tf_op jit(solution)/shard_map/ppermute | solution.py:95
  12.2 1.4 %collective-permute-start.4 = (f32[3,8,512]{2,1,0:T(8,128)S(1)}, f32[3,8,512]{2,1,0:T(8,128)S(1)}, u32[]{:S(2)}, u32[]{:S(2)}) collective-permute-start(f32[3,8,512]{2,1,0:T(8,128)S(1)} %get-tuple-element.44), channel_id=1, source_target_pairs={{0,12},{2,14},{4,8},{6,10},{8,4},{10,6},{12,0},{14,2},{1,13},{3,15... | collective-permute-start | bytes 147464 | tf_op jit(solution)/shard_map/ppermute | solution.py:95
  13.5 0.8 %collective-permute-start.6 = (f32[3,8,512]{2,1,0:T(8,128)S(1)}, f32[3,8,512]{2,1,0:T(8,128)S(1)}, u32[]{:S(2)}, u32[]{:S(2)}) collective-permute-start(f32[3,8,512]{2,1,0:T(8,128)S(1)} %get-tuple-element.46), channel_id=1, source_target_pairs={{0,2},{2,0},{4,6},{6,4},{8,10},{10,8},{12,14},{14,12},{1,3},{3,1},... | collective-permute-start | bytes 147464 | tf_op jit(solution)/shard_map/ppermute | solution.py:95
  14.4 0.3 shard_map.119
  14.7 0.3 collective-permute-done.3.refs_3_
  15.0 3.2 %collective-permute-done.4.refs_4_ = f32[3,8,512]{2,1,0:T(8,128)S(1)} collective-permute-done((f32[3,8,512]{2,1,0:T(8,128)S(1)}, f32[3,8,512]{2,1,0:T(8,128)S(1)}, u32[]{:S(2)}, u32[]{:S(2)}) %collective-permute-start.4) | collective-permute-done | bytes 49184 | tf_op jit(solution)/shard_map/ppermute | solution.py:95
  18.2 2.1 %shard_map.120 = (f32[104,128]{1,0:T(8,128)S(1)}, f32[104,128]{1,0:T(8,128)S(1)}, f32[104,128]{1,0:T(8,128)S(1)}, f32[104,128]{1,0:T(8,128)S(1)}, f32[104,128]{1...) custom-call(bf16[2,512,256]{2,1,0:T(8,128)(2,1)S(1)} %get-tuple-element.35.outer_ref, ...), custom_call_target="tpu_custom_call" | custom-call | tf_op jit(solution)/shard_map/pallas_call | solution.py:207
  20.3 2.0 %collective-permute-start.7 = (f32[104,128]{1,0:T(8,128)S(1)}, f32[104,128]{1,0:T(8,128)S(1)}, u32[]{:S(2)}, u32[]{:S(2)}) collective-permute-start(f32[104,128]{1,0:T(8,128)S(1)} %get-tuple-element.48), channel_id=1, source_target_pairs={{0,14},{2,12},{4,10},{6,8},{8,6},{10,4},{12,2},{14,0},{1,15},{3,13... | collective-permute-start | bytes 159752 | tf_op jit(solution)/shard_map/ppermute | solution.py:95
  22.3 2.0 %collective-permute-start.8 = (f32[104,128]{1,0:T(8,128)S(1)}, f32[104,128]{1,0:T(8,128)S(1)}, u32[]{:S(2)}, u32[]{:S(2)}) collective-permute-start(f32[104,128]{1,0:T(8,128)S(1)} %get-tuple-element.49), channel_id=1, source_target_pairs={{0,6},{2,4},{4,2},{6,0},{8,14},{10,12},{12,10},{14,8},{1,7},{3,5},... | collective-permute-start | bytes 159752 | tf_op jit(solution)/shard_map/ppermute | solution.py:95
  24.3 1.3 %collective-permute-start.9 = (f32[104,128]{1,0:T(8,128)S(1)}, f32[104,128]{1,0:T(8,128)S(1)}, u32[]{:S(2)}, u32[]{:S(2)}) collective-permute-start(f32[104,128]{1,0:T(8,128)S(1)} %get-tuple-element.50), channel_id=1, source_target_pairs={{0,12},{2,14},{4,8},{6,10},{8,4},{10,6},{12,0},{14,2},{1,13},{3,15... | collective-permute-start | bytes 159752 | tf_op jit(solution)/shard_map/ppermute | solution.py:95
  25.7 1.1 %collective-permute-start.10 = (f32[104,128]{1,0:T(8,128)S(1)}, f32[104,128]{1,0:T(8,128)S(1)}, u32[]{:S(2)}, u32[]{:S(2)}) collective-permute-start(f32[104,128]{1,0:T(8,128)S(1)} %get-tuple-element.51), channel_id=1, source_target_pairs={{0,10},{2,8},{4,14},{6,12},{8,2},{10,0},{12,6},{14,4},{1,11},{3,9}... | collective-permute-start | bytes 159752 | tf_op jit(solution)/shard_map/ppermute | solution.py:95
  26.7 1.8 %collective-permute-start.11 = (f32[104,128]{1,0:T(8,128)S(1)}, f32[104,128]{1,0:T(8,128)S(1)}, u32[]{:S(2)}, u32[]{:S(2)}) collective-permute-start(f32[104,128]{1,0:T(8,128)S(1)} %get-tuple-element.52), channel_id=1, source_target_pairs={{0,8},{2,10},{4,12},{6,14},{8,0},{10,2},{12,4},{14,6},{1,9},{3,11}... | collective-permute-start | bytes 159752 | tf_op jit(solution)/shard_map/ppermute | solution.py:95
  28.6 0.5 %collective-permute-start.12 = (f32[104,128]{1,0:T(8,128)S(1)}, f32[104,128]{1,0:T(8,128)S(1)}, u32[]{:S(2)}, u32[]{:S(2)}) collective-permute-start(f32[104,128]{1,0:T(8,128)S(1)} %get-tuple-element.53), channel_id=1, source_target_pairs={{0,4},{2,6},{4,0},{6,2},{8,12},{10,14},{12,8},{14,10},{1,5},{3,7},... | collective-permute-start | bytes 159752 | tf_op jit(solution)/shard_map/ppermute | solution.py:95
  29.1 1.5 %collective-permute-start.13 = (f32[104,128]{1,0:T(8,128)S(1)}, f32[104,128]{1,0:T(8,128)S(1)}, u32[]{:S(2)}, u32[]{:S(2)}) collective-permute-start(f32[104,128]{1,0:T(8,128)S(1)} %get-tuple-element.54), channel_id=1, source_target_pairs={{0,2},{2,0},{4,6},{6,4},{8,10},{10,8},{12,14},{14,12},{1,3},{3,1},... | collective-permute-start | bytes 159752 | tf_op jit(solution)/shard_map/ppermute | solution.py:95
  30.6 1.5 %collective-permute-done.10.refs_3_ = f32[104,128]{1,0:T(8,128)S(1)} collective-permute-done((f32[104,128]{1,0:T(8,128)S(1)}, f32[104,128]{1,0:T(8,128)S(1)}, u32[]{:S(2)}, u32[]{:S(2)}) %collective-permute-start.10) | collective-permute-done | bytes 53280 | tf_op jit(solution)/shard_map/ppermute | solution.py:95
  32.1 0.1 collective-permute-done.11.refs_4_
  32.2 0.6 %collective-permute-done.12.refs_5_ = f32[104,128]{1,0:T(8,128)S(1)} collective-permute-done((f32[104,128]{1,0:T(8,128)S(1)}, f32[104,128]{1,0:T(8,128)S(1)}, u32[]{:S(2)}, u32[]{:S(2)}) %collective-permute-start.12) | collective-permute-done | bytes 53280 | tf_op jit(solution)/shard_map/ppermute | solution.py:95
  32.8 0.4 %collective-permute-done.13.refs_6_ = f32[104,128]{1,0:T(8,128)S(1)} collective-permute-done((f32[104,128]{1,0:T(8,128)S(1)}, f32[104,128]{1,0:T(8,128)S(1)}, u32[]{:S(2)}, u32[]{:S(2)}) %collective-permute-start.13) | collective-permute-done | bytes 53280 | tf_op jit(solution)/shard_map/ppermute | solution.py:95
  33.2 0.9 %shard_map.121 = (f32[64,512]{1,0:T(8,128)}, f32[64,512]{1,0:T(8,128)}, f32[64,512]{1,0:T(8,128)}, f32[64,512]{1,0:T(8,128)}, f32[64,512]{1,0:T(8,128)}, /*index=5*/f32[1,64]{1,0:T(1,128)}) custom-call(bf16[4,64,512]{2,1,0:T(8,128)(2,1)S(1)} %get-tuple-element.34.kept_ref, f32[104,128]{1,0:T(8,128)S(1)} %collective-permute-done.7.refs_0_, ...), custom_call_target="tpu_custom_call" | custom-call | tf_op jit(solution)/shard_map/pallas_call | solution.py:207
  (10 shorter events, 0.0 us)
Async XLA Ops:
  0.6 13.7 %copy-start = (f32[584,128]{1,0:T(8,128)S(1)}, f32[584,128]{1,0:T(8,128)}, u32[]{:S(2)}) copy-start(f32[584,128]{1,0:T(8,128)} %constant.2.clone.in_ref) | copy-start | bytes 897028
  1.9 11.7 %collective-permute-start = (f32[3,8,512]{2,1,0:T(8,128)S(1)}, f32[3,8,512]{2,1,0:T(8,128)S(1)}, u32[]{:S(2)}, u32[]{:S(2)}) collective-permute-start(f32[3,8,512]{2,1,0:T(8,128)S(1)} %get-tuple-element.40), channel_id=1, source_target_pairs={{0,8},{2,10},{4,12},{6,14},{8,0},{10,2},{12,4},{14,6},{1,9},{3,11}... | collective-permute-start | bytes 147464 | tf_op jit(solution)/shard_map/ppermute | solution.py:95
  6.0 7.6 %collective-permute-start.1 = (f32[3,8,512]{2,1,0:T(8,128)S(1)}, f32[3,8,512]{2,1,0:T(8,128)S(1)}, u32[]{:S(2)}, u32[]{:S(2)}) collective-permute-start(f32[3,8,512]{2,1,0:T(8,128)S(1)} %get-tuple-element.41), channel_id=1, source_target_pairs={{0,14},{2,12},{4,10},{6,8},{8,6},{10,4},{12,2},{14,0},{1,15},{3,13... | collective-permute-start | bytes 147464 | tf_op jit(solution)/shard_map/ppermute | solution.py:95
  8.2 6.4 %collective-permute-start.2 = (f32[3,8,512]{2,1,0:T(8,128)S(1)}, f32[3,8,512]{2,1,0:T(8,128)S(1)}, u32[]{:S(2)}, u32[]{:S(2)}) collective-permute-start(f32[3,8,512]{2,1,0:T(8,128)S(1)} %get-tuple-element.42), channel_id=1, source_target_pairs={{0,6},{2,4},{4,2},{6,0},{8,14},{10,12},{12,10},{14,8},{1,7},{3,5},... | collective-permute-start | bytes 147464 | tf_op jit(solution)/shard_map/ppermute | solution.py:95
  8.5 6.5 %collective-permute-start.3 = (f32[3,8,512]{2,1,0:T(8,128)S(1)}, f32[3,8,512]{2,1,0:T(8,128)S(1)}, u32[]{:S(2)}, u32[]{:S(2)}) collective-permute-start(f32[3,8,512]{2,1,0:T(8,128)S(1)} %get-tuple-element.43), channel_id=1, source_target_pairs={{0,10},{2,8},{4,14},{6,12},{8,2},{10,0},{12,6},{14,4},{1,11},{3,9}... | collective-permute-start | bytes 147464 | tf_op jit(solution)/shard_map/ppermute | solution.py:95
  12.2 6.0 %collective-permute-start.4 = (f32[3,8,512]{2,1,0:T(8,128)S(1)}, f32[3,8,512]{2,1,0:T(8,128)S(1)}, u32[]{:S(2)}, u32[]{:S(2)}) collective-permute-start(f32[3,8,512]{2,1,0:T(8,128)S(1)} %get-tuple-element.44), channel_id=1, source_target_pairs={{0,12},{2,14},{4,8},{6,10},{8,4},{10,6},{12,0},{14,2},{1,13},{3,15... | collective-permute-start | bytes 147464 | tf_op jit(solution)/shard_map/ppermute | solution.py:95
  13.5 4.6 %collective-permute-start.5 = (f32[3,8,512]{2,1,0:T(8,128)S(1)}, f32[3,8,512]{2,1,0:T(8,128)S(1)}, u32[]{:S(2)}, u32[]{:S(2)}) collective-permute-start(f32[3,8,512]{2,1,0:T(8,128)S(1)} %get-tuple-element.45), channel_id=1, source_target_pairs={{0,4},{2,6},{4,0},{6,2},{8,12},{10,14},{12,8},{14,10},{1,5},{3,7},... | collective-permute-start | bytes 147464 | tf_op jit(solution)/shard_map/ppermute | solution.py:95
  13.5 4.6 %collective-permute-start.6 = (f32[3,8,512]{2,1,0:T(8,128)S(1)}, f32[3,8,512]{2,1,0:T(8,128)S(1)}, u32[]{:S(2)}, u32[]{:S(2)}) collective-permute-start(f32[3,8,512]{2,1,0:T(8,128)S(1)} %get-tuple-element.46), channel_id=1, source_target_pairs={{0,2},{2,0},{4,6},{6,4},{8,10},{10,8},{12,14},{14,12},{1,3},{3,1},... | collective-permute-start | bytes 147464 | tf_op jit(solution)/shard_map/ppermute | solution.py:95
  20.3 8.3 %collective-permute-start.7 = (f32[104,128]{1,0:T(8,128)S(1)}, f32[104,128]{1,0:T(8,128)S(1)}, u32[]{:S(2)}, u32[]{:S(2)}) collective-permute-start(f32[104,128]{1,0:T(8,128)S(1)} %get-tuple-element.48), channel_id=1, source_target_pairs={{0,14},{2,12},{4,10},{6,8},{8,6},{10,4},{12,2},{14,0},{1,15},{3,13... | collective-permute-start | bytes 159752 | tf_op jit(solution)/shard_map/ppermute | solution.py:95
  22.3 6.8 %collective-permute-start.8 = (f32[104,128]{1,0:T(8,128)S(1)}, f32[104,128]{1,0:T(8,128)S(1)}, u32[]{:S(2)}, u32[]{:S(2)}) collective-permute-start(f32[104,128]{1,0:T(8,128)S(1)} %get-tuple-element.49), channel_id=1, source_target_pairs={{0,6},{2,4},{4,2},{6,0},{8,14},{10,12},{12,10},{14,8},{1,7},{3,5},... | collective-permute-start | bytes 159752 | tf_op jit(solution)/shard_map/ppermute | solution.py:95
  24.3 6.3 %collective-permute-start.9 = (f32[104,128]{1,0:T(8,128)S(1)}, f32[104,128]{1,0:T(8,128)S(1)}, u32[]{:S(2)}, u32[]{:S(2)}) collective-permute-start(f32[104,128]{1,0:T(8,128)S(1)} %get-tuple-element.50), channel_id=1, source_target_pairs={{0,12},{2,14},{4,8},{6,10},{8,4},{10,6},{12,0},{14,2},{1,13},{3,15... | collective-permute-start | bytes 159752 | tf_op jit(solution)/shard_map/ppermute | solution.py:95
  25.7 6.5 %collective-permute-start.10 = (f32[104,128]{1,0:T(8,128)S(1)}, f32[104,128]{1,0:T(8,128)S(1)}, u32[]{:S(2)}, u32[]{:S(2)}) collective-permute-start(f32[104,128]{1,0:T(8,128)S(1)} %get-tuple-element.51), channel_id=1, source_target_pairs={{0,10},{2,8},{4,14},{6,12},{8,2},{10,0},{12,6},{14,4},{1,11},{3,9}... | collective-permute-start | bytes 159752 | tf_op jit(solution)/shard_map/ppermute | solution.py:95
  26.7 5.5 %collective-permute-start.11 = (f32[104,128]{1,0:T(8,128)S(1)}, f32[104,128]{1,0:T(8,128)S(1)}, u32[]{:S(2)}, u32[]{:S(2)}) collective-permute-start(f32[104,128]{1,0:T(8,128)S(1)} %get-tuple-element.52), channel_id=1, source_target_pairs={{0,8},{2,10},{4,12},{6,14},{8,0},{10,2},{12,4},{14,6},{1,9},{3,11}... | collective-permute-start | bytes 159752 | tf_op jit(solution)/shard_map/ppermute | solution.py:95
  28.6 4.2 %collective-permute-start.12 = (f32[104,128]{1,0:T(8,128)S(1)}, f32[104,128]{1,0:T(8,128)S(1)}, u32[]{:S(2)}, u32[]{:S(2)}) collective-permute-start(f32[104,128]{1,0:T(8,128)S(1)} %get-tuple-element.53), channel_id=1, source_target_pairs={{0,4},{2,6},{4,0},{6,2},{8,12},{10,14},{12,8},{14,10},{1,5},{3,7},... | collective-permute-start | bytes 159752 | tf_op jit(solution)/shard_map/ppermute | solution.py:95
  29.1 4.1 %collective-permute-start.13 = (f32[104,128]{1,0:T(8,128)S(1)}, f32[104,128]{1,0:T(8,128)S(1)}, u32[]{:S(2)}, u32[]{:S(2)}) collective-permute-start(f32[104,128]{1,0:T(8,128)S(1)} %get-tuple-element.54), channel_id=1, source_target_pairs={{0,2},{2,0},{4,6},{6,4},{8,10},{10,8},{12,14},{14,12},{1,3},{3,1},... | collective-permute-start | bytes 159752 | tf_op jit(solution)/shard_map/ppermute | solution.py:95

commit v4 on v3

--- a/solution.py
+++ b/solution.py
@@ -9,8 +9,8 @@
 from jax.sharding import PartitionSpec as P
 
 HIGHEST = lax.Precision.HIGHEST
-OUTWARD = (4, 7, 3, 5, 6, 2, 1, 0)
-HOMEWARD = (7, 3, 6, 5, 4, 2, 1, 0)
+OUTWARD = ((6, 7), (2, 3), (5,), (1,), (4,))
+HOMEWARD = ((6, 7), (2, 3), (1,), (5,), (4,))
 LANES = 128
 ROWS = 8
 VMEM = pl.BlockSpec(memory_space=pltpu.VMEM)
@@ -84,16 +84,43 @@
     twist_ref[1] = spread_rows(take(groups + 1), False)
 
 
-def turns(shards, order):
-    return order if len(order) == shards else tuple(range(shards - 1, -1, -1))
-
-
-def swap(slabs, order):
-    moved = []
-    for turn, slab in zip(order, slabs):
-        pairs = [(i, i ^ turn) for i in range(len(slabs))]
-        moved.append(lax.ppermute(slab, "ctx", pairs) if turn else slab)
-    return moved
+def sent(shards, groups):
+    if sum(map(len, groups)) != shards - 1:
+        groups = tuple((turn,) for turn in range(shards - 1, 0, -1))
+    return (*groups, (0,))
+
+
+def received(shards, groups):
+    groups = sent(shards, groups)
+    first = [(group[0], *(None for _ in group[1:])) for group in groups]
+    return (*first[:-1], *(group[1:] for group in groups if len(group) > 1), (0,))
+
+
+def swap(arrays, groups):
+    *arrays, own = arrays
+    shards = lax.axis_size("ctx")
+
+    def move(array, turn):
+        return lax.ppermute(array, "ctx", [(i, i ^ turn) for i in range(shards)])
+
+    moved = [move(x, members[0]) for members, x in zip(sent(shards, groups), arrays)]
+    relayed = [move(x[1:], 1) for x in moved if x.shape[0] > 1]
+    return (*moved, *relayed, own)
+
+
+def gather(place_ref, in_refs, groups):
+    me = lax.axis_index("ctx")
+    for members, ref in zip(received(place_ref.shape[0], groups), in_refs):
+        for i, turn in enumerate(members):
+            if turn is not None:
+                place_ref[me ^ turn] = ref[i]
+
+
+def scatter(out_refs, place_ref, groups):
+    me = lax.axis_index("ctx")
+    for members, ref in zip(sent(place_ref.shape[0], groups), out_refs):
+        for i, turn in enumerate(members):
+            ref[i] = place_ref[me ^ turn]
 
 
 def gate_kernel(first_hbm, values_hbm, grad_hbm, second_hbm, filters_hbm, gain_hbm, *refs):
@@ -104,7 +131,7 @@
     copies = [pltpu.make_async_copy(source, place, sems.at[i]) for i, (source, place) in enumerate(zip(sources, places))]
     for copy in copies:
         copy.start()
-    shards = len(out_refs)
+    shards = all_ref.shape[0]
     channels, blocks = filters_ref.shape
     me = lax.axis_index("ctx")
 
@@ -126,17 +153,15 @@
     copies[4].wait()
     copies[5].wait()
     place(2, kept_ref[2].astype(jnp.float32) * kept_ref[3].astype(jnp.float32))
-    for turn, out_ref in zip(turns(shards, OUTWARD), out_refs):
-        out_ref[...] = all_ref[me ^ turn]
+    scatter(out_refs, all_ref, OUTWARD)
 
 
 def spectral_kernel(outer_ref, back_ref, forward_ref, inverse_ref, twist_ref, *refs):
     *refs, all_ref, in_ref = refs
-    shards = len(refs) // 2
-    in_refs, out_refs = refs[:shards], refs[shards:]
-    me = lax.axis_index("ctx")
-    for turn, ref in zip(turns(shards, OUTWARD), in_refs):
-        in_ref[me ^ turn] = ref[...]
+    shards = in_ref.shape[0]
+    count = len(received(shards, OUTWARD))
+    in_refs, out_refs = refs[:count], refs[count:]
+    gather(in_ref, in_refs, OUTWARD)
     tiles = in_ref.shape[3] // LANES
     span = tiles * ROWS
     rows = shards * span
@@ -175,22 +200,24 @@
     result = long_dot(back_ref, split(jnp.concatenate(reverted, axis=1)))
     for s in range(3):
         all_ref[:, s * span : (s + 1) * span, :] = result[:, s * LANES : (s + 1) * LANES].reshape(shards, span, LANES)
-    for turn, out_ref in zip(turns(shards, HOMEWARD), out_refs):
-        out_ref[...] = all_ref[me ^ turn]
+    scatter(out_refs, all_ref, HOMEWARD)
 
 
 def output_kernel(kept_ref, *refs):
     _, channels, blocks = kept_ref.shape
     tiles = blocks // LANES
-    shards = channels // ROWS
-    in_refs, (out_ref, gfirst_ref, gsecond_ref, gvalues_ref, gfilters_ref, gskip_ref, result_ref, total_ref) = refs[:shards], refs[shards:]
+    count = len(received(channels // ROWS, HOMEWARD))
+    in_refs, (out_ref, gfirst_ref, gsecond_ref, gvalues_ref, gfilters_ref, gskip_ref, result_ref, total_ref) = refs[:count], refs[count:]
     me = lax.axis_index("ctx")
-    for turn, in_ref in zip(turns(shards, HOMEWARD), in_refs):
-        own = pl.ds(pl.multiple_of((me ^ turn) * ROWS, ROWS), ROWS)
-        for s, dst_ref in enumerate((result_ref.at[0], result_ref.at[1], gfilters_ref)):
-            for j in range(tiles):
-                dst_ref[own, j * LANES : (j + 1) * LANES] = in_ref[(s * tiles + j) * ROWS : (s * tiles + j + 1) * ROWS, :]
-        total_ref[own, :] = in_ref[3 * tiles * ROWS :, :]
+    for members, ref in zip(received(channels // ROWS, HOMEWARD), in_refs):
+        for i, turn in enumerate(members):
+            if turn is None:
+                continue
+            own = pl.ds(pl.multiple_of((me ^ turn) * ROWS, ROWS), ROWS)
+            for s, dst_ref in enumerate((result_ref.at[0], result_ref.at[1], gfilters_ref)):
+                for j in range(tiles):
+                    dst_ref[own, j * LANES : (j + 1) * LANES] = ref[i, (s * tiles + j) * ROWS : (s * tiles + j + 1) * ROWS, :]
+            total_ref[own, :] = ref[i, 3 * tiles * ROWS :, :]
     first, values, grad, second = [kept_ref[i].astype(jnp.float32) for i in range(4)]
     before = result_ref[0]
     out_ref[...] = second * before
@@ -222,13 +249,15 @@
     rows = length // LANES * ROWS
     wide, half = jnp.float32, jnp.bfloat16
     sources = (first_gate, values, grad_output, second_gate, filters, skip_gain.reshape(1, channels))
+    slab = (3, ROWS, blocks)
+    outs = [pltpu.VMEM((len(members), *slab), wide) for members in sent(shards, OUTWARD)]
     *slabs, kept = pl.pallas_call(
         gate_kernel,
-        out_shape=[pltpu.VMEM((3, ROWS, blocks), wide)] * shards + [pltpu.VMEM((4, channels, blocks), half)],
+        out_shape=[*outs, pltpu.VMEM((4, channels, blocks), half)],
         in_specs=[HBM] * len(sources),
-        out_specs=[VMEM] * (shards + 1),
+        out_specs=[VMEM] * (len(outs) + 1),
         scratch_shapes=[
-            pltpu.VMEM((shards, 3, ROWS, blocks), wide),
+            pltpu.VMEM((shards, *slab), wide),
             pltpu.VMEM((channels, blocks), wide),
             pltpu.VMEM((1, channels), wide),
             pltpu.SemaphoreType.DMA((len(sources),)),
@@ -246,17 +275,17 @@
         ],
         [jnp.asarray(make_tables(length))],
     )
-    slab = ((3 * tiles + 1) * ROWS, LANES)
+    result = ((3 * tiles + 1) * ROWS, LANES)
     slabs = call(
         spectral_kernel,
-        [pltpu.VMEM(slab, wide)] * shards,
-        (*tables, *swap(slabs, turns(shards, OUTWARD))),
-        [pltpu.VMEM((shards, *slab), wide), pltpu.VMEM((shards, 3, ROWS, blocks), wide)],
+        [pltpu.VMEM((len(members), *result), wide) for members in sent(shards, HOMEWARD)],
+        (*tables, *swap(slabs, OUTWARD)),
+        [pltpu.VMEM((shards, *result), wide), pltpu.VMEM((shards, *slab), wide)],
     )
     *full, grad_skip = call(
         output_kernel,
         [jax.ShapeDtypeStruct((channels, blocks), wide)] * 5 + [jax.ShapeDtypeStruct((1, channels), wide)],
-        (kept, *swap(slabs, turns(shards, HOMEWARD))),
+        (kept, *swap(slabs, HOMEWARD)),
         [pltpu.VMEM((2, channels, blocks), wide), pltpu.VMEM((channels, LANES), wide)],
     )
     return (*full, grad_skip.reshape(channels))

time: 34.3 us -> 33.5 us (0.977)
  starting transfers between devices: 22.8 us -> 21.9 us
    ppermute x14, starting transfers between devices: 22.8 us -> 21.9 us  [move(): return lax.ppermute(array, 'ctx', [(i, i ^ turn) for i in range(shards)])]
  transfers between devices with their start and end apart: 14 -> 14, of which waited for: 6 -> 9; matrix products, arithmetic and copies ran while one was open for 0% -> 0% of each run, Pallas kernels for 1% -> 1%
where the time goes in v4:
time: 33.5 us; the launch traced here: 33.4 us
  starting transfers between devices  21.9 us (65%)
  waiting for transfers between devices  6.28 us (19%)
  Pallas kernels  4.5 us (13%)
  between operations  0.68 us (2%)
    ppermute x14, starting transfers between devices, move(): return lax.ppermute(array, 'ctx', [(i, i ^ turn) for i in range(shards)])  21.9 us
    ppermute x14, waiting for transfers between devices, move(): return lax.ppermute(array, 'ctx', [(i, i ^ turn) for i in range(shards)])  6.28 us
    pallas_call x3, Pallas kernels, call(): pl.pallas_call(kernel, out_shape=out_shape, in_specs=[VMEM] * len(args),...  3.3 us
    pallas_call x1, Pallas kernels, by_channels(): pl.pallas_call(gate_kernel, out_shape=[*outs, pltpu.VMEM((4, channels, bl...  1.2 us
  transfers between devices with their start and end apart: 14, of which 9 were waited for; matrix products, arithmetic and copies ran while one was open for 0% of the time, Pallas kernels for 1%

profile of v4, /device:TPU:0, one launch (start us, length us, event | category | flops | bytes accessed | tf_op | source)
XLA Modules:
  0.0 33.4 jit_solution(11750995692343684257)
XLA Ops:
  0.6 1.2 %shard_map.118 = (f32[2,3,8,512]{3,2,1,0:T(8,128)S(1)}, f32[2,3,8,512]{3,2,1,0:T(8,128)S(1)}, f32[1,3,8,512]{3,2,1,0:T(8,128)S(1)}, f32[1,3,8,512]{3,2,1,0:T(8,1...) custom-call(bf16[64,512]{1,0:T(8,128)(2,1)} %first_hbm.1, ...), custom_call_target="tpu_custom_call" | custom-call | tf_op jit(solution)/shard_map/pallas_call | solution.py:254
  1.9 5.1 %collective-permute-start = (f32[2,3,8,512]{3,2,1,0:T(8,128)S(1)}, f32[2,3,8,512]{3,2,1,0:T(8,128)S(1)}, u32[]{:S(2)}, u32[]{:S(2)}) collective-permute-start(f32[2,3,8,512]{3,2,1,0:T(8,128)S(1)} %get-tuple-element.36), channel_id=1, source_target_pairs={{0,12},{2,14},{4,8},{6,10},{8,4},{10,6},{12,0},{14,2},{1,13},{3,15... | collective-permute-start | bytes 294920 | tf_op jit(solution)/shard_map/ppermute | solution.py:104
  7.0 1.7 %collective-permute-start.2 = (f32[1,3,8,512]{3,2,1,0:T(8,128)S(1)}, f32[1,3,8,512]{3,2,1,0:T(8,128)S(1)}, u32[]{:S(2)}, u32[]{:S(2)}) collective-permute-start(f32[1,3,8,512]{3,2,1,0:T(8,128)S(1)} %get-tuple-element.38), channel_id=1, source_target_pairs={{0,10},{2,8},{4,14},{6,12},{8,2},{10,0},{12,6},{14,4},{1,11},{3,9}... | collective-permute-start | bytes 147464 | tf_op jit(solution)/shard_map/ppermute | solution.py:104
  8.7 0.4 %collective-permute-start.3 = (f32[1,3,8,512]{3,2,1,0:T(8,128)S(1)}, f32[1,3,8,512]{3,2,1,0:T(8,128)S(1)}, u32[]{:S(2)}, u32[]{:S(2)}) collective-permute-start(f32[1,3,8,512]{3,2,1,0:T(8,128)S(1)} %get-tuple-element.39), channel_id=1, source_target_pairs={{0,2},{2,0},{4,6},{6,4},{8,10},{10,8},{12,14},{14,12},{1,3},{3,1},... | collective-permute-start | bytes 147464 | tf_op jit(solution)/shard_map/ppermute | solution.py:104
  9.1 2.3 %collective-permute-start.4 = (f32[1,3,8,512]{3,2,1,0:T(8,128)S(1)}, f32[1,3,8,512]{3,2,1,0:T(8,128)S(1)}, u32[]{:S(2)}, u32[]{:S(2)}) collective-permute-start(f32[1,3,8,512]{3,2,1,0:T(8,128)S(1)} %get-tuple-element.40), channel_id=1, source_target_pairs={{0,8},{2,10},{4,12},{6,14},{8,0},{10,2},{12,4},{14,6},{1,9},{3,11}... | collective-permute-start | bytes 147464 | tf_op jit(solution)/shard_map/ppermute | solution.py:104
  11.4 1.6 %collective-permute-start.5 = (f32[1,3,8,512]{3,2,1,0:T(8,128)S(1)}, f32[1,3,8,512]{3,2,1,0:T(8,128)S(1)}, u32[]{:S(2)}, u32[]{:S(2)}) collective-permute-start(f32[1,3,8,512]{3,2,1,0:T(8,128)S(1)} %slice.16), channel_id=1, source_target_pairs={{0,2},{2,0},{4,6},{6,4},{8,10},{10,8},{12,14},{14,12},{1,3},{3,1},... | collective-permute-start | bytes 147464 | tf_op jit(solution)/shard_map/ppermute | solution.py:104
  12.9 0.2 collective-permute-done.1.refs_1_
  13.1 1.4 %collective-permute-start.6 = (f32[1,3,8,512]{3,2,1,0:T(8,128)S(1)}, f32[1,3,8,512]{3,2,1,0:T(8,128)S(1)}, u32[]{:S(2)}, u32[]{:S(2)}) collective-permute-start(f32[1,3,8,512]{3,2,1,0:T(8,128)S(1)} %slice.17), channel_id=1, source_target_pairs={{0,2},{2,0},{4,6},{6,4},{8,10},{10,8},{12,14},{14,12},{1,3},{3,1},... | collective-permute-start | bytes 147464 | tf_op jit(solution)/shard_map/ppermute | solution.py:104
  14.5 0.3 shard_map.119
  14.8 0.4 %collective-permute-done.2.refs_2_ = f32[1,3,8,512]{3,2,1,0:T(8,128)S(1)} collective-permute-done((f32[1,3,8,512]{3,2,1,0:T(8,128)S(1)}, f32[1,3,8,512]{3,2,1,0:T(8,128)S(1)}, u32[]{:S(2)}, u32[]{:S(2)}) %collective-permute-start.2) | collective-permute-done | bytes 49184 | tf_op jit(solution)/shard_map/ppermute | solution.py:104
  15.3 0.8 %collective-permute-done.5.refs_5_ = f32[1,3,8,512]{3,2,1,0:T(8,128)S(1)} collective-permute-done((f32[1,3,8,512]{3,2,1,0:T(8,128)S(1)}, f32[1,3,8,512]{3,2,1,0:T(8,128)S(1)}, u32[]{:S(2)}, u32[]{:S(2)}) %collective-permute-start.5) | collective-permute-done | bytes 49184 | tf_op jit(solution)/shard_map/ppermute | solution.py:104
  16.1 1.1 %collective-permute-done.6.refs_6_ = f32[1,3,8,512]{3,2,1,0:T(8,128)S(1)} collective-permute-done((f32[1,3,8,512]{3,2,1,0:T(8,128)S(1)}, f32[1,3,8,512]{3,2,1,0:T(8,128)S(1)}, u32[]{:S(2)}, u32[]{:S(2)}) %collective-permute-start.6) | collective-permute-done | bytes 49184 | tf_op jit(solution)/shard_map/ppermute | solution.py:104
  17.2 2.1 %shard_map.120 = (f32[2,104,128]{2,1,0:T(8,128)S(1)}, f32[2,104,128]{2,1,0:T(8,128)S(1)}, f32[1,104,128]{2,1,0:T(8,128)S(1)}, f32[1,104,128]{2,1,0:T(8,128)S(1)}...) custom-call(bf16[2,512,256]{2,1,0:T(8,128)(2,1)S(1)} %get-tuple-element.31.outer_ref, ...), custom_call_target="tpu_custom_call" | custom-call | tf_op jit(solution)/shard_map/pallas_call | solution.py:234
  19.3 3.0 %collective-permute-start.7 = (f32[2,104,128]{2,1,0:T(8,128)S(1)}, f32[2,104,128]{2,1,0:T(8,128)S(1)}, u32[]{:S(2)}, u32[]{:S(2)}) collective-permute-start(f32[2,104,128]{2,1,0:T(8,128)S(1)} %get-tuple-element.42), channel_id=1, source_target_pairs={{0,12},{2,14},{4,8},{6,10},{8,4},{10,6},{12,0},{14,2},{1,13},{3,15... | collective-permute-start | bytes 319496 | tf_op jit(solution)/shard_map/ppermute | solution.py:104
  22.3 0.5 %collective-permute-start.9 = (f32[1,104,128]{2,1,0:T(8,128)S(1)}, f32[1,104,128]{2,1,0:T(8,128)S(1)}, u32[]{:S(2)}, u32[]{:S(2)}) collective-permute-start(f32[1,104,128]{2,1,0:T(8,128)S(1)} %get-tuple-element.44), channel_id=1, source_target_pairs={{0,2},{2,0},{4,6},{6,4},{8,10},{10,8},{12,14},{14,12},{1,3},{3,1},... | collective-permute-start | bytes 159752 | tf_op jit(solution)/shard_map/ppermute | solution.py:104
  22.8 2.4 %collective-permute-start.10 = (f32[1,104,128]{2,1,0:T(8,128)S(1)}, f32[1,104,128]{2,1,0:T(8,128)S(1)}, u32[]{:S(2)}, u32[]{:S(2)}) collective-permute-start(f32[1,104,128]{2,1,0:T(8,128)S(1)} %get-tuple-element.45), channel_id=1, source_target_pairs={{0,10},{2,8},{4,14},{6,12},{8,2},{10,0},{12,6},{14,4},{1,11},{3,9}... | collective-permute-start | bytes 159752 | tf_op jit(solution)/shard_map/ppermute | solution.py:104
  25.3 1.5 %collective-permute-start.11 = (f32[1,104,128]{2,1,0:T(8,128)S(1)}, f32[1,104,128]{2,1,0:T(8,128)S(1)}, u32[]{:S(2)}, u32[]{:S(2)}) collective-permute-start(f32[1,104,128]{2,1,0:T(8,128)S(1)} %get-tuple-element.46), channel_id=1, source_target_pairs={{0,8},{2,10},{4,12},{6,14},{8,0},{10,2},{12,4},{14,6},{1,9},{3,11}... | collective-permute-start | bytes 159752 | tf_op jit(solution)/shard_map/ppermute | solution.py:104
  26.7 0.5 %collective-permute-done.7.refs_0_ = f32[2,104,128]{2,1,0:T(8,128)S(1)} collective-permute-done((f32[2,104,128]{2,1,0:T(8,128)S(1)}, f32[2,104,128]{2,1,0:T(8,128)S(1)}, u32[]{:S(2)}, u32[]{:S(2)}) %collective-permute-start.7) | collective-permute-done | bytes 106528 | tf_op jit(solution)/shard_map/ppermute | solution.py:104
  27.2 1.0 %collective-permute-start.12 = (f32[1,104,128]{2,1,0:T(8,128)S(1)}, f32[1,104,128]{2,1,0:T(8,128)S(1)}, u32[]{:S(2)}, u32[]{:S(2)}) collective-permute-start(f32[1,104,128]{2,1,0:T(8,128)S(1)} %slice.18), channel_id=1, source_target_pairs={{0,2},{2,0},{4,6},{6,4},{8,10},{10,8},{12,14},{14,12},{1,3},{3,1},... | collective-permute-start | bytes 159752 | tf_op jit(solution)/shard_map/ppermute | solution.py:104
  28.3 1.0 %collective-permute-start.13 = (f32[1,104,128]{2,1,0:T(8,128)S(1)}, f32[1,104,128]{2,1,0:T(8,128)S(1)}, u32[]{:S(2)}, u32[]{:S(2)}) collective-permute-start(f32[1,104,128]{2,1,0:T(8,128)S(1)} %slice.19), channel_id=1, source_target_pairs={{0,2},{2,0},{4,6},{6,4},{8,10},{10,8},{12,14},{14,12},{1,3},{3,1},... | collective-permute-start | bytes 159752 | tf_op jit(solution)/shard_map/ppermute | solution.py:104
  29.3 0.2 collective-permute-done.10.refs_3_
  29.5 1.9 %collective-permute-done.11.refs_4_ = f32[1,104,128]{2,1,0:T(8,128)S(1)} collective-permute-done((f32[1,104,128]{2,1,0:T(8,128)S(1)}, f32[1,104,128]{2,1,0:T(8,128)S(1)}, u32[]{:S(2)}, u32[]{:S(2)}) %collective-permute-start.11) | collective-permute-done | bytes 53280 | tf_op jit(solution)/shard_map/ppermute | solution.py:104
  31.4 1.1 %collective-permute-done.13.refs_6_ = f32[1,104,128]{2,1,0:T(8,128)S(1)} collective-permute-done((f32[1,104,128]{2,1,0:T(8,128)S(1)}, f32[1,104,128]{2,1,0:T(8,128)S(1)}, u32[]{:S(2)}, u32[]{:S(2)}) %collective-permute-start.13) | collective-permute-done | bytes 53280 | tf_op jit(solution)/shard_map/ppermute | solution.py:104
  32.5 0.9 %shard_map.121 = (f32[64,512]{1,0:T(8,128)}, f32[64,512]{1,0:T(8,128)}, f32[64,512]{1,0:T(8,128)}, f32[64,512]{1,0:T(8,128)}, f32[64,512]{1,0:T(8,128)}, /*index=5*/f32[1,64]{1,0:T(1,128)}) custom-call(bf16[4,64,512]{2,1,0:T(8,128)(2,1)S(1)} %get-tuple-element.30.kept_ref, f32[2,104,128]{2,1,0:T(8,128)S(1)} %collective-permute-done.7.refs_0_, ...), custom_call_target="tpu_custom_call" | custom-call | tf_op jit(solution)/shard_map/pallas_call | solution.py:234
  (14 shorter events, 0.1 us)
Async XLA Ops:
  0.6 13.8 %copy-start = (f32[584,128]{1,0:T(8,128)S(1)}, f32[584,128]{1,0:T(8,128)}, u32[]{:S(2)}) copy-start(f32[584,128]{1,0:T(8,128)} %constant.2.clone.in_ref) | copy-start | bytes 897028
  1.9 9.5 %collective-permute-start = (f32[2,3,8,512]{3,2,1,0:T(8,128)S(1)}, f32[2,3,8,512]{3,2,1,0:T(8,128)S(1)}, u32[]{:S(2)}, u32[]{:S(2)}) collective-permute-start(f32[2,3,8,512]{3,2,1,0:T(8,128)S(1)} %get-tuple-element.36), channel_id=1, source_target_pairs={{0,12},{2,14},{4,8},{6,10},{8,4},{10,6},{12,0},{14,2},{1,13},{3,15... | collective-permute-start | bytes 294920 | tf_op jit(solution)/shard_map/ppermute | solution.py:104
  7.0 6.1 %collective-permute-start.1 = (f32[2,3,8,512]{3,2,1,0:T(8,128)S(1)}, f32[2,3,8,512]{3,2,1,0:T(8,128)S(1)}, u32[]{:S(2)}, u32[]{:S(2)}) collective-permute-start(f32[2,3,8,512]{3,2,1,0:T(8,128)S(1)} %get-tuple-element.37), channel_id=1, source_target_pairs={{0,4},{2,6},{4,0},{6,2},{8,12},{10,14},{12,8},{14,10},{1,5},{3,7},... | collective-permute-start | bytes 294920 | tf_op jit(solution)/shard_map/ppermute | solution.py:104
  7.0 8.2 %collective-permute-start.2 = (f32[1,3,8,512]{3,2,1,0:T(8,128)S(1)}, f32[1,3,8,512]{3,2,1,0:T(8,128)S(1)}, u32[]{:S(2)}, u32[]{:S(2)}) collective-permute-start(f32[1,3,8,512]{3,2,1,0:T(8,128)S(1)} %get-tuple-element.38), channel_id=1, source_target_pairs={{0,10},{2,8},{4,14},{6,12},{8,2},{10,0},{12,6},{14,4},{1,11},{3,9}... | collective-permute-start | bytes 147464 | tf_op jit(solution)/shard_map/ppermute | solution.py:104
  8.7 6.5 %collective-permute-start.3 = (f32[1,3,8,512]{3,2,1,0:T(8,128)S(1)}, f32[1,3,8,512]{3,2,1,0:T(8,128)S(1)}, u32[]{:S(2)}, u32[]{:S(2)}) collective-permute-start(f32[1,3,8,512]{3,2,1,0:T(8,128)S(1)} %get-tuple-element.39), channel_id=1, source_target_pairs={{0,2},{2,0},{4,6},{6,4},{8,10},{10,8},{12,14},{14,12},{1,3},{3,1},... | collective-permute-start | bytes 147464 | tf_op jit(solution)/shard_map/ppermute | solution.py:104
  9.1 6.2 %collective-permute-start.4 = (f32[1,3,8,512]{3,2,1,0:T(8,128)S(1)}, f32[1,3,8,512]{3,2,1,0:T(8,128)S(1)}, u32[]{:S(2)}, u32[]{:S(2)}) collective-permute-start(f32[1,3,8,512]{3,2,1,0:T(8,128)S(1)} %get-tuple-element.40), channel_id=1, source_target_pairs={{0,8},{2,10},{4,12},{6,14},{8,0},{10,2},{12,4},{14,6},{1,9},{3,11}... | collective-permute-start | bytes 147464 | tf_op jit(solution)/shard_map/ppermute | solution.py:104
  11.4 4.7 %collective-permute-start.5 = (f32[1,3,8,512]{3,2,1,0:T(8,128)S(1)}, f32[1,3,8,512]{3,2,1,0:T(8,128)S(1)}, u32[]{:S(2)}, u32[]{:S(2)}) collective-permute-start(f32[1,3,8,512]{3,2,1,0:T(8,128)S(1)} %slice.16), channel_id=1, source_target_pairs={{0,2},{2,0},{4,6},{6,4},{8,10},{10,8},{12,14},{14,12},{1,3},{3,1},... | collective-permute-start | bytes 147464 | tf_op jit(solution)/shard_map/ppermute | solution.py:104
  13.1 4.1 %collective-permute-start.6 = (f32[1,3,8,512]{3,2,1,0:T(8,128)S(1)}, f32[1,3,8,512]{3,2,1,0:T(8,128)S(1)}, u32[]{:S(2)}, u32[]{:S(2)}) collective-permute-start(f32[1,3,8,512]{3,2,1,0:T(8,128)S(1)} %slice.17), channel_id=1, source_target_pairs={{0,2},{2,0},{4,6},{6,4},{8,10},{10,8},{12,14},{14,12},{1,3},{3,1},... | collective-permute-start | bytes 147464 | tf_op jit(solution)/shard_map/ppermute | solution.py:104
  19.3 7.9 %collective-permute-start.7 = (f32[2,104,128]{2,1,0:T(8,128)S(1)}, f32[2,104,128]{2,1,0:T(8,128)S(1)}, u32[]{:S(2)}, u32[]{:S(2)}) collective-permute-start(f32[2,104,128]{2,1,0:T(8,128)S(1)} %get-tuple-element.42), channel_id=1, source_target_pairs={{0,12},{2,14},{4,8},{6,10},{8,4},{10,6},{12,0},{14,2},{1,13},{3,15... | collective-permute-start | bytes 319496 | tf_op jit(solution)/shard_map/ppermute | solution.py:104
  22.3 6.0 %collective-permute-start.8 = (f32[2,104,128]{2,1,0:T(8,128)S(1)}, f32[2,104,128]{2,1,0:T(8,128)S(1)}, u32[]{:S(2)}, u32[]{:S(2)}) collective-permute-start(f32[2,104,128]{2,1,0:T(8,128)S(1)} %get-tuple-element.43), channel_id=1, source_target_pairs={{0,4},{2,6},{4,0},{6,2},{8,12},{10,14},{12,8},{14,10},{1,5},{3,7},... | collective-permute-start | bytes 319496 | tf_op jit(solution)/shard_map/ppermute | solution.py:104
  22.3 7.0 %collective-permute-start.9 = (f32[1,104,128]{2,1,0:T(8,128)S(1)}, f32[1,104,128]{2,1,0:T(8,128)S(1)}, u32[]{:S(2)}, u32[]{:S(2)}) collective-permute-start(f32[1,104,128]{2,1,0:T(8,128)S(1)} %get-tuple-element.44), channel_id=1, source_target_pairs={{0,2},{2,0},{4,6},{6,4},{8,10},{10,8},{12,14},{14,12},{1,3},{3,1},... | collective-permute-start | bytes 159752 | tf_op jit(solution)/shard_map/ppermute | solution.py:104
  22.8 6.6 %collective-permute-start.10 = (f32[1,104,128]{2,1,0:T(8,128)S(1)}, f32[1,104,128]{2,1,0:T(8,128)S(1)}, u32[]{:S(2)}, u32[]{:S(2)}) collective-permute-start(f32[1,104,128]{2,1,0:T(8,128)S(1)} %get-tuple-element.45), channel_id=1, source_target_pairs={{0,10},{2,8},{4,14},{6,12},{8,2},{10,0},{12,6},{14,4},{1,11},{3,9}... | collective-permute-start | bytes 159752 | tf_op jit(solution)/shard_map/ppermute | solution.py:104
  25.3 6.2 %collective-permute-start.11 = (f32[1,104,128]{2,1,0:T(8,128)S(1)}, f32[1,104,128]{2,1,0:T(8,128)S(1)}, u32[]{:S(2)}, u32[]{:S(2)}) collective-permute-start(f32[1,104,128]{2,1,0:T(8,128)S(1)} %get-tuple-element.46), channel_id=1, source_target_pairs={{0,8},{2,10},{4,12},{6,14},{8,0},{10,2},{12,4},{14,6},{1,9},{3,11}... | collective-permute-start | bytes 159752 | tf_op jit(solution)/shard_map/ppermute | solution.py:104
  27.2 4.2 %collective-permute-start.12 = (f32[1,104,128]{2,1,0:T(8,128)S(1)}, f32[1,104,128]{2,1,0:T(8,128)S(1)}, u32[]{:S(2)}, u32[]{:S(2)}) collective-permute-start(f32[1,104,128]{2,1,0:T(8,128)S(1)} %slice.18), channel_id=1, source_target_pairs={{0,2},{2,0},{4,6},{6,4},{8,10},{10,8},{12,14},{14,12},{1,3},{3,1},... | collective-permute-start | bytes 159752 | tf_op jit(solution)/shard_map/ppermute | solution.py:104
  28.3 4.2 %collective-permute-start.13 = (f32[1,104,128]{2,1,0:T(8,128)S(1)}, f32[1,104,128]{2,1,0:T(8,128)S(1)}, u32[]{:S(2)}, u32[]{:S(2)}) collective-permute-start(f32[1,104,128]{2,1,0:T(8,128)S(1)} %slice.19), channel_id=1, source_target_pairs={{0,2},{2,0},{4,6},{6,4},{8,10},{10,8},{12,14},{14,12},{1,3},{3,1},... | collective-permute-start | bytes 159752 | tf_op jit(solution)/shard_map/ppermute | solution.py:104

commit v5 on v4

--- a/solution.py
+++ b/solution.py
@@ -9,8 +9,8 @@
 from jax.sharding import PartitionSpec as P
 
 HIGHEST = lax.Precision.HIGHEST
-OUTWARD = ((6, 7), (2, 3), (5,), (1,), (4,))
-HOMEWARD = ((6, 7), (2, 3), (1,), (5,), (4,))
+OUTWARD = ((6, 7), (1, 3), (2,), (5,), (4,))
+HOMEWARD = ((6, 7), (1, 3), (4,), (2,), (5,))
 LANES = 128
 ROWS = 8
 VMEM = pl.BlockSpec(memory_space=pltpu.VMEM)
@@ -93,7 +93,7 @@
 def received(shards, groups):
     groups = sent(shards, groups)
     first = [(group[0], *(None for _ in group[1:])) for group in groups]
-    return (*first[:-1], *(group[1:] for group in groups if len(group) > 1), (0,))
+    return (*first[:-1], *((turn,) for group in groups for turn in group[1:]), (0,))
 
 
 def swap(arrays, groups):
@@ -103,8 +103,10 @@
     def move(array, turn):
         return lax.ppermute(array, "ctx", [(i, i ^ turn) for i in range(shards)])
 
-    moved = [move(x, members[0]) for members, x in zip(sent(shards, groups), arrays)]
-    relayed = [move(x[1:], 1) for x in moved if x.shape[0] > 1]
+    moved, relayed = [], []
+    for members, array in zip(sent(shards, groups), arrays):
+        moved.append(move(array, members[0]))
+        relayed += [move(moved[-1][i : i + 1], members[0] ^ members[i]) for i in range(1, len(members))]
     return (*moved, *relayed, own)
 
 

time: 33.5 us -> 32.7 us (0.976)
  waiting for transfers between devices: 6.28 us -> 4.12 us
  starting transfers between devices: 21.9 us -> 23.2 us
    ppermute x14, waiting for transfers between devices: 6.28 us -> 4.12 us  [move(): return lax.ppermute(array, 'ctx', [(i, i ^ turn) for i in range(shards)])]
    ppermute x14, starting transfers between devices: 21.9 us -> 23.2 us  [move(): return lax.ppermute(array, 'ctx', [(i, i ^ turn) for i in range(shards)])]
  transfers between devices with their start and end apart: 14 -> 14, of which waited for: 9 -> 6; matrix products, arithmetic and copies ran while one was open for 0% -> 0% of each run, Pallas kernels for 1% -> 1%
where the time goes in v5:
time: 32.7 us; the launch traced here: 32.6 us
  starting transfers between devices  23.2 us (71%)
  Pallas kernels  4.5 us (14%)
  waiting for transfers between devices  4.12 us (13%)
  between operations  0.7 us (2%)
    ppermute x14, starting transfers between devices, move(): return lax.ppermute(array, 'ctx', [(i, i ^ turn) for i in range(shards)])  23.2 us
    ppermute x14, waiting for transfers between devices, move(): return lax.ppermute(array, 'ctx', [(i, i ^ turn) for i in range(shards)])  4.12 us
    pallas_call x3, Pallas kernels, call(): pl.pallas_call(kernel, out_shape=out_shape, in_specs=[VMEM] * len(args),...  3.3 us
    pallas_call x1, Pallas kernels, by_channels(): pl.pallas_call(gate_kernel, out_shape=[*outs, pltpu.VMEM((4, channels, bl...  1.2 us
  transfers between devices with their start and end apart: 14, of which 6 were waited for; matrix products, arithmetic and copies ran while one was open for 0% of the time, Pallas kernels for 1%

profile of v5, /device:TPU:0, one launch (start us, length us, event | category | flops | bytes accessed | tf_op | source)
XLA Modules:
  0.0 32.6 jit_solution(7199147961984051519)
XLA Ops:
  0.6 1.2 %shard_map.118 = (f32[2,3,8,512]{3,2,1,0:T(8,128)S(1)}, f32[2,3,8,512]{3,2,1,0:T(8,128)S(1)}, f32[1,3,8,512]{3,2,1,0:T(8,128)S(1)}, f32[1,3,8,512]{3,2,1,0:T(8,1...) custom-call(bf16[64,512]{1,0:T(8,128)(2,1)} %first_hbm.1, ...), custom_call_target="tpu_custom_call" | custom-call | tf_op jit(solution)/shard_map/pallas_call | solution.py:256
  1.9 5.1 %collective-permute-start = (f32[2,3,8,512]{3,2,1,0:T(8,128)S(1)}, f32[2,3,8,512]{3,2,1,0:T(8,128)S(1)}, u32[]{:S(2)}, u32[]{:S(2)}) collective-permute-start(f32[2,3,8,512]{3,2,1,0:T(8,128)S(1)} %get-tuple-element.36), channel_id=1, source_target_pairs={{0,12},{2,14},{4,8},{6,10},{8,4},{10,6},{12,0},{14,2},{1,13},{3,15... | collective-permute-start | bytes 294920 | tf_op jit(solution)/shard_map/ppermute | solution.py:104
  7.0 1.5 %collective-permute-start.1 = (f32[2,3,8,512]{3,2,1,0:T(8,128)S(1)}, f32[2,3,8,512]{3,2,1,0:T(8,128)S(1)}, u32[]{:S(2)}, u32[]{:S(2)}) collective-permute-start(f32[2,3,8,512]{3,2,1,0:T(8,128)S(1)} %get-tuple-element.37), channel_id=1, source_target_pairs={{0,2},{2,0},{4,6},{6,4},{8,10},{10,8},{12,14},{14,12},{1,3},{3,1},... | collective-permute-start | bytes 294920 | tf_op jit(solution)/shard_map/ppermute | solution.py:104
  8.5 0.6 %collective-permute-start.3 = (f32[1,3,8,512]{3,2,1,0:T(8,128)S(1)}, f32[1,3,8,512]{3,2,1,0:T(8,128)S(1)}, u32[]{:S(2)}, u32[]{:S(2)}) collective-permute-start(f32[1,3,8,512]{3,2,1,0:T(8,128)S(1)} %get-tuple-element.39), channel_id=1, source_target_pairs={{0,10},{2,8},{4,14},{6,12},{8,2},{10,0},{12,6},{14,4},{1,11},{3,9}... | collective-permute-start | bytes 147464 | tf_op jit(solution)/shard_map/ppermute | solution.py:104
  9.1 2.3 %collective-permute-start.4 = (f32[1,3,8,512]{3,2,1,0:T(8,128)S(1)}, f32[1,3,8,512]{3,2,1,0:T(8,128)S(1)}, u32[]{:S(2)}, u32[]{:S(2)}) collective-permute-start(f32[1,3,8,512]{3,2,1,0:T(8,128)S(1)} %get-tuple-element.40), channel_id=1, source_target_pairs={{0,8},{2,10},{4,12},{6,14},{8,0},{10,2},{12,4},{14,6},{1,9},{3,11}... | collective-permute-start | bytes 147464 | tf_op jit(solution)/shard_map/ppermute | solution.py:104
  11.4 1.6 %collective-permute-start.5 = (f32[1,3,8,512]{3,2,1,0:T(8,128)S(1)}, f32[1,3,8,512]{3,2,1,0:T(8,128)S(1)}, u32[]{:S(2)}, u32[]{:S(2)}) collective-permute-start(f32[1,3,8,512]{3,2,1,0:T(8,128)S(1)} %slice.16), channel_id=1, source_target_pairs={{0,2},{2,0},{4,6},{6,4},{8,10},{10,8},{12,14},{14,12},{1,3},{3,1},... | collective-permute-start | bytes 147464 | tf_op jit(solution)/shard_map/ppermute | solution.py:104
  12.9 2.1 %collective-permute-start.6 = (f32[1,3,8,512]{3,2,1,0:T(8,128)S(1)}, f32[1,3,8,512]{3,2,1,0:T(8,128)S(1)}, u32[]{:S(2)}, u32[]{:S(2)}) collective-permute-start(f32[1,3,8,512]{3,2,1,0:T(8,128)S(1)} %slice.17), channel_id=1, source_target_pairs={{0,4},{2,6},{4,0},{6,2},{8,12},{10,14},{12,8},{14,10},{1,5},{3,7},... | collective-permute-start | bytes 147464 | tf_op jit(solution)/shard_map/ppermute | solution.py:104
  15.0 0.3 shard_map.119
  15.3 0.2 collective-permute-done.5.refs_5_
  15.5 1.6 %collective-permute-done.6.refs_6_ = f32[1,3,8,512]{3,2,1,0:T(8,128)S(1)} collective-permute-done((f32[1,3,8,512]{3,2,1,0:T(8,128)S(1)}, f32[1,3,8,512]{3,2,1,0:T(8,128)S(1)}, u32[]{:S(2)}, u32[]{:S(2)}) %collective-permute-start.6) | collective-permute-done | bytes 49184 | tf_op jit(solution)/shard_map/ppermute | solution.py:104
  17.1 2.1 %shard_map.120 = (f32[2,104,128]{2,1,0:T(8,128)S(1)}, f32[2,104,128]{2,1,0:T(8,128)S(1)}, f32[1,104,128]{2,1,0:T(8,128)S(1)}, f32[1,104,128]{2,1,0:T(8,128)S(1)}...) custom-call(bf16[2,512,256]{2,1,0:T(8,128)(2,1)S(1)} %get-tuple-element.31.outer_ref, ...), custom_call_target="tpu_custom_call" | custom-call | tf_op jit(solution)/shard_map/pallas_call | solution.py:236
  19.2 3.0 %collective-permute-start.7 = (f32[2,104,128]{2,1,0:T(8,128)S(1)}, f32[2,104,128]{2,1,0:T(8,128)S(1)}, u32[]{:S(2)}, u32[]{:S(2)}) collective-permute-start(f32[2,104,128]{2,1,0:T(8,128)S(1)} %get-tuple-element.42), channel_id=1, source_target_pairs={{0,12},{2,14},{4,8},{6,10},{8,4},{10,6},{12,0},{14,2},{1,13},{3,15... | collective-permute-start | bytes 319496 | tf_op jit(solution)/shard_map/ppermute | solution.py:104
  22.2 0.5 %collective-permute-start.8 = (f32[2,104,128]{2,1,0:T(8,128)S(1)}, f32[2,104,128]{2,1,0:T(8,128)S(1)}, u32[]{:S(2)}, u32[]{:S(2)}) collective-permute-start(f32[2,104,128]{2,1,0:T(8,128)S(1)} %get-tuple-element.43), channel_id=1, source_target_pairs={{0,2},{2,0},{4,6},{6,4},{8,10},{10,8},{12,14},{14,12},{1,3},{3,1},... | collective-permute-start | bytes 319496 | tf_op jit(solution)/shard_map/ppermute | solution.py:104
  22.7 0.5 %collective-permute-start.9 = (f32[1,104,128]{2,1,0:T(8,128)S(1)}, f32[1,104,128]{2,1,0:T(8,128)S(1)}, u32[]{:S(2)}, u32[]{:S(2)}) collective-permute-start(f32[1,104,128]{2,1,0:T(8,128)S(1)} %get-tuple-element.44), channel_id=1, source_target_pairs={{0,8},{2,10},{4,12},{6,14},{8,0},{10,2},{12,4},{14,6},{1,9},{3,11}... | collective-permute-start | bytes 159752 | tf_op jit(solution)/shard_map/ppermute | solution.py:104
  23.3 1.0 %collective-permute-start.10 = (f32[1,104,128]{2,1,0:T(8,128)S(1)}, f32[1,104,128]{2,1,0:T(8,128)S(1)}, u32[]{:S(2)}, u32[]{:S(2)}) collective-permute-start(f32[1,104,128]{2,1,0:T(8,128)S(1)} %get-tuple-element.45), channel_id=1, source_target_pairs={{0,4},{2,6},{4,0},{6,2},{8,12},{10,14},{12,8},{14,10},{1,5},{3,7},... | collective-permute-start | bytes 159752 | tf_op jit(solution)/shard_map/ppermute | solution.py:104
  24.3 2.4 %collective-permute-start.11 = (f32[1,104,128]{2,1,0:T(8,128)S(1)}, f32[1,104,128]{2,1,0:T(8,128)S(1)}, u32[]{:S(2)}, u32[]{:S(2)}) collective-permute-start(f32[1,104,128]{2,1,0:T(8,128)S(1)} %get-tuple-element.46), channel_id=1, source_target_pairs={{0,10},{2,8},{4,14},{6,12},{8,2},{10,0},{12,6},{14,4},{1,11},{3,9}... | collective-permute-start | bytes 159752 | tf_op jit(solution)/shard_map/ppermute | solution.py:104
  26.6 0.2 collective-permute-done.7.refs_0_
  26.9 0.3 %collective-permute-start.12 = (f32[1,104,128]{2,1,0:T(8,128)S(1)}, f32[1,104,128]{2,1,0:T(8,128)S(1)}, u32[]{:S(2)}, u32[]{:S(2)}) collective-permute-start(f32[1,104,128]{2,1,0:T(8,128)S(1)} %slice.18), channel_id=1, source_target_pairs={{0,2},{2,0},{4,6},{6,4},{8,10},{10,8},{12,14},{14,12},{1,3},{3,1},... | collective-permute-start | bytes 159752 | tf_op jit(solution)/shard_map/ppermute | solution.py:104
  27.2 0.0 collective-permute-done.8.refs_1_
  27.2 2.4 %collective-permute-start.13 = (f32[1,104,128]{2,1,0:T(8,128)S(1)}, f32[1,104,128]{2,1,0:T(8,128)S(1)}, u32[]{:S(2)}, u32[]{:S(2)}) collective-permute-start(f32[1,104,128]{2,1,0:T(8,128)S(1)} %slice.19), channel_id=1, source_target_pairs={{0,4},{2,6},{4,0},{6,2},{8,12},{10,14},{12,8},{14,10},{1,5},{3,7},... | collective-permute-start | bytes 159752 | tf_op jit(solution)/shard_map/ppermute | solution.py:104
  29.6 0.6 %collective-permute-done.11.refs_4_ = f32[1,104,128]{2,1,0:T(8,128)S(1)} collective-permute-done((f32[1,104,128]{2,1,0:T(8,128)S(1)}, f32[1,104,128]{2,1,0:T(8,128)S(1)}, u32[]{:S(2)}, u32[]{:S(2)}) %collective-permute-start.11) | collective-permute-done | bytes 53280 | tf_op jit(solution)/shard_map/ppermute | solution.py:104
  30.2 0.8 %collective-permute-done.12.refs_5_ = f32[1,104,128]{2,1,0:T(8,128)S(1)} collective-permute-done((f32[1,104,128]{2,1,0:T(8,128)S(1)}, f32[1,104,128]{2,1,0:T(8,128)S(1)}, u32[]{:S(2)}, u32[]{:S(2)}) %collective-permute-start.12) | collective-permute-done | bytes 53280 | tf_op jit(solution)/shard_map/ppermute | solution.py:104
  31.0 0.7 %collective-permute-done.13.refs_6_ = f32[1,104,128]{2,1,0:T(8,128)S(1)} collective-permute-done((f32[1,104,128]{2,1,0:T(8,128)S(1)}, f32[1,104,128]{2,1,0:T(8,128)S(1)}, u32[]{:S(2)}, u32[]{:S(2)}) %collective-permute-start.13) | collective-permute-done | bytes 53280 | tf_op jit(solution)/shard_map/ppermute | solution.py:104
  31.7 0.9 %shard_map.121 = (f32[64,512]{1,0:T(8,128)}, f32[64,512]{1,0:T(8,128)}, f32[64,512]{1,0:T(8,128)}, f32[64,512]{1,0:T(8,128)}, f32[64,512]{1,0:T(8,128)}, /*index=5*/f32[1,64]{1,0:T(1,128)}) custom-call(bf16[4,64,512]{2,1,0:T(8,128)(2,1)S(1)} %get-tuple-element.30.kept_ref, f32[2,104,128]{2,1,0:T(8,128)S(1)} %collective-permute-done.7.refs_0_, ...), custom_call_target="tpu_custom_call" | custom-call | tf_op jit(solution)/shard_map/pallas_call | solution.py:236
  (14 shorter events, 0.0 us)
Async XLA Ops:
  0.6 14.4 %copy-start = (f32[584,128]{1,0:T(8,128)S(1)}, f32[584,128]{1,0:T(8,128)}, u32[]{:S(2)}) copy-start(f32[584,128]{1,0:T(8,128)} %constant.2.clone.in_ref) | copy-start | bytes 897028
  1.9 9.5 %collective-permute-start = (f32[2,3,8,512]{3,2,1,0:T(8,128)S(1)}, f32[2,3,8,512]{3,2,1,0:T(8,128)S(1)}, u32[]{:S(2)}, u32[]{:S(2)}) collective-permute-start(f32[2,3,8,512]{3,2,1,0:T(8,128)S(1)} %get-tuple-element.36), channel_id=1, source_target_pairs={{0,12},{2,14},{4,8},{6,10},{8,4},{10,6},{12,0},{14,2},{1,13},{3,15... | collective-permute-start | bytes 294920 | tf_op jit(solution)/shard_map/ppermute | solution.py:104
  7.0 6.0 %collective-permute-start.1 = (f32[2,3,8,512]{3,2,1,0:T(8,128)S(1)}, f32[2,3,8,512]{3,2,1,0:T(8,128)S(1)}, u32[]{:S(2)}, u32[]{:S(2)}) collective-permute-start(f32[2,3,8,512]{3,2,1,0:T(8,128)S(1)} %get-tuple-element.37), channel_id=1, source_target_pairs={{0,2},{2,0},{4,6},{6,4},{8,10},{10,8},{12,14},{14,12},{1,3},{3,1},... | collective-permute-start | bytes 294920 | tf_op jit(solution)/shard_map/ppermute | solution.py:104
  8.5 6.9 %collective-permute-start.2 = (f32[1,3,8,512]{3,2,1,0:T(8,128)S(1)}, f32[1,3,8,512]{3,2,1,0:T(8,128)S(1)}, u32[]{:S(2)}, u32[]{:S(2)}) collective-permute-start(f32[1,3,8,512]{3,2,1,0:T(8,128)S(1)} %get-tuple-element.38), channel_id=1, source_target_pairs={{0,4},{2,6},{4,0},{6,2},{8,12},{10,14},{12,8},{14,10},{1,5},{3,7},... | collective-permute-start | bytes 147464 | tf_op jit(solution)/shard_map/ppermute | solution.py:104
  8.5 6.9 %collective-permute-start.3 = (f32[1,3,8,512]{3,2,1,0:T(8,128)S(1)}, f32[1,3,8,512]{3,2,1,0:T(8,128)S(1)}, u32[]{:S(2)}, u32[]{:S(2)}) collective-permute-start(f32[1,3,8,512]{3,2,1,0:T(8,128)S(1)} %get-tuple-element.39), channel_id=1, source_target_pairs={{0,10},{2,8},{4,14},{6,12},{8,2},{10,0},{12,6},{14,4},{1,11},{3,9}... | collective-permute-start | bytes 147464 | tf_op jit(solution)/shard_map/ppermute | solution.py:104
  9.1 6.3 %collective-permute-start.4 = (f32[1,3,8,512]{3,2,1,0:T(8,128)S(1)}, f32[1,3,8,512]{3,2,1,0:T(8,128)S(1)}, u32[]{:S(2)}, u32[]{:S(2)}) collective-permute-start(f32[1,3,8,512]{3,2,1,0:T(8,128)S(1)} %get-tuple-element.40), channel_id=1, source_target_pairs={{0,8},{2,10},{4,12},{6,14},{8,0},{10,2},{12,4},{14,6},{1,9},{3,11}... | collective-permute-start | bytes 147464 | tf_op jit(solution)/shard_map/ppermute | solution.py:104
  11.4 4.2 %collective-permute-start.5 = (f32[1,3,8,512]{3,2,1,0:T(8,128)S(1)}, f32[1,3,8,512]{3,2,1,0:T(8,128)S(1)}, u32[]{:S(2)}, u32[]{:S(2)}) collective-permute-start(f32[1,3,8,512]{3,2,1,0:T(8,128)S(1)} %slice.16), channel_id=1, source_target_pairs={{0,2},{2,0},{4,6},{6,4},{8,10},{10,8},{12,14},{14,12},{1,3},{3,1},... | collective-permute-start | bytes 147464 | tf_op jit(solution)/shard_map/ppermute | solution.py:104
  12.9 4.2 %collective-permute-start.6 = (f32[1,3,8,512]{3,2,1,0:T(8,128)S(1)}, f32[1,3,8,512]{3,2,1,0:T(8,128)S(1)}, u32[]{:S(2)}, u32[]{:S(2)}) collective-permute-start(f32[1,3,8,512]{3,2,1,0:T(8,128)S(1)} %slice.17), channel_id=1, source_target_pairs={{0,4},{2,6},{4,0},{6,2},{8,12},{10,14},{12,8},{14,10},{1,5},{3,7},... | collective-permute-start | bytes 147464 | tf_op jit(solution)/shard_map/ppermute | solution.py:104
  19.2 7.7 %collective-permute-start.7 = (f32[2,104,128]{2,1,0:T(8,128)S(1)}, f32[2,104,128]{2,1,0:T(8,128)S(1)}, u32[]{:S(2)}, u32[]{:S(2)}) collective-permute-start(f32[2,104,128]{2,1,0:T(8,128)S(1)} %get-tuple-element.42), channel_id=1, source_target_pairs={{0,12},{2,14},{4,8},{6,10},{8,4},{10,6},{12,0},{14,2},{1,13},{3,15... | collective-permute-start | bytes 319496 | tf_op jit(solution)/shard_map/ppermute | solution.py:104
  22.2 5.0 %collective-permute-start.8 = (f32[2,104,128]{2,1,0:T(8,128)S(1)}, f32[2,104,128]{2,1,0:T(8,128)S(1)}, u32[]{:S(2)}, u32[]{:S(2)}) collective-permute-start(f32[2,104,128]{2,1,0:T(8,128)S(1)} %get-tuple-element.43), channel_id=1, source_target_pairs={{0,2},{2,0},{4,6},{6,4},{8,10},{10,8},{12,14},{14,12},{1,3},{3,1},... | collective-permute-start | bytes 319496 | tf_op jit(solution)/shard_map/ppermute | solution.py:104
  22.7 6.9 %collective-permute-start.9 = (f32[1,104,128]{2,1,0:T(8,128)S(1)}, f32[1,104,128]{2,1,0:T(8,128)S(1)}, u32[]{:S(2)}, u32[]{:S(2)}) collective-permute-start(f32[1,104,128]{2,1,0:T(8,128)S(1)} %get-tuple-element.44), channel_id=1, source_target_pairs={{0,8},{2,10},{4,12},{6,14},{8,0},{10,2},{12,4},{14,6},{1,9},{3,11}... | collective-permute-start | bytes 159752 | tf_op jit(solution)/shard_map/ppermute | solution.py:104
  23.3 6.3 %collective-permute-start.10 = (f32[1,104,128]{2,1,0:T(8,128)S(1)}, f32[1,104,128]{2,1,0:T(8,128)S(1)}, u32[]{:S(2)}, u32[]{:S(2)}) collective-permute-start(f32[1,104,128]{2,1,0:T(8,128)S(1)} %get-tuple-element.45), channel_id=1, source_target_pairs={{0,4},{2,6},{4,0},{6,2},{8,12},{10,14},{12,8},{14,10},{1,5},{3,7},... | collective-permute-start | bytes 159752 | tf_op jit(solution)/shard_map/ppermute | solution.py:104
  24.3 5.9 %collective-permute-start.11 = (f32[1,104,128]{2,1,0:T(8,128)S(1)}, f32[1,104,128]{2,1,0:T(8,128)S(1)}, u32[]{:S(2)}, u32[]{:S(2)}) collective-permute-start(f32[1,104,128]{2,1,0:T(8,128)S(1)} %get-tuple-element.46), channel_id=1, source_target_pairs={{0,10},{2,8},{4,14},{6,12},{8,2},{10,0},{12,6},{14,4},{1,11},{3,9}... | collective-permute-start | bytes 159752 | tf_op jit(solution)/shard_map/ppermute | solution.py:104
  26.9 4.1 %collective-permute-start.12 = (f32[1,104,128]{2,1,0:T(8,128)S(1)}, f32[1,104,128]{2,1,0:T(8,128)S(1)}, u32[]{:S(2)}, u32[]{:S(2)}) collective-permute-start(f32[1,104,128]{2,1,0:T(8,128)S(1)} %slice.18), channel_id=1, source_target_pairs={{0,2},{2,0},{4,6},{6,4},{8,10},{10,8},{12,14},{14,12},{1,3},{3,1},... | collective-permute-start | bytes 159752 | tf_op jit(solution)/shard_map/ppermute | solution.py:104
  27.2 4.5 %collective-permute-start.13 = (f32[1,104,128]{2,1,0:T(8,128)S(1)}, f32[1,104,128]{2,1,0:T(8,128)S(1)}, u32[]{:S(2)}, u32[]{:S(2)}) collective-permute-start(f32[1,104,128]{2,1,0:T(8,128)S(1)} %slice.19), channel_id=1, source_target_pairs={{0,4},{2,6},{4,0},{6,2},{8,12},{10,14},{12,8},{14,10},{1,5},{3,7},... | collective-permute-start | bytes 159752 | tf_op jit(solution)/shard_map/ppermute | solution.py:104

commit v6 on v5

--- a/solution.py
+++ b/solution.py
@@ -63,6 +63,13 @@
     return dot(left[0], right[0]) + (dot(left[0], right[1]) + dot(left[1], right[0]))
 
 
+def table_dot(table, data):
+    high, low = split(data)
+    both = dot(table[0], jnp.concatenate([high, low], axis=1))
+    columns = data.shape[1]
+    return both[:, :columns] + (both[:, columns:] + dot(table[1], high))
+
+
 def table_kernel(in_ref, outer_ref, back_ref, forward_ref, inverse_ref, twist_ref):
     groups = outer_ref.shape[2] // ROWS
     tiles = outer_ref.shape[2] // LANES
@@ -178,7 +185,7 @@
     total = jnp.sum((signals[0] * signals[2]).reshape(rows // ROWS, ROWS, LANES), axis=0)
     total = jnp.broadcast_to(jnp.sum(total, axis=1, keepdims=True), (ROWS, LANES))
     all_ref[:, 3 * span :, :] = jnp.broadcast_to(total[None], (shards, ROWS, LANES))
-    columns = long_dot(outer_ref, split(jnp.concatenate(signals, axis=1)))
+    columns = table_dot(outer_ref, jnp.concatenate(signals, axis=1))
     edge = jnp.zeros((ROWS, LANES), jnp.float32)
     spectra = []
     for s in range(3):
@@ -199,7 +206,7 @@
         real, imag = waves[:, :LANES], waves[:, LANES:]
         turned_imag = real * sine + imag * cosine
         reverted.append(jnp.concatenate([real * cosine - imag * sine, turned_imag[ROWS:-ROWS]], axis=0))
-    result = long_dot(back_ref, split(jnp.concatenate(reverted, axis=1)))
+    result = table_dot(back_ref, jnp.concatenate(reverted, axis=1))
     for s in range(3):
         all_ref[:, s * span : (s + 1) * span, :] = result[:, s * LANES : (s + 1) * LANES].reshape(shards, span, LANES)
     scatter(out_refs, all_ref, HOMEWARD)

time: 32.7 us -> 32.6 us (level)
  no operation moved by 1% of the time
where the time goes in v6:
time: 32.6 us; the launch traced here: 32.5 us
  starting transfers between devices  23.3 us (71%)
  Pallas kernels  4.37 us (13%)
  waiting for transfers between devices  4.12 us (13%)
  between operations  0.7 us (2%)
    ppermute x14, starting transfers between devices, move(): return lax.ppermute(array, 'ctx', [(i, i ^ turn) for i in range(shards)])  23.3 us
    ppermute x14, waiting for transfers between devices, move(): return lax.ppermute(array, 'ctx', [(i, i ^ turn) for i in range(shards)])  4.12 us
    pallas_call x3, Pallas kernels, call(): pl.pallas_call(kernel, out_shape=out_shape, in_specs=[VMEM] * len(args),...  3.17 us
    pallas_call x1, Pallas kernels, by_channels(): pl.pallas_call(gate_kernel, out_shape=[*outs, pltpu.VMEM((4, channels, bl...  1.2 us
  transfers between devices with their start and end apart: 14, of which 6 were waited for; matrix products, arithmetic and copies ran while one was open for 0% of the time, Pallas kernels for 1%

profile of v6, /device:TPU:0, one launch (start us, length us, event | category | flops | bytes accessed | tf_op | source)
XLA Modules:
  0.0 32.5 jit_solution(7860871399851015192)
XLA Ops:
  0.6 1.2 %shard_map.118 = (f32[2,3,8,512]{3,2,1,0:T(8,128)S(1)}, f32[2,3,8,512]{3,2,1,0:T(8,128)S(1)}, f32[1,3,8,512]{3,2,1,0:T(8,128)S(1)}, f32[1,3,8,512]{3,2,1,0:T(8,1...) custom-call(bf16[64,512]{1,0:T(8,128)(2,1)} %first_hbm.1, ...), custom_call_target="tpu_custom_call" | custom-call | tf_op jit(solution)/shard_map/pallas_call | solution.py:263
  1.9 5.1 %collective-permute-start = (f32[2,3,8,512]{3,2,1,0:T(8,128)S(1)}, f32[2,3,8,512]{3,2,1,0:T(8,128)S(1)}, u32[]{:S(2)}, u32[]{:S(2)}) collective-permute-start(f32[2,3,8,512]{3,2,1,0:T(8,128)S(1)} %get-tuple-element.36), channel_id=1, source_target_pairs={{0,12},{2,14},{4,8},{6,10},{8,4},{10,6},{12,0},{14,2},{1,13},{3,15... | collective-permute-start | bytes 294920 | tf_op jit(solution)/shard_map/ppermute | solution.py:111
  7.0 1.5 %collective-permute-start.1 = (f32[2,3,8,512]{3,2,1,0:T(8,128)S(1)}, f32[2,3,8,512]{3,2,1,0:T(8,128)S(1)}, u32[]{:S(2)}, u32[]{:S(2)}) collective-permute-start(f32[2,3,8,512]{3,2,1,0:T(8,128)S(1)} %get-tuple-element.37), channel_id=1, source_target_pairs={{0,2},{2,0},{4,6},{6,4},{8,10},{10,8},{12,14},{14,12},{1,3},{3,1},... | collective-permute-start | bytes 294920 | tf_op jit(solution)/shard_map/ppermute | solution.py:111
  8.5 0.6 %collective-permute-start.3 = (f32[1,3,8,512]{3,2,1,0:T(8,128)S(1)}, f32[1,3,8,512]{3,2,1,0:T(8,128)S(1)}, u32[]{:S(2)}, u32[]{:S(2)}) collective-permute-start(f32[1,3,8,512]{3,2,1,0:T(8,128)S(1)} %get-tuple-element.39), channel_id=1, source_target_pairs={{0,10},{2,8},{4,14},{6,12},{8,2},{10,0},{12,6},{14,4},{1,11},{3,9}... | collective-permute-start | bytes 147464 | tf_op jit(solution)/shard_map/ppermute | solution.py:111
  9.1 2.3 %collective-permute-start.4 = (f32[1,3,8,512]{3,2,1,0:T(8,128)S(1)}, f32[1,3,8,512]{3,2,1,0:T(8,128)S(1)}, u32[]{:S(2)}, u32[]{:S(2)}) collective-permute-start(f32[1,3,8,512]{3,2,1,0:T(8,128)S(1)} %get-tuple-element.40), channel_id=1, source_target_pairs={{0,8},{2,10},{4,12},{6,14},{8,0},{10,2},{12,4},{14,6},{1,9},{3,11}... | collective-permute-start | bytes 147464 | tf_op jit(solution)/shard_map/ppermute | solution.py:111
  11.4 1.6 %collective-permute-start.5 = (f32[1,3,8,512]{3,2,1,0:T(8,128)S(1)}, f32[1,3,8,512]{3,2,1,0:T(8,128)S(1)}, u32[]{:S(2)}, u32[]{:S(2)}) collective-permute-start(f32[1,3,8,512]{3,2,1,0:T(8,128)S(1)} %slice.16), channel_id=1, source_target_pairs={{0,2},{2,0},{4,6},{6,4},{8,10},{10,8},{12,14},{14,12},{1,3},{3,1},... | collective-permute-start | bytes 147464 | tf_op jit(solution)/shard_map/ppermute | solution.py:111
  12.9 2.1 %collective-permute-start.6 = (f32[1,3,8,512]{3,2,1,0:T(8,128)S(1)}, f32[1,3,8,512]{3,2,1,0:T(8,128)S(1)}, u32[]{:S(2)}, u32[]{:S(2)}) collective-permute-start(f32[1,3,8,512]{3,2,1,0:T(8,128)S(1)} %slice.17), channel_id=1, source_target_pairs={{0,4},{2,6},{4,0},{6,2},{8,12},{10,14},{12,8},{14,10},{1,5},{3,7},... | collective-permute-start | bytes 147464 | tf_op jit(solution)/shard_map/ppermute | solution.py:111
  15.0 0.3 shard_map.119
  15.3 0.2 collective-permute-done.5.refs_5_
  15.5 1.6 %collective-permute-done.6.refs_6_ = f32[1,3,8,512]{3,2,1,0:T(8,128)S(1)} collective-permute-done((f32[1,3,8,512]{3,2,1,0:T(8,128)S(1)}, f32[1,3,8,512]{3,2,1,0:T(8,128)S(1)}, u32[]{:S(2)}, u32[]{:S(2)}) %collective-permute-start.6) | collective-permute-done | bytes 49184 | tf_op jit(solution)/shard_map/ppermute | solution.py:111
  17.1 2.0 %shard_map.120 = (f32[2,104,128]{2,1,0:T(8,128)S(1)}, f32[2,104,128]{2,1,0:T(8,128)S(1)}, f32[1,104,128]{2,1,0:T(8,128)S(1)}, f32[1,104,128]{2,1,0:T(8,128)S(1)}...) custom-call(bf16[2,512,256]{2,1,0:T(8,128)(2,1)S(1)} %get-tuple-element.31.outer_ref, ...), custom_call_target="tpu_custom_call" | custom-call | tf_op jit(solution)/shard_map/pallas_call | solution.py:243
  19.1 3.0 %collective-permute-start.7 = (f32[2,104,128]{2,1,0:T(8,128)S(1)}, f32[2,104,128]{2,1,0:T(8,128)S(1)}, u32[]{:S(2)}, u32[]{:S(2)}) collective-permute-start(f32[2,104,128]{2,1,0:T(8,128)S(1)} %get-tuple-element.42), channel_id=1, source_target_pairs={{0,12},{2,14},{4,8},{6,10},{8,4},{10,6},{12,0},{14,2},{1,13},{3,15... | collective-permute-start | bytes 319496 | tf_op jit(solution)/shard_map/ppermute | solution.py:111
  22.1 0.5 %collective-permute-start.8 = (f32[2,104,128]{2,1,0:T(8,128)S(1)}, f32[2,104,128]{2,1,0:T(8,128)S(1)}, u32[]{:S(2)}, u32[]{:S(2)}) collective-permute-start(f32[2,104,128]{2,1,0:T(8,128)S(1)} %get-tuple-element.43), channel_id=1, source_target_pairs={{0,2},{2,0},{4,6},{6,4},{8,10},{10,8},{12,14},{14,12},{1,3},{3,1},... | collective-permute-start | bytes 319496 | tf_op jit(solution)/shard_map/ppermute | solution.py:111
  22.6 0.5 %collective-permute-start.9 = (f32[1,104,128]{2,1,0:T(8,128)S(1)}, f32[1,104,128]{2,1,0:T(8,128)S(1)}, u32[]{:S(2)}, u32[]{:S(2)}) collective-permute-start(f32[1,104,128]{2,1,0:T(8,128)S(1)} %get-tuple-element.44), channel_id=1, source_target_pairs={{0,8},{2,10},{4,12},{6,14},{8,0},{10,2},{12,4},{14,6},{1,9},{3,11}... | collective-permute-start | bytes 159752 | tf_op jit(solution)/shard_map/ppermute | solution.py:111
  23.2 1.0 %collective-permute-start.10 = (f32[1,104,128]{2,1,0:T(8,128)S(1)}, f32[1,104,128]{2,1,0:T(8,128)S(1)}, u32[]{:S(2)}, u32[]{:S(2)}) collective-permute-start(f32[1,104,128]{2,1,0:T(8,128)S(1)} %get-tuple-element.45), channel_id=1, source_target_pairs={{0,4},{2,6},{4,0},{6,2},{8,12},{10,14},{12,8},{14,10},{1,5},{3,7},... | collective-permute-start | bytes 159752 | tf_op jit(solution)/shard_map/ppermute | solution.py:111
  24.2 2.4 %collective-permute-start.11 = (f32[1,104,128]{2,1,0:T(8,128)S(1)}, f32[1,104,128]{2,1,0:T(8,128)S(1)}, u32[]{:S(2)}, u32[]{:S(2)}) collective-permute-start(f32[1,104,128]{2,1,0:T(8,128)S(1)} %get-tuple-element.46), channel_id=1, source_target_pairs={{0,10},{2,8},{4,14},{6,12},{8,2},{10,0},{12,6},{14,4},{1,11},{3,9}... | collective-permute-start | bytes 159752 | tf_op jit(solution)/shard_map/ppermute | solution.py:111
  26.5 0.2 collective-permute-done.7.refs_0_
  26.7 0.3 %collective-permute-start.12 = (f32[1,104,128]{2,1,0:T(8,128)S(1)}, f32[1,104,128]{2,1,0:T(8,128)S(1)}, u32[]{:S(2)}, u32[]{:S(2)}) collective-permute-start(f32[1,104,128]{2,1,0:T(8,128)S(1)} %slice.18), channel_id=1, source_target_pairs={{0,2},{2,0},{4,6},{6,4},{8,10},{10,8},{12,14},{14,12},{1,3},{3,1},... | collective-permute-start | bytes 159752 | tf_op jit(solution)/shard_map/ppermute | solution.py:111
  27.1 0.0 collective-permute-done.8.refs_1_
  27.1 2.4 %collective-permute-start.13 = (f32[1,104,128]{2,1,0:T(8,128)S(1)}, f32[1,104,128]{2,1,0:T(8,128)S(1)}, u32[]{:S(2)}, u32[]{:S(2)}) collective-permute-start(f32[1,104,128]{2,1,0:T(8,128)S(1)} %slice.19), channel_id=1, source_target_pairs={{0,4},{2,6},{4,0},{6,2},{8,12},{10,14},{12,8},{14,10},{1,5},{3,7},... | collective-permute-start | bytes 159752 | tf_op jit(solution)/shard_map/ppermute | solution.py:111
  29.5 0.6 %collective-permute-done.11.refs_4_ = f32[1,104,128]{2,1,0:T(8,128)S(1)} collective-permute-done((f32[1,104,128]{2,1,0:T(8,128)S(1)}, f32[1,104,128]{2,1,0:T(8,128)S(1)}, u32[]{:S(2)}, u32[]{:S(2)}) %collective-permute-start.11) | collective-permute-done | bytes 53280 | tf_op jit(solution)/shard_map/ppermute | solution.py:111
  30.1 0.8 %collective-permute-done.12.refs_5_ = f32[1,104,128]{2,1,0:T(8,128)S(1)} collective-permute-done((f32[1,104,128]{2,1,0:T(8,128)S(1)}, f32[1,104,128]{2,1,0:T(8,128)S(1)}, u32[]{:S(2)}, u32[]{:S(2)}) %collective-permute-start.12) | collective-permute-done | bytes 53280 | tf_op jit(solution)/shard_map/ppermute | solution.py:111
  30.9 0.7 %collective-permute-done.13.refs_6_ = f32[1,104,128]{2,1,0:T(8,128)S(1)} collective-permute-done((f32[1,104,128]{2,1,0:T(8,128)S(1)}, f32[1,104,128]{2,1,0:T(8,128)S(1)}, u32[]{:S(2)}, u32[]{:S(2)}) %collective-permute-start.13) | collective-permute-done | bytes 53280 | tf_op jit(solution)/shard_map/ppermute | solution.py:111
  31.6 0.9 %shard_map.121 = (f32[64,512]{1,0:T(8,128)}, f32[64,512]{1,0:T(8,128)}, f32[64,512]{1,0:T(8,128)}, f32[64,512]{1,0:T(8,128)}, f32[64,512]{1,0:T(8,128)}, /*index=5*/f32[1,64]{1,0:T(1,128)}) custom-call(bf16[4,64,512]{2,1,0:T(8,128)(2,1)S(1)} %get-tuple-element.30.kept_ref, f32[2,104,128]{2,1,0:T(8,128)S(1)} %collective-permute-done.7.refs_0_, ...), custom_call_target="tpu_custom_call" | custom-call | tf_op jit(solution)/shard_map/pallas_call | solution.py:243
  (14 shorter events, 0.0 us)
Async XLA Ops:
  0.6 14.4 %copy-start = (f32[584,128]{1,0:T(8,128)S(1)}, f32[584,128]{1,0:T(8,128)}, u32[]{:S(2)}) copy-start(f32[584,128]{1,0:T(8,128)} %constant.2.clone.in_ref) | copy-start | bytes 897028
  1.9 9.5 %collective-permute-start = (f32[2,3,8,512]{3,2,1,0:T(8,128)S(1)}, f32[2,3,8,512]{3,2,1,0:T(8,128)S(1)}, u32[]{:S(2)}, u32[]{:S(2)}) collective-permute-start(f32[2,3,8,512]{3,2,1,0:T(8,128)S(1)} %get-tuple-element.36), channel_id=1, source_target_pairs={{0,12},{2,14},{4,8},{6,10},{8,4},{10,6},{12,0},{14,2},{1,13},{3,15... | collective-permute-start | bytes 294920 | tf_op jit(solution)/shard_map/ppermute | solution.py:111
  7.0 6.0 %collective-permute-start.1 = (f32[2,3,8,512]{3,2,1,0:T(8,128)S(1)}, f32[2,3,8,512]{3,2,1,0:T(8,128)S(1)}, u32[]{:S(2)}, u32[]{:S(2)}) collective-permute-start(f32[2,3,8,512]{3,2,1,0:T(8,128)S(1)} %get-tuple-element.37), channel_id=1, source_target_pairs={{0,2},{2,0},{4,6},{6,4},{8,10},{10,8},{12,14},{14,12},{1,3},{3,1},... | collective-permute-start | bytes 294920 | tf_op jit(solution)/shard_map/ppermute | solution.py:111
  8.5 6.9 %collective-permute-start.2 = (f32[1,3,8,512]{3,2,1,0:T(8,128)S(1)}, f32[1,3,8,512]{3,2,1,0:T(8,128)S(1)}, u32[]{:S(2)}, u32[]{:S(2)}) collective-permute-start(f32[1,3,8,512]{3,2,1,0:T(8,128)S(1)} %get-tuple-element.38), channel_id=1, source_target_pairs={{0,4},{2,6},{4,0},{6,2},{8,12},{10,14},{12,8},{14,10},{1,5},{3,7},... | collective-permute-start | bytes 147464 | tf_op jit(solution)/shard_map/ppermute | solution.py:111
  8.5 6.9 %collective-permute-start.3 = (f32[1,3,8,512]{3,2,1,0:T(8,128)S(1)}, f32[1,3,8,512]{3,2,1,0:T(8,128)S(1)}, u32[]{:S(2)}, u32[]{:S(2)}) collective-permute-start(f32[1,3,8,512]{3,2,1,0:T(8,128)S(1)} %get-tuple-element.39), channel_id=1, source_target_pairs={{0,10},{2,8},{4,14},{6,12},{8,2},{10,0},{12,6},{14,4},{1,11},{3,9}... | collective-permute-start | bytes 147464 | tf_op jit(solution)/shard_map/ppermute | solution.py:111
  9.1 6.3 %collective-permute-start.4 = (f32[1,3,8,512]{3,2,1,0:T(8,128)S(1)}, f32[1,3,8,512]{3,2,1,0:T(8,128)S(1)}, u32[]{:S(2)}, u32[]{:S(2)}) collective-permute-start(f32[1,3,8,512]{3,2,1,0:T(8,128)S(1)} %get-tuple-element.40), channel_id=1, source_target_pairs={{0,8},{2,10},{4,12},{6,14},{8,0},{10,2},{12,4},{14,6},{1,9},{3,11}... | collective-permute-start | bytes 147464 | tf_op jit(solution)/shard_map/ppermute | solution.py:111
  11.4 4.2 %collective-permute-start.5 = (f32[1,3,8,512]{3,2,1,0:T(8,128)S(1)}, f32[1,3,8,512]{3,2,1,0:T(8,128)S(1)}, u32[]{:S(2)}, u32[]{:S(2)}) collective-permute-start(f32[1,3,8,512]{3,2,1,0:T(8,128)S(1)} %slice.16), channel_id=1, source_target_pairs={{0,2},{2,0},{4,6},{6,4},{8,10},{10,8},{12,14},{14,12},{1,3},{3,1},... | collective-permute-start | bytes 147464 | tf_op jit(solution)/shard_map/ppermute | solution.py:111
  12.9 4.2 %collective-permute-start.6 = (f32[1,3,8,512]{3,2,1,0:T(8,128)S(1)}, f32[1,3,8,512]{3,2,1,0:T(8,128)S(1)}, u32[]{:S(2)}, u32[]{:S(2)}) collective-permute-start(f32[1,3,8,512]{3,2,1,0:T(8,128)S(1)} %slice.17), channel_id=1, source_target_pairs={{0,4},{2,6},{4,0},{6,2},{8,12},{10,14},{12,8},{14,10},{1,5},{3,7},... | collective-permute-start | bytes 147464 | tf_op jit(solution)/shard_map/ppermute | solution.py:111
  19.1 7.7 %collective-permute-start.7 = (f32[2,104,128]{2,1,0:T(8,128)S(1)}, f32[2,104,128]{2,1,0:T(8,128)S(1)}, u32[]{:S(2)}, u32[]{:S(2)}) collective-permute-start(f32[2,104,128]{2,1,0:T(8,128)S(1)} %get-tuple-element.42), channel_id=1, source_target_pairs={{0,12},{2,14},{4,8},{6,10},{8,4},{10,6},{12,0},{14,2},{1,13},{3,15... | collective-permute-start | bytes 319496 | tf_op jit(solution)/shard_map/ppermute | solution.py:111
  22.1 5.0 %collective-permute-start.8 = (f32[2,104,128]{2,1,0:T(8,128)S(1)}, f32[2,104,128]{2,1,0:T(8,128)S(1)}, u32[]{:S(2)}, u32[]{:S(2)}) collective-permute-start(f32[2,104,128]{2,1,0:T(8,128)S(1)} %get-tuple-element.43), channel_id=1, source_target_pairs={{0,2},{2,0},{4,6},{6,4},{8,10},{10,8},{12,14},{14,12},{1,3},{3,1},... | collective-permute-start | bytes 319496 | tf_op jit(solution)/shard_map/ppermute | solution.py:111
  22.6 6.9 %collective-permute-start.9 = (f32[1,104,128]{2,1,0:T(8,128)S(1)}, f32[1,104,128]{2,1,0:T(8,128)S(1)}, u32[]{:S(2)}, u32[]{:S(2)}) collective-permute-start(f32[1,104,128]{2,1,0:T(8,128)S(1)} %get-tuple-element.44), channel_id=1, source_target_pairs={{0,8},{2,10},{4,12},{6,14},{8,0},{10,2},{12,4},{14,6},{1,9},{3,11}... | collective-permute-start | bytes 159752 | tf_op jit(solution)/shard_map/ppermute | solution.py:111
  23.2 6.3 %collective-permute-start.10 = (f32[1,104,128]{2,1,0:T(8,128)S(1)}, f32[1,104,128]{2,1,0:T(8,128)S(1)}, u32[]{:S(2)}, u32[]{:S(2)}) collective-permute-start(f32[1,104,128]{2,1,0:T(8,128)S(1)} %get-tuple-element.45), channel_id=1, source_target_pairs={{0,4},{2,6},{4,0},{6,2},{8,12},{10,14},{12,8},{14,10},{1,5},{3,7},... | collective-permute-start | bytes 159752 | tf_op jit(solution)/shard_map/ppermute | solution.py:111
  24.2 5.9 %collective-permute-start.11 = (f32[1,104,128]{2,1,0:T(8,128)S(1)}, f32[1,104,128]{2,1,0:T(8,128)S(1)}, u32[]{:S(2)}, u32[]{:S(2)}) collective-permute-start(f32[1,104,128]{2,1,0:T(8,128)S(1)} %get-tuple-element.46), channel_id=1, source_target_pairs={{0,10},{2,8},{4,14},{6,12},{8,2},{10,0},{12,6},{14,4},{1,11},{3,9}... | collective-permute-start | bytes 159752 | tf_op jit(solution)/shard_map/ppermute | solution.py:111
  26.7 4.1 %collective-permute-start.12 = (f32[1,104,128]{2,1,0:T(8,128)S(1)}, f32[1,104,128]{2,1,0:T(8,128)S(1)}, u32[]{:S(2)}, u32[]{:S(2)}) collective-permute-start(f32[1,104,128]{2,1,0:T(8,128)S(1)} %slice.18), channel_id=1, source_target_pairs={{0,2},{2,0},{4,6},{6,4},{8,10},{10,8},{12,14},{14,12},{1,3},{3,1},... | collective-permute-start | bytes 159752 | tf_op jit(solution)/shard_map/ppermute | solution.py:111
  27.1 4.5 %collective-permute-start.13 = (f32[1,104,128]{2,1,0:T(8,128)S(1)}, f32[1,104,128]{2,1,0:T(8,128)S(1)}, u32[]{:S(2)}, u32[]{:S(2)}) collective-permute-start(f32[1,104,128]{2,1,0:T(8,128)S(1)} %slice.19), channel_id=1, source_target_pairs={{0,4},{2,6},{4,0},{6,2},{8,12},{10,14},{12,8},{14,10},{1,5},{3,7},... | collective-permute-start | bytes 159752 | tf_op jit(solution)/shard_map/ppermute | solution.py:111

commit v7 on v6

--- a/solution.py
+++ b/solution.py
@@ -148,6 +148,9 @@
         for j in range(blocks // LANES):
             tile = signal[:, j * LANES : (j + 1) * LANES].reshape(shards, ROWS, LANES)
             all_ref[:, s, :, j * LANES : (j + 1) * LANES] = tile
+        for members, ref in zip(sent(shards, OUTWARD), out_refs):
+            for i, turn in enumerate(members):
+                ref[i, s] = all_ref[me ^ turn, s]
 
     copies[0].wait()
     copies[1].wait()
@@ -162,7 +165,6 @@
     copies[4].wait()
     copies[5].wait()
     place(2, kept_ref[2].astype(jnp.float32) * kept_ref[3].astype(jnp.float32))
-    scatter(out_refs, all_ref, OUTWARD)
 
 
 def spectral_kernel(outer_ref, back_ref, forward_ref, inverse_ref, twist_ref, *refs):

time: 32.6 us -> 32.6 us (level)
  no operation moved by 1% of the time
where the time goes in v7:
time: 32.6 us; the launch traced here: 32.5 us
  starting transfers between devices  23.2 us (71%)
  Pallas kernels  4.37 us (13%)
  waiting for transfers between devices  4.11 us (13%)
  between operations  0.7 us (2%)
    ppermute x14, starting transfers between devices, move(): return lax.ppermute(array, 'ctx', [(i, i ^ turn) for i in range(shards)])  23.2 us
    ppermute x14, waiting for transfers between devices, move(): return lax.ppermute(array, 'ctx', [(i, i ^ turn) for i in range(shards)])  4.11 us
    pallas_call x3, Pallas kernels, call(): pl.pallas_call(kernel, out_shape=out_shape, in_specs=[VMEM] * len(args),...  3.16 us
    pallas_call x1, Pallas kernels, by_channels(): pl.pallas_call(gate_kernel, out_shape=[*outs, pltpu.VMEM((4, channels, bl...  1.2 us
  transfers between devices with their start and end apart: 14, of which 6 were waited for; matrix products, arithmetic and copies ran while one was open for 0% of the time, Pallas kernels for 1%

profile of v7, /device:TPU:0, one launch (start us, length us, event | category | flops | bytes accessed | tf_op | source)
XLA Modules:
  0.0 32.5 jit_solution(13149026860182179943)
XLA Ops:
  0.6 1.2 %shard_map.118 = (f32[2,3,8,512]{3,2,1,0:T(8,128)S(1)}, f32[2,3,8,512]{3,2,1,0:T(8,128)S(1)}, f32[1,3,8,512]{3,2,1,0:T(8,128)S(1)}, f32[1,3,8,512]{3,2,1,0:T(8,1...) custom-call(bf16[64,512]{1,0:T(8,128)(2,1)} %first_hbm.1, ...), custom_call_target="tpu_custom_call" | custom-call | tf_op jit(solution)/shard_map/pallas_call | solution.py:265
  1.9 5.1 %collective-permute-start = (f32[2,3,8,512]{3,2,1,0:T(8,128)S(1)}, f32[2,3,8,512]{3,2,1,0:T(8,128)S(1)}, u32[]{:S(2)}, u32[]{:S(2)}) collective-permute-start(f32[2,3,8,512]{3,2,1,0:T(8,128)S(1)} %get-tuple-element.36), channel_id=1, source_target_pairs={{0,12},{2,14},{4,8},{6,10},{8,4},{10,6},{12,0},{14,2},{1,13},{3,15... | collective-permute-start | bytes 294920 | tf_op jit(solution)/shard_map/ppermute | solution.py:111
  7.0 1.5 %collective-permute-start.1 = (f32[2,3,8,512]{3,2,1,0:T(8,128)S(1)}, f32[2,3,8,512]{3,2,1,0:T(8,128)S(1)}, u32[]{:S(2)}, u32[]{:S(2)}) collective-permute-start(f32[2,3,8,512]{3,2,1,0:T(8,128)S(1)} %get-tuple-element.37), channel_id=1, source_target_pairs={{0,2},{2,0},{4,6},{6,4},{8,10},{10,8},{12,14},{14,12},{1,3},{3,1},... | collective-permute-start | bytes 294920 | tf_op jit(solution)/shard_map/ppermute | solution.py:111
  8.5 0.6 %collective-permute-start.3 = (f32[1,3,8,512]{3,2,1,0:T(8,128)S(1)}, f32[1,3,8,512]{3,2,1,0:T(8,128)S(1)}, u32[]{:S(2)}, u32[]{:S(2)}) collective-permute-start(f32[1,3,8,512]{3,2,1,0:T(8,128)S(1)} %get-tuple-element.39), channel_id=1, source_target_pairs={{0,10},{2,8},{4,14},{6,12},{8,2},{10,0},{12,6},{14,4},{1,11},{3,9}... | collective-permute-start | bytes 147464 | tf_op jit(solution)/shard_map/ppermute | solution.py:111
  9.1 2.3 %collective-permute-start.4 = (f32[1,3,8,512]{3,2,1,0:T(8,128)S(1)}, f32[1,3,8,512]{3,2,1,0:T(8,128)S(1)}, u32[]{:S(2)}, u32[]{:S(2)}) collective-permute-start(f32[1,3,8,512]{3,2,1,0:T(8,128)S(1)} %get-tuple-element.40), channel_id=1, source_target_pairs={{0,8},{2,10},{4,12},{6,14},{8,0},{10,2},{12,4},{14,6},{1,9},{3,11}... | collective-permute-start | bytes 147464 | tf_op jit(solution)/shard_map/ppermute | solution.py:111
  11.4 1.6 %collective-permute-start.5 = (f32[1,3,8,512]{3,2,1,0:T(8,128)S(1)}, f32[1,3,8,512]{3,2,1,0:T(8,128)S(1)}, u32[]{:S(2)}, u32[]{:S(2)}) collective-permute-start(f32[1,3,8,512]{3,2,1,0:T(8,128)S(1)} %slice.16), channel_id=1, source_target_pairs={{0,2},{2,0},{4,6},{6,4},{8,10},{10,8},{12,14},{14,12},{1,3},{3,1},... | collective-permute-start | bytes 147464 | tf_op jit(solution)/shard_map/ppermute | solution.py:111
  12.9 2.1 %collective-permute-start.6 = (f32[1,3,8,512]{3,2,1,0:T(8,128)S(1)}, f32[1,3,8,512]{3,2,1,0:T(8,128)S(1)}, u32[]{:S(2)}, u32[]{:S(2)}) collective-permute-start(f32[1,3,8,512]{3,2,1,0:T(8,128)S(1)} %slice.17), channel_id=1, source_target_pairs={{0,4},{2,6},{4,0},{6,2},{8,12},{10,14},{12,8},{14,10},{1,5},{3,7},... | collective-permute-start | bytes 147464 | tf_op jit(solution)/shard_map/ppermute | solution.py:111
  15.0 0.3 shard_map.119
  15.3 0.2 collective-permute-done.5.refs_5_
  15.5 1.6 %collective-permute-done.6.refs_6_ = f32[1,3,8,512]{3,2,1,0:T(8,128)S(1)} collective-permute-done((f32[1,3,8,512]{3,2,1,0:T(8,128)S(1)}, f32[1,3,8,512]{3,2,1,0:T(8,128)S(1)}, u32[]{:S(2)}, u32[]{:S(2)}) %collective-permute-start.6) | collective-permute-done | bytes 49184 | tf_op jit(solution)/shard_map/ppermute | solution.py:111
  17.1 2.0 %shard_map.120 = (f32[2,104,128]{2,1,0:T(8,128)S(1)}, f32[2,104,128]{2,1,0:T(8,128)S(1)}, f32[1,104,128]{2,1,0:T(8,128)S(1)}, f32[1,104,128]{2,1,0:T(8,128)S(1)}...) custom-call(bf16[2,512,256]{2,1,0:T(8,128)(2,1)S(1)} %get-tuple-element.31.outer_ref, ...), custom_call_target="tpu_custom_call" | custom-call | tf_op jit(solution)/shard_map/pallas_call | solution.py:245
  19.1 3.0 %collective-permute-start.7 = (f32[2,104,128]{2,1,0:T(8,128)S(1)}, f32[2,104,128]{2,1,0:T(8,128)S(1)}, u32[]{:S(2)}, u32[]{:S(2)}) collective-permute-start(f32[2,104,128]{2,1,0:T(8,128)S(1)} %get-tuple-element.42), channel_id=1, source_target_pairs={{0,12},{2,14},{4,8},{6,10},{8,4},{10,6},{12,0},{14,2},{1,13},{3,15... | collective-permute-start | bytes 319496 | tf_op jit(solution)/shard_map/ppermute | solution.py:111
  22.1 0.5 %collective-permute-start.8 = (f32[2,104,128]{2,1,0:T(8,128)S(1)}, f32[2,104,128]{2,1,0:T(8,128)S(1)}, u32[]{:S(2)}, u32[]{:S(2)}) collective-permute-start(f32[2,104,128]{2,1,0:T(8,128)S(1)} %get-tuple-element.43), channel_id=1, source_target_pairs={{0,2},{2,0},{4,6},{6,4},{8,10},{10,8},{12,14},{14,12},{1,3},{3,1},... | collective-permute-start | bytes 319496 | tf_op jit(solution)/shard_map/ppermute | solution.py:111
  22.6 0.6 %collective-permute-start.9 = (f32[1,104,128]{2,1,0:T(8,128)S(1)}, f32[1,104,128]{2,1,0:T(8,128)S(1)}, u32[]{:S(2)}, u32[]{:S(2)}) collective-permute-start(f32[1,104,128]{2,1,0:T(8,128)S(1)} %get-tuple-element.44), channel_id=1, source_target_pairs={{0,8},{2,10},{4,12},{6,14},{8,0},{10,2},{12,4},{14,6},{1,9},{3,11}... | collective-permute-start | bytes 159752 | tf_op jit(solution)/shard_map/ppermute | solution.py:111
  23.2 1.0 %collective-permute-start.10 = (f32[1,104,128]{2,1,0:T(8,128)S(1)}, f32[1,104,128]{2,1,0:T(8,128)S(1)}, u32[]{:S(2)}, u32[]{:S(2)}) collective-permute-start(f32[1,104,128]{2,1,0:T(8,128)S(1)} %get-tuple-element.45), channel_id=1, source_target_pairs={{0,4},{2,6},{4,0},{6,2},{8,12},{10,14},{12,8},{14,10},{1,5},{3,7},... | collective-permute-start | bytes 159752 | tf_op jit(solution)/shard_map/ppermute | solution.py:111
  24.1 2.4 %collective-permute-start.11 = (f32[1,104,128]{2,1,0:T(8,128)S(1)}, f32[1,104,128]{2,1,0:T(8,128)S(1)}, u32[]{:S(2)}, u32[]{:S(2)}) collective-permute-start(f32[1,104,128]{2,1,0:T(8,128)S(1)} %get-tuple-element.46), channel_id=1, source_target_pairs={{0,10},{2,8},{4,14},{6,12},{8,2},{10,0},{12,6},{14,4},{1,11},{3,9}... | collective-permute-start | bytes 159752 | tf_op jit(solution)/shard_map/ppermute | solution.py:111
  26.5 0.2 collective-permute-done.7.refs_0_
  26.7 0.3 %collective-permute-start.12 = (f32[1,104,128]{2,1,0:T(8,128)S(1)}, f32[1,104,128]{2,1,0:T(8,128)S(1)}, u32[]{:S(2)}, u32[]{:S(2)}) collective-permute-start(f32[1,104,128]{2,1,0:T(8,128)S(1)} %slice.18), channel_id=1, source_target_pairs={{0,2},{2,0},{4,6},{6,4},{8,10},{10,8},{12,14},{14,12},{1,3},{3,1},... | collective-permute-start | bytes 159752 | tf_op jit(solution)/shard_map/ppermute | solution.py:111
  27.1 0.0 collective-permute-done.8.refs_1_
  27.1 2.4 %collective-permute-start.13 = (f32[1,104,128]{2,1,0:T(8,128)S(1)}, f32[1,104,128]{2,1,0:T(8,128)S(1)}, u32[]{:S(2)}, u32[]{:S(2)}) collective-permute-start(f32[1,104,128]{2,1,0:T(8,128)S(1)} %slice.19), channel_id=1, source_target_pairs={{0,4},{2,6},{4,0},{6,2},{8,12},{10,14},{12,8},{14,10},{1,5},{3,7},... | collective-permute-start | bytes 159752 | tf_op jit(solution)/shard_map/ppermute | solution.py:111
  29.5 0.6 %collective-permute-done.11.refs_4_ = f32[1,104,128]{2,1,0:T(8,128)S(1)} collective-permute-done((f32[1,104,128]{2,1,0:T(8,128)S(1)}, f32[1,104,128]{2,1,0:T(8,128)S(1)}, u32[]{:S(2)}, u32[]{:S(2)}) %collective-permute-start.11) | collective-permute-done | bytes 53280 | tf_op jit(solution)/shard_map/ppermute | solution.py:111
  30.1 0.8 %collective-permute-done.12.refs_5_ = f32[1,104,128]{2,1,0:T(8,128)S(1)} collective-permute-done((f32[1,104,128]{2,1,0:T(8,128)S(1)}, f32[1,104,128]{2,1,0:T(8,128)S(1)}, u32[]{:S(2)}, u32[]{:S(2)}) %collective-permute-start.12) | collective-permute-done | bytes 53280 | tf_op jit(solution)/shard_map/ppermute | solution.py:111
  30.9 0.7 %collective-permute-done.13.refs_6_ = f32[1,104,128]{2,1,0:T(8,128)S(1)} collective-permute-done((f32[1,104,128]{2,1,0:T(8,128)S(1)}, f32[1,104,128]{2,1,0:T(8,128)S(1)}, u32[]{:S(2)}, u32[]{:S(2)}) %collective-permute-start.13) | collective-permute-done | bytes 53280 | tf_op jit(solution)/shard_map/ppermute | solution.py:111
  31.6 0.9 %shard_map.121 = (f32[64,512]{1,0:T(8,128)}, f32[64,512]{1,0:T(8,128)}, f32[64,512]{1,0:T(8,128)}, f32[64,512]{1,0:T(8,128)}, f32[64,512]{1,0:T(8,128)}, /*index=5*/f32[1,64]{1,0:T(1,128)}) custom-call(bf16[4,64,512]{2,1,0:T(8,128)(2,1)S(1)} %get-tuple-element.30.kept_ref, f32[2,104,128]{2,1,0:T(8,128)S(1)} %collective-permute-done.7.refs_0_, ...), custom_call_target="tpu_custom_call" | custom-call | tf_op jit(solution)/shard_map/pallas_call | solution.py:245
  (14 shorter events, 0.0 us)
Async XLA Ops:
  0.6 14.4 %copy-start = (f32[584,128]{1,0:T(8,128)S(1)}, f32[584,128]{1,0:T(8,128)}, u32[]{:S(2)}) copy-start(f32[584,128]{1,0:T(8,128)} %constant.2.clone.in_ref) | copy-start | bytes 897028
  1.9 9.5 %collective-permute-start = (f32[2,3,8,512]{3,2,1,0:T(8,128)S(1)}, f32[2,3,8,512]{3,2,1,0:T(8,128)S(1)}, u32[]{:S(2)}, u32[]{:S(2)}) collective-permute-start(f32[2,3,8,512]{3,2,1,0:T(8,128)S(1)} %get-tuple-element.36), channel_id=1, source_target_pairs={{0,12},{2,14},{4,8},{6,10},{8,4},{10,6},{12,0},{14,2},{1,13},{3,15... | collective-permute-start | bytes 294920 | tf_op jit(solution)/shard_map/ppermute | solution.py:111
  7.0 6.0 %collective-permute-start.1 = (f32[2,3,8,512]{3,2,1,0:T(8,128)S(1)}, f32[2,3,8,512]{3,2,1,0:T(8,128)S(1)}, u32[]{:S(2)}, u32[]{:S(2)}) collective-permute-start(f32[2,3,8,512]{3,2,1,0:T(8,128)S(1)} %get-tuple-element.37), channel_id=1, source_target_pairs={{0,2},{2,0},{4,6},{6,4},{8,10},{10,8},{12,14},{14,12},{1,3},{3,1},... | collective-permute-start | bytes 294920 | tf_op jit(solution)/shard_map/ppermute | solution.py:111
  8.5 6.9 %collective-permute-start.2 = (f32[1,3,8,512]{3,2,1,0:T(8,128)S(1)}, f32[1,3,8,512]{3,2,1,0:T(8,128)S(1)}, u32[]{:S(2)}, u32[]{:S(2)}) collective-permute-start(f32[1,3,8,512]{3,2,1,0:T(8,128)S(1)} %get-tuple-element.38), channel_id=1, source_target_pairs={{0,4},{2,6},{4,0},{6,2},{8,12},{10,14},{12,8},{14,10},{1,5},{3,7},... | collective-permute-start | bytes 147464 | tf_op jit(solution)/shard_map/ppermute | solution.py:111
  8.5 6.9 %collective-permute-start.3 = (f32[1,3,8,512]{3,2,1,0:T(8,128)S(1)}, f32[1,3,8,512]{3,2,1,0:T(8,128)S(1)}, u32[]{:S(2)}, u32[]{:S(2)}) collective-permute-start(f32[1,3,8,512]{3,2,1,0:T(8,128)S(1)} %get-tuple-element.39), channel_id=1, source_target_pairs={{0,10},{2,8},{4,14},{6,12},{8,2},{10,0},{12,6},{14,4},{1,11},{3,9}... | collective-permute-start | bytes 147464 | tf_op jit(solution)/shard_map/ppermute | solution.py:111
  9.1 6.3 %collective-permute-start.4 = (f32[1,3,8,512]{3,2,1,0:T(8,128)S(1)}, f32[1,3,8,512]{3,2,1,0:T(8,128)S(1)}, u32[]{:S(2)}, u32[]{:S(2)}) collective-permute-start(f32[1,3,8,512]{3,2,1,0:T(8,128)S(1)} %get-tuple-element.40), channel_id=1, source_target_pairs={{0,8},{2,10},{4,12},{6,14},{8,0},{10,2},{12,4},{14,6},{1,9},{3,11}... | collective-permute-start | bytes 147464 | tf_op jit(solution)/shard_map/ppermute | solution.py:111
  11.4 4.2 %collective-permute-start.5 = (f32[1,3,8,512]{3,2,1,0:T(8,128)S(1)}, f32[1,3,8,512]{3,2,1,0:T(8,128)S(1)}, u32[]{:S(2)}, u32[]{:S(2)}) collective-permute-start(f32[1,3,8,512]{3,2,1,0:T(8,128)S(1)} %slice.16), channel_id=1, source_target_pairs={{0,2},{2,0},{4,6},{6,4},{8,10},{10,8},{12,14},{14,12},{1,3},{3,1},... | collective-permute-start | bytes 147464 | tf_op jit(solution)/shard_map/ppermute | solution.py:111
  12.9 4.2 %collective-permute-start.6 = (f32[1,3,8,512]{3,2,1,0:T(8,128)S(1)}, f32[1,3,8,512]{3,2,1,0:T(8,128)S(1)}, u32[]{:S(2)}, u32[]{:S(2)}) collective-permute-start(f32[1,3,8,512]{3,2,1,0:T(8,128)S(1)} %slice.17), channel_id=1, source_target_pairs={{0,4},{2,6},{4,0},{6,2},{8,12},{10,14},{12,8},{14,10},{1,5},{3,7},... | collective-permute-start | bytes 147464 | tf_op jit(solution)/shard_map/ppermute | solution.py:111
  19.1 7.7 %collective-permute-start.7 = (f32[2,104,128]{2,1,0:T(8,128)S(1)}, f32[2,104,128]{2,1,0:T(8,128)S(1)}, u32[]{:S(2)}, u32[]{:S(2)}) collective-permute-start(f32[2,104,128]{2,1,0:T(8,128)S(1)} %get-tuple-element.42), channel_id=1, source_target_pairs={{0,12},{2,14},{4,8},{6,10},{8,4},{10,6},{12,0},{14,2},{1,13},{3,15... | collective-permute-start | bytes 319496 | tf_op jit(solution)/shard_map/ppermute | solution.py:111
  22.1 5.0 %collective-permute-start.8 = (f32[2,104,128]{2,1,0:T(8,128)S(1)}, f32[2,104,128]{2,1,0:T(8,128)S(1)}, u32[]{:S(2)}, u32[]{:S(2)}) collective-permute-start(f32[2,104,128]{2,1,0:T(8,128)S(1)} %get-tuple-element.43), channel_id=1, source_target_pairs={{0,2},{2,0},{4,6},{6,4},{8,10},{10,8},{12,14},{14,12},{1,3},{3,1},... | collective-permute-start | bytes 319496 | tf_op jit(solution)/shard_map/ppermute | solution.py:111
  22.6 6.9 %collective-permute-start.9 = (f32[1,104,128]{2,1,0:T(8,128)S(1)}, f32[1,104,128]{2,1,0:T(8,128)S(1)}, u32[]{:S(2)}, u32[]{:S(2)}) collective-permute-start(f32[1,104,128]{2,1,0:T(8,128)S(1)} %get-tuple-element.44), channel_id=1, source_target_pairs={{0,8},{2,10},{4,12},{6,14},{8,0},{10,2},{12,4},{14,6},{1,9},{3,11}... | collective-permute-start | bytes 159752 | tf_op jit(solution)/shard_map/ppermute | solution.py:111
  23.2 6.3 %collective-permute-start.10 = (f32[1,104,128]{2,1,0:T(8,128)S(1)}, f32[1,104,128]{2,1,0:T(8,128)S(1)}, u32[]{:S(2)}, u32[]{:S(2)}) collective-permute-start(f32[1,104,128]{2,1,0:T(8,128)S(1)} %get-tuple-element.45), channel_id=1, source_target_pairs={{0,4},{2,6},{4,0},{6,2},{8,12},{10,14},{12,8},{14,10},{1,5},{3,7},... | collective-permute-start | bytes 159752 | tf_op jit(solution)/shard_map/ppermute | solution.py:111
  24.1 5.9 %collective-permute-start.11 = (f32[1,104,128]{2,1,0:T(8,128)S(1)}, f32[1,104,128]{2,1,0:T(8,128)S(1)}, u32[]{:S(2)}, u32[]{:S(2)}) collective-permute-start(f32[1,104,128]{2,1,0:T(8,128)S(1)} %get-tuple-element.46), channel_id=1, source_target_pairs={{0,10},{2,8},{4,14},{6,12},{8,2},{10,0},{12,6},{14,4},{1,11},{3,9}... | collective-permute-start | bytes 159752 | tf_op jit(solution)/shard_map/ppermute | solution.py:111
  26.7 4.1 %collective-permute-start.12 = (f32[1,104,128]{2,1,0:T(8,128)S(1)}, f32[1,104,128]{2,1,0:T(8,128)S(1)}, u32[]{:S(2)}, u32[]{:S(2)}) collective-permute-start(f32[1,104,128]{2,1,0:T(8,128)S(1)} %slice.18), channel_id=1, source_target_pairs={{0,2},{2,0},{4,6},{6,4},{8,10},{10,8},{12,14},{14,12},{1,3},{3,1},... | collective-permute-start | bytes 159752 | tf_op jit(solution)/shard_map/ppermute | solution.py:111
  27.1 4.5 %collective-permute-start.13 = (f32[1,104,128]{2,1,0:T(8,128)S(1)}, f32[1,104,128]{2,1,0:T(8,128)S(1)}, u32[]{:S(2)}, u32[]{:S(2)}) collective-permute-start(f32[1,104,128]{2,1,0:T(8,128)S(1)} %slice.19), channel_id=1, source_target_pairs={{0,4},{2,6},{4,0},{6,2},{8,12},{10,14},{12,8},{14,10},{1,5},{3,7},... | collective-permute-start | bytes 159752 | tf_op jit(solution)/shard_map/ppermute | solution.py:111
